TPU v7x, 32 devices: a whole 2x2x4 slice. The times are simulated.
32 devices in a mesh: frame: 4 (over x, core), band: 8 (over z, y).
Axes of the slice: x: 2, y: 2, z: 4, core: 2. Of those that a mesh axis runs over, the one named last changes fastest.
Arguments:
- noisy_snapshot_stack: bfloat16 [4, 8, 180, 512], P('frame', 'band'), may hold values from -6 to 6
- gaussian_perturbation: bfloat16 [4, 8, 180, 512], P('frame', 'band'), may hold values from -6 to 6
- snapshot_noise_indices: int32 [4], P('frame'), may hold values from 0 to 3, each once
- partition_longitude_starts: int32 [4], P('frame'), may hold values from 0 to 59
- latitude_patch_tally: int32 [8], replicated, may hold values from 90 to 180
- normalizer_scaling: float32 [512], replicated, may hold values from 0.1 to 1.9
- head_score_scales: float32 [2, 8], replicated, may hold values from 0.5 to 100
- local_projection_matrices: bfloat16 [512, 1536], P(None, 'band'), may hold values from -0.25 to 0.25
- time_projection_matrices: bfloat16 [512, 1536], P(None, 'band'), may hold values from -0.25 to 0.25
- final_projection_matrices: bfloat16 [1024, 512], P(None, 'band'), may hold values from -0.1875 to 0.1875
Outputs:
- next_state: bfloat16 [4, 8, 180, 512], P('frame', 'band')
Inputs may be any that keep to these rules, and one draw needn't show every extreme that they name: `snapshot_noise_indices`: each level index 0 to 3 belongs to exactly one frame.
All inputs are finite; a program needn't handle non-finite values.
Results may differ from a plain program's by a relative error of at most 0.0071.
Values may be sent and summed in bfloat16 or wider, within the bound.
No kernel may reach another device: no remote copies, remote signals or barrier semaphores. Data moves between devices by JAX's collectives and lax.ppermute only.
A program may use at most 64 MiB of HBM per device.

v0:
```python
import math

import jax
import jax.numpy as jnp
from jax import lax
from jax.sharding import PartitionSpec as P

HEADS = 8
HEAD_DIM = 64
WINDOW = 60
PRIOR_SNAPSHOTS = 3


epsilon = 1e-06
sigma_low = 0.1
sigma_high = 2.0
keep_share = 0.8
fresh_share = 0.6


def extended(cells, sides, width):
    for axis, dim in sides:
        count = lax.axis_size(axis)
        ends = count - 1
        head = lax.slice_in_dim(cells, 0, width, axis=dim)
        tail = lax.slice_in_dim(cells, cells.shape[dim] - width, cells.shape[dim], axis=dim)
        cells = jnp.concatenate(
            [
                lax.ppermute(tail, axis, [(i, (i + 1) % count) for i in range(ends)]),
                cells,
                lax.ppermute(head, axis, [((i + 1) % count, i) for i in range(ends)]),
            ],
            axis=dim,
        )
    return cells


def shifted(block, axis, distance):
    devices = range(lax.axis_size(axis))
    route = [(i - distance, i) for i in devices if i - distance in devices]
    return lax.ppermute(block, axis, route)


def sigma_of(level, total_levels):
    return sigma_low * jnp.power(
        sigma_high / sigma_low, (level.astype(jnp.float32) + 1.0) / total_levels
    )


def unit_heads(content_vectors):
    shaped = content_vectors.reshape(content_vectors.shape[:-1] + (HEADS, HEAD_DIM))
    scale = lax.rsqrt(jnp.mean(shaped * shaped, axis=-1, keepdims=True) + epsilon)
    return (shaped * scale).reshape(content_vectors.shape)


def pick(table, index):
    return jnp.sum(jnp.where(jnp.arange(table.shape[0]) == index, table, 0))


def with_past(local, frame_dim, shifter):
    frames = local.shape[frame_dim]
    hops = -(-PRIOR_SNAPSHOTS // frames)
    pieces = [shifter(local, hop) for hop in range(hops, 0, -1)]
    joined = jnp.concatenate(pieces + [local], axis=frame_dim)
    return joined


def local_patch_mixer(
    asking_vectors,
    fringe_lookup_vectors,
    fringe_content_vectors,
    fringe_present_flags,
    snapshot_longitude_shift,
    temper,
):
    rows, lon, token_extent = asking_vectors.shape
    wins = lon // WINDOW
    asking_vectors = jnp.roll(asking_vectors, -snapshot_longitude_shift, axis=1).reshape(
        rows, wins, WINDOW, HEADS, HEAD_DIM
    )
    fringe_lookup_vectors = jnp.roll(
        fringe_lookup_vectors, -snapshot_longitude_shift, axis=1
    ).reshape(rows + 2, wins, WINDOW, HEADS, HEAD_DIM)
    fringe_content_vectors = jnp.roll(
        fringe_content_vectors, -snapshot_longitude_shift, axis=1
    ).reshape(rows + 2, wins, WINDOW, HEADS, HEAD_DIM)
    fringe_present_flags = jnp.roll(
        fringe_present_flags, -snapshot_longitude_shift, axis=1
    ).reshape(rows + 2, wins, WINDOW)
    lookup_vectors = jnp.concatenate(
        [fringe_lookup_vectors[:-2], fringe_lookup_vectors[1:-1], fringe_lookup_vectors[2:]], axis=2
    )
    content_vectors = jnp.concatenate(
        [fringe_content_vectors[:-2], fringe_content_vectors[1:-1], fringe_content_vectors[2:]],
        axis=2,
    )
    permitted_mask = jnp.concatenate(
        [fringe_present_flags[:-2], fringe_present_flags[1:-1], fringe_present_flags[2:]], axis=2
    )
    inner = jnp.arange(WINDOW)
    middle = jnp.arange(3 * WINDOW)
    itself = middle[None, :] == inner[:, None] + WINDOW
    permitted_mask = permitted_mask[:, :, None, None, :] | itself[None, None, None]
    scores = jnp.einsum(
        "rwqhd,rwkhd->rwhqk", asking_vectors, lookup_vectors, preferred_element_type=jnp.float32
    )
    scores = scores * (temper / math.sqrt(HEAD_DIM))[None, None, :, None, None]
    top = jnp.max(jnp.where(permitted_mask, scores, -jnp.inf), axis=-1, keepdims=True)
    weights = jnp.where(permitted_mask, jnp.exp(scores - top), 0.0)
    probs = (weights / jnp.sum(weights, axis=-1, keepdims=True)).astype(jnp.bfloat16)
    combined_result_field = jnp.einsum(
        "rwhqk,rwkhd->rwqhd", probs, content_vectors, preferred_element_type=jnp.float32
    )
    combined_result_field = combined_result_field.reshape(rows, lon, token_extent)
    return jnp.roll(combined_result_field, snapshot_longitude_shift, axis=1).astype(jnp.bfloat16)


def across_time_mixer(asking_vectors, lookup_vectors, content_vectors, permitted_mask, temper):
    count, token_extent = asking_vectors.shape
    span = lookup_vectors.shape[0]
    query_heads = asking_vectors.reshape(count, HEADS, HEAD_DIM)
    key_heads = lookup_vectors.reshape(span, count, HEADS, HEAD_DIM)
    value_heads = content_vectors.reshape(span, count, HEADS, HEAD_DIM)
    scores = jnp.einsum("thd,jthd->jht", query_heads, key_heads, preferred_element_type=jnp.float32)
    scores = scores * (temper / math.sqrt(HEAD_DIM))[None, :, None]
    top = jnp.max(jnp.where(permitted_mask, scores, -jnp.inf), axis=0, keepdims=True)
    weights = jnp.where(permitted_mask, jnp.exp(scores - top), 0.0)
    probs = (weights / jnp.sum(weights, axis=0, keepdims=True)).astype(jnp.bfloat16)
    combined_result_field = jnp.einsum(
        "jht,jthd->thd", probs, value_heads, preferred_element_type=jnp.float32
    )
    return combined_result_field.reshape(count, token_extent).astype(jnp.bfloat16)


def body(
    noisy_snapshot_stack,
    gaussian_perturbation,
    snapshot_noise_indices,
    partition_longitude_starts,
    latitude_patch_tally,
    normalizer_scaling,
    head_score_scales,
    local_projection_matrices,
    time_projection_matrices,
    final_projection_matrices,
):
    frames, rows, lon, token_extent = noisy_snapshot_stack.shape
    token_grid = frames * rows * lon
    band = lax.axis_index("band")
    frame_base = lax.axis_index("frame") * frames
    total_levels = lax.axis_size("frame") * frames
    state_f = noisy_snapshot_stack.astype(jnp.float32)
    normed = (
        state_f
        * lax.rsqrt(jnp.mean(state_f * state_f, axis=-1, keepdims=True) + epsilon)
        * normalizer_scaling
    ).astype(jnp.bfloat16)
    margin = 0
    space_rows = normed.reshape(-1, token_extent)
    space_proj = jnp.dot(
        space_rows,
        lax.all_gather(local_projection_matrices, "band", axis=1, tiled=True),
        preferred_element_type=jnp.float32,
    )
    space_proj = space_proj.reshape(frames, rows + 2 * margin, lon, 3 * token_extent)
    window_queries = unit_heads(space_proj[:, margin : margin + rows, :, :token_extent]).astype(
        jnp.bfloat16
    )
    space_key = unit_heads(space_proj[..., token_extent : 2 * token_extent]).astype(jnp.bfloat16)
    space_value = space_proj[..., 2 * token_extent :].astype(jnp.bfloat16)
    stacked = extended(jnp.stack([space_key, space_value]), (("band", 2),), 1)
    fringe_lookup_vectors = stacked[0]
    fringe_content_vectors = stacked[1]
    plane = rows * lon
    time_rows = normed.reshape(-1, token_extent)
    time_proj = jnp.dot(
        time_rows,
        lax.all_gather(time_projection_matrices, "band", axis=1, tiled=True),
        preferred_element_type=jnp.float32,
    )
    span = PRIOR_SNAPSHOTS + 1
    time_proj = time_proj.reshape(normed.shape[0], rows, lon, 3 * token_extent)
    temporal_queries = unit_heads(time_proj[-frames:, :, :, :token_extent]).astype(jnp.bfloat16)
    time_key = unit_heads(time_proj[..., token_extent : 2 * token_extent]).astype(jnp.bfloat16)
    time_value = time_proj[..., 2 * token_extent :].astype(jnp.bfloat16)

    def shift_values(block, hop):
        return shifted(block, "frame", hop)

    joined = with_past(jnp.stack([time_key, time_value]), 1, shift_values)
    keys_all = joined[0]
    values_all = joined[1]
    key_columns = jnp.stack([keys_all[j : j + frames] for j in range(span)]).reshape(
        span, token_grid, token_extent
    )
    value_columns = jnp.stack([values_all[j : j + frames] for j in range(span)]).reshape(
        span, token_grid, token_extent
    )
    frame_of = jnp.arange(token_grid) // plane
    position = frame_base + frame_of[None, :] - PRIOR_SNAPSHOTS + jnp.arange(span)[:, None]
    permitted_mask = (position >= 0)[:, None, :]
    time_mix = across_time_mixer(
        temporal_queries.reshape(token_grid, token_extent),
        key_columns,
        value_columns,
        permitted_mask,
        head_score_scales[1],
    )
    inner = jnp.arange(rows)[:, None] * lon + jnp.arange(lon)[None, :]
    own_valid = inner < pick(latitude_patch_tally, band)
    above = inner < pick(latitude_patch_tally, band - 1)
    below = inner < pick(latitude_patch_tally, band + 1)
    fringe_present_flags = jnp.concatenate([above, own_valid, below], axis=0)
    space_parts = [
        local_patch_mixer(
            window_queries[0],
            fringe_lookup_vectors[0],
            fringe_content_vectors[0],
            fringe_present_flags,
            partition_longitude_starts[0],
            head_score_scales[0],
        )
    ]
    space_mix = jnp.stack(space_parts).reshape(token_grid, token_extent)
    mixed = jnp.concatenate([space_mix, time_mix], axis=1)
    update = jnp.dot(
        mixed,
        lax.all_gather(final_projection_matrices, "band", axis=1, tiled=True),
        preferred_element_type=jnp.float32,
    ).reshape(frames, rows, lon, token_extent)
    sigma = sigma_of(snapshot_noise_indices, total_levels)[:, None, None, None]
    sigma_next = sigma_of(snapshot_noise_indices - 1, total_levels)[:, None, None, None]
    denoised = state_f / (1.0 + sigma * sigma) + sigma * lax.rsqrt(1.0 + sigma * sigma) * update
    noise_f = gaussian_perturbation.astype(jnp.float32)
    stepped = denoised + sigma_next * (
        keep_share * (state_f - denoised) / sigma + fresh_share * noise_f
    )
    finished = (snapshot_noise_indices == 0)[:, None, None, None]
    return jnp.where(finished, sigma_high * noise_f, stepped).astype(jnp.bfloat16)


def solution(mesh):
    return jax.shard_map(
        body,
        mesh=mesh,
        in_specs=(
            P("frame", "band", None, None),
            P("frame", "band", None, None),
            P("frame"),
            P("frame"),
            P(),
            P(),
            P(),
            P(None, "band"),
            P(None, "band"),
            P(None, "band"),
        ),
        out_specs=P("frame", "band", None, None),
        check_vma=False,
    )
```

profile of v0, /device:TPU:0, one launch (start us, length us, event | category | flops | bytes accessed | tf_op | source)
XLA Modules:
  0.0 159.1 jit_solution(10543922075528884963)
XLA Ops:
  9.4 1.0 fusion.24
  11.3 1.4 fusion.55
  13.3 1.3 iota_compare_fusion.2
  16.0 40.5 %all-gather.4.cloned.1.call-done = bf16[512,1536]{0,1:T(8,128)(2,1)} async-done(((bf16[512,192]{0,1:T(8,128)(2,1)}), bf16[512,1536]{0,1:T(8,128)(2,1)}) %all-gather.4.cloned.1.call-update) | async-done | bytes 1572880 | tf_op jit(solution)/shard_map/all_gather | solution.py:162
  56.5 2.2 %convolution_bitcast_fusion.1 = f32[1,1,180,1536]{3,2,1,0:T(8,128)S(1)} fusion(bf16[512,1536]{0,1:T(8,128)(2,1)} %all-gather.4.cloned.1.call-done, bf16[1,1,180,512]{3,2,1,0:T(8,128)(2,1)} %param.12, f32[512]{0:T(512)} %param.17, f32[180]{0:T(256)S(1)} %add_rsqrt_fusion.4), kind=kOutput, calls=%fused_computation.2 | convolution fusion | flops 283484160 | bytes 2865872 | tf_op jit(solution)/shard_map/dot_general | solution.py:160
  61.4 3.2 %collective-permute-start = (bf16[2,1,1,180,512]{4,3,2,1,0:T(8,128)(2,1)}, bf16[2,1,1,180,512]{4,3,2,1,0:T(8,128)(2,1)}, u32[]{:S(2)}, u32[]{:S(2)}) collective-permute-start(bf16[2,1,1,180,512]{4,3,2,1,0:T(8,128)(2,1)} %pad_maximum_fusion.1), channel_id=1, source_target_pairs={{0,1},{1,2},{2,3},{3,4},{4,5},{5,6},{6,7},{8,9},{9,10},{10,11},{11... | collective-permute-start | bytes 1105928 | tf_op jit(solution)/shard_map/ppermute | solution.py:29
  64.6 1.3 collective-permute-start.1
  65.9 43.0 %all-gather.6.cloned.1.call-done = bf16[512,1536]{0,1:T(8,128)(2,1)} async-done(((bf16[512,192]{0,1:T(8,128)(2,1)}), bf16[512,1536]{0,1:T(8,128)(2,1)}) %all-gather.6.cloned.1.call-update) | async-done | bytes 1572880 | tf_op jit(solution)/shard_map/all_gather | solution.py:178
  108.8 2.1 %convolution_bitcast_fusion = f32[1,1,180,1536]{3,2,1,0:T(8,128)S(1)} fusion(bf16[512,1536]{0,1:T(8,128)(2,1)} %all-gather.6.cloned.1.call-done, bf16[1,1,180,512]{3,2,1,0:T(8,128)(2,1)S(1)} %copy-done, f32[512]{0:T(512)S(1)} %copy-done.4, f32[180]{0:T(256)S(1)} %add_rsqrt_fusion.4), kind=kOutput, calls=%fused_computation.1 | convolution fusion | flops 283484160 | bytes 2865872 | tf_op jit(solution)/shard_map/dot_general | solution.py:176
  113.0 2.9 %collective-permute-start.2 = (bf16[2,1,1,180,512]{4,3,2,1,0:T(8,128)(2,1)}, bf16[2,1,1,180,512]{4,3,2,1,0:T(8,128)(2,1)}, u32[]{:S(2)}, u32[]{:S(2)}) collective-permute-start(bf16[2,1,1,180,512]{4,3,2,1,0:T(8,128)(2,1)} %pad_maximum_fusion.2), channel_id=1, source_target_pairs={{0,24},{1,25},{2,26},{3,27},{4,28},{5,29},{6,30},{7,31}} | collective-permute-start | bytes 1105928 | tf_op jit(solution)/shard_map/ppermute | solution.py:41
  115.9 2.6 %collective-permute-start.3 = (bf16[2,1,1,180,512]{4,3,2,1,0:T(8,128)(2,1)}, bf16[2,1,1,180,512]{4,3,2,1,0:T(8,128)(2,1)}, u32[]{:S(2)}, u32[]{:S(2)}) collective-permute-start(bf16[2,1,1,180,512]{4,3,2,1,0:T(8,128)(2,1)} %pad_maximum_fusion.2), channel_id=1, source_target_pairs={{0,16},{8,24},{1,17},{9,25},{2,18},{10,26},{3,19},{11,27},{4,20},{... | collective-permute-start | bytes 1105928 | tf_op jit(solution)/shard_map/ppermute | solution.py:41
  118.5 2.0 %collective-permute-start.4 = (bf16[2,1,1,180,512]{4,3,2,1,0:T(8,128)(2,1)}, bf16[2,1,1,180,512]{4,3,2,1,0:T(8,128)(2,1)}, u32[]{:S(2)}, u32[]{:S(2)}) collective-permute-start(bf16[2,1,1,180,512]{4,3,2,1,0:T(8,128)(2,1)} %pad_maximum_fusion.2), channel_id=1, source_target_pairs={{0,8},{8,16},{16,24},{1,9},{9,17},{17,25},{2,10},{10,18},{18,26},{... | collective-permute-start | bytes 1105928 | tf_op jit(solution)/shard_map/ppermute | solution.py:41
  122.3 1.2 pad_maximum_fusion
  123.7 1.2 fusion.16
  127.3 1.7 %fusion.67 = (f32[3,8,60]{2,1,0:T(8,128)S(1)}, f32[3,8,60,180]{3,2,1,0:T(8,128)}) fusion(f32[3,8,60,180]{3,2,1,0:T(8,128)S(1)} %convolution_multiply_fusion, pred[3,60,180]{2,1,0:T(8,128)(4,1)S(1)} %broadcast_or_fusion), kind=kOutput, calls=%fused_computation.140 | output fusion | flops 1036979 | bytes 2111760 | tf_op jit(solution)/shard_map/sub | solution.py:109
  129.3 1.1 copy.45
  130.5 1.1 copy.46
  132.1 2.7 %convolution_bitcast_fusion.2 = bf16[1,3,60,8,64]{2,4,3,1,0:T(8,128)(2,1)} fusion(bf16[1,3,60,8,64]{2,4,3,1,0:T(8,128)(2,1)S(1)} %copy.47, bf16[1,3,60,8,64]{2,4,3,1,0:T(8,128)(2,1)} %copy.46, bf16[1,3,60,8,64]{2,4,3,1,0:T(8,128)(2,1)} %copy.45, f32[3,8,60,180]{3,2,1,0:T(8,128)S(1)} %copy-done.1, f32[3,8,60]{2,1,0:T(8,128)S(1)} %get-tuple-element.36), kind=kOutput, calls=%fused_computation.10 | convolution fusion | flops 35354880 | bytes 1779840 | tf_op jit(solution)/shard_map/rwhqk,rwkhd->rwqhd/dot_general | solution.py:111
  134.8 1.3 copy.54
  136.3 1.0 fusion.64
  137.5 1.0 fusion.65
  138.7 1.1 fusion.66
  141.8 8.2 %all-gather.8.cloned.1.call-done = bf16[1024,512]{0,1:T(8,128)(2,1)} async-done(((bf16[1024,64]{0,1:T(8,128)(2,1)}), bf16[1024,512]{0,1:T(8,128)(2,1)}) %all-gather.8.cloned.1.call-update) | async-done | bytes 1048592 | tf_op jit(solution)/shard_map/all_gather | solution.py:228
  150.0 2.5 %fusion.20 = bf16[1,1,180,512]{3,2,1,0:T(8,128)(2,1)} fusion(bf16[1,1,180,512]{3,2,1,0:T(8,128)(2,1)S(1)} %copy-done.5, bf16[1,1,180,512]{3,2,1,0:T(8,128)(2,1)S(1)} %copy-done, bf16[1024,512]{0,1:T(8,128)(2,1)} %all-gather.8.cloned.1.call-done, bf16[180,512]{1,0:T(8,128)(2,1)S(1)} %copy.68, bf16[180,512]{1,0:T(8,128)(2,1)S(1)} %fusion.38, f32[]{:T(128)} %bitcast.51, ...), kind=kOutput, calls=%fused_computation.47 | convolution fusion | flops 190863360 | bytes 1970193 | tf_op jit(solution)/shard_map/dot_general | solution.py:226
  (100 shorter events, 16.5 us)
Async XLA Ops:
  6.5 49.9 %all-gather.4.cloned.1.call-start = ((), (), s32[]{:S(2)}) async-start(), calls=%async_computation | async-start | bytes 1769472 | tf_op jit(solution)/shard_map/all_gather | solution.py:162
  7.3 101.6 %all-gather.6.cloned.1.call-start = ((), (), s32[]{:S(2)}) async-start(), calls=%async_computation.1 | async-start | bytes 1769472 | tf_op jit(solution)/shard_map/all_gather | solution.py:178
  8.0 142.0 %all-gather.8.cloned.1.call-start = ((), (), s32[]{:S(2)}) async-start(), calls=%async_computation.2 | async-start | bytes 1179648 | tf_op jit(solution)/shard_map/all_gather | solution.py:228
  59.6 49.2 %copy-start = (bf16[1,1,180,512]{3,2,1,0:T(8,128)(2,1)S(1)}, bf16[1,1,180,512]{3,2,1,0:T(8,128)(2,1)}, u32[]{:S(2)}) copy-start(bf16[1,1,180,512]{3,2,1,0:T(8,128)(2,1)} %param.12) | copy-start | bytes 552964
  59.6 49.2 %copy-start.4 = (f32[512]{0:T(512)S(1)}, f32[512]{0:T(512)}, u32[]{:S(2)}) copy-start(f32[512]{0:T(512)} %param.17) | copy-start | bytes 6148
  61.4 61.0 %collective-permute-start = (bf16[2,1,1,180,512]{4,3,2,1,0:T(8,128)(2,1)}, bf16[2,1,1,180,512]{4,3,2,1,0:T(8,128)(2,1)}, u32[]{:S(2)}, u32[]{:S(2)}) collective-permute-start(bf16[2,1,1,180,512]{4,3,2,1,0:T(8,128)(2,1)} %pad_maximum_fusion.1), channel_id=1, source_target_pairs={{0,1},{1,2},{2,3},{3,4},{4,5},{5,6},{6,7},{8,9},{9,10},{10,11},{11... | collective-permute-start | bytes 1105928 | tf_op jit(solution)/shard_map/ppermute | solution.py:29
  64.6 57.8 %collective-permute-start.1 = (bf16[2,1,1,180,512]{4,3,2,1,0:T(8,128)(2,1)}, bf16[2,1,1,180,512]{4,3,2,1,0:T(8,128)(2,1)}, u32[]{:S(2)}, u32[]{:S(2)}) collective-permute-start(bf16[2,1,1,180,512]{4,3,2,1,0:T(8,128)(2,1)} %pad_maximum_fusion.1), channel_id=1, source_target_pairs={{1,0},{2,1},{3,2},{4,3},{5,4},{6,5},{7,6},{9,8},{10,9},{11,10},{12... | collective-permute-start | bytes 1105928 | tf_op jit(solution)/shard_map/ppermute | solution.py:31
  112.0 8.7 %copy-start.3 = (bf16[1,180,512]{2,1,0:T(8,128)(2,1)S(1)}, bf16[1,180,512]{2,1,0:T(8,128)(2,1)}, u32[]{:S(2)}) copy-start(bf16[1,180,512]{2,1,0:T(8,128)(2,1)} %get-tuple-element.12) | copy-start | bytes 552964
  113.0 23.3 %collective-permute-start.2 = (bf16[2,1,1,180,512]{4,3,2,1,0:T(8,128)(2,1)}, bf16[2,1,1,180,512]{4,3,2,1,0:T(8,128)(2,1)}, u32[]{:S(2)}, u32[]{:S(2)}) collective-permute-start(bf16[2,1,1,180,512]{4,3,2,1,0:T(8,128)(2,1)} %pad_maximum_fusion.2), channel_id=1, source_target_pairs={{0,24},{1,25},{2,26},{3,27},{4,28},{5,29},{6,30},{7,31}} | collective-permute-start | bytes 1105928 | tf_op jit(solution)/shard_map/ppermute | solution.py:41
  115.9 21.6 %collective-permute-start.3 = (bf16[2,1,1,180,512]{4,3,2,1,0:T(8,128)(2,1)}, bf16[2,1,1,180,512]{4,3,2,1,0:T(8,128)(2,1)}, u32[]{:S(2)}, u32[]{:S(2)}) collective-permute-start(bf16[2,1,1,180,512]{4,3,2,1,0:T(8,128)(2,1)} %pad_maximum_fusion.2), channel_id=1, source_target_pairs={{0,16},{8,24},{1,17},{9,25},{2,18},{10,26},{3,19},{11,27},{4,20},{... | collective-permute-start | bytes 1105928 | tf_op jit(solution)/shard_map/ppermute | solution.py:41
  118.5 20.2 %collective-permute-start.4 = (bf16[2,1,1,180,512]{4,3,2,1,0:T(8,128)(2,1)}, bf16[2,1,1,180,512]{4,3,2,1,0:T(8,128)(2,1)}, u32[]{:S(2)}, u32[]{:S(2)}) collective-permute-start(bf16[2,1,1,180,512]{4,3,2,1,0:T(8,128)(2,1)} %pad_maximum_fusion.2), channel_id=1, source_target_pairs={{0,8},{8,16},{16,24},{1,9},{9,17},{17,25},{2,10},{10,18},{18,26},{... | collective-permute-start | bytes 1105928 | tf_op jit(solution)/shard_map/ppermute | solution.py:41
  129.2 2.9 %copy-start.1 = (f32[3,8,60,180]{3,2,1,0:T(8,128)S(1)}, f32[3,8,60,180]{3,2,1,0:T(8,128)}, u32[]{:S(2)}) copy-start(f32[3,8,60,180]{3,2,1,0:T(8,128)} %get-tuple-element.37) | copy-start | bytes 3110404
  139.9 1.0 copy-start.2
  140.7 9.3 %copy-start.5 = (bf16[1,1,180,512]{3,2,1,0:T(8,128)(2,1)S(1)}, bf16[1,1,180,512]{3,2,1,0:T(8,128)(2,1)}, u32[]{:S(2)}) copy-start(bf16[1,1,180,512]{3,2,1,0:T(8,128)(2,1)} %param.13) | copy-start | bytes 552964
Sparse Core Ops, SparseCore 0:
  9.5 46.8 all-gather.3
  58.6 50.1 all-gather.5
  111.0 39.0 all-gather.7
where the time goes:
time: 160 us; the launch traced here: 159 us
  waiting for transfers between devices  93.8 us (59%)
  between operations  15.2 us (10%)
  other arithmetic  14 us (9%)
  local copies, waits for them, and re-layouts  13.8 us (9%)
  starting transfers between devices  12.1 us (8%)
  matrix products  10.2 us (6%)
    all_gather x1, waiting for transfers between devices, body(): lax.all_gather(time_projection_matrices, 'band', axis=1, tiled=True)  43 us
    all_gather x1, waiting for transfers between devices, body(): lax.all_gather(local_projection_matrices, 'band', axis=1, tiled=True)  40.5 us
    all_gather x1, waiting for transfers between devices, body(): lax.all_gather(final_projection_matrices, 'band', axis=1, tiled=True)  8.25 us
    ppermute x3, starting transfers between devices, shifted(): return lax.ppermute(block, axis, route)  7.54 us
    slice x6, local copies, waits for them, and re-layouts, body(): keys_all[j:j + frames]  3.53 us
  transfers between devices with their start and end apart: 8, of which 3 were waited for; matrix products, arithmetic and copies ran while one was open for 22% of the time, Pallas kernels for 0%

commit v1 on v0

v1 whole, which is shorter than its diff:
```python
import functools
import math

import jax
import jax.numpy as jnp
from jax import lax
from jax.experimental import pallas as pl
from jax.experimental.pallas import tpu as pltpu
from jax.sharding import PartitionSpec as P

HEADS = 8
HEAD_DIM = 64
WINDOW = 60
PRIOR_SNAPSHOTS = 3

epsilon = 1e-06
sigma_low = 0.1
sigma_high = 2.0
keep_share = 0.8
fresh_share = 0.6
LOG2E = 1.4426950408889634
FAR = -1e30

AXES = ("frame", "band")
BF = jnp.bfloat16
F32 = jnp.float32


def ring_band(pos, n):
    return jnp.where(pos < n // 2, 2 * pos, 2 * (n - 1 - pos) + 1)


def ring_pairs(nf, n):
    order = list(range(0, n, 2)) + list(range(1, n, 2))[::-1]
    pairs = []
    for f in range(nf):
        step = 1 if f % 2 == 0 else -1
        for p in range(n):
            pairs.append((f * n + order[p], f * n + order[(p + step) % n]))
    return pairs


def core_pairs(nf, n):
    return [(f * n + b, (f ^ 1) * n + b) for f in range(nf) for b in range(n)]


def shift_frame(block, hop):
    nf = lax.axis_size("frame")
    return lax.ppermute(block, "frame", [(i, i + hop) for i in range(nf - hop)])


def shift_band(block, hop):
    n = lax.axis_size("band")
    return lax.ppermute(block, "band", [(i, i + hop) for i in range(n) if 0 <= i + hop < n])


def unit_rows(block):
    shaped = block.reshape(HEADS, HEAD_DIM, block.shape[-1])
    mean = jnp.mean(shaped * shaped, axis=1, keepdims=True)
    return (shaped * lax.rsqrt(mean + epsilon)).reshape(block.shape)


def kernel(
    slots, n_time, n_bands, total_levels,
    meta, scales, tally, gain_ref, state_ref, noise_ref, *rest,
):
    space_refs = (state_ref,) + rest[:2]
    time_refs = (state_ref,) + rest[2 : 1 + n_time]
    rest = rest[1 + n_time :]
    first, second = rest[:slots], rest[slots : 2 * slots]
    out_ref = rest[2 * slots]
    weights, final, qs, ks, vs, mix = rest[2 * slots + 1 :]
    lon, width = state_ref.shape
    parity, shift, level = meta[slots], meta[slots + 1], meta[slots + 2]
    frame, band = meta[slots + 3], meta[slots + 4]
    r3 = 3 * width // n_bands
    r1 = width // n_bands

    for group, which in ((first, parity), (second, 1 - parity)):
        for i, ref in enumerate(group):
            b = meta[i]
            weights[which, pl.ds(pl.multiple_of(b * r3, 16), r3), :] = ref[0:r3, :]
            final[which, pl.ds(pl.multiple_of(b * r1, 16), r1), :] = ref[r3 : r3 + r1, :]

    def normed(ref):
        x = ref[...].astype(F32)
        scale = lax.rsqrt(jnp.mean(x * x, axis=-1, keepdims=True) + epsilon)
        return (x * scale * gain_ref[...]).astype(BF)

    nt = (((1,), (1,)), ((), ()))

    def proj(which, part, x):
        return lax.dot_general(
            weights[which, part * width : (part + 1) * width, :], x, nt, preferred_element_type=F32
        )

    own = normed(state_ref)
    qs[0] = unit_rows(proj(0, 0, own)).astype(BF)
    for j, ref in enumerate(space_refs):
        x = own if j == 0 else normed(ref)
        ks[j] = unit_rows(proj(0, 1, x)).astype(BF)
        vs[j] = proj(0, 2, x).astype(BF)
    qs[1] = unit_rows(proj(1, 0, own)).astype(BF)
    for j, ref in enumerate(time_refs):
        x = own if j == 0 else normed(ref)
        ks[3 + j] = unit_rows(proj(1, 1, x)).astype(BF)
        vs[3 + j] = proj(1, 2, x).astype(BF)

    kcol = lax.broadcasted_iota(jnp.int32, (lon, lon), 0)
    qcol = lax.broadcasted_iota(jnp.int32, (lon, lon), 1)

    def window(col):
        c = col - shift
        c = jnp.where(c < 0, c + lon, c)
        w = jnp.zeros_like(c)
        for edge in range(WINDOW, lon, WINDOW):
            w = w + (c >= edge).astype(jnp.int32)
        return w

    same = window(kcol) == window(qcol)
    biases = []
    for j, off in enumerate((0, -1, 1)):
        row = band + off
        exists = (row >= 0) & (row < n_bands)
        limit = jnp.where(exists, tally[jnp.clip(row, 0, n_bands - 1)], 0)
        seen = same & (kcol < limit)
        if j == 0:
            seen = seen | (kcol == qcol)
        biases.append(jnp.where(seen, 0.0, FAR).astype(F32))
    tn = (((0,), (0,)), ((), ()))
    for h in range(HEADS):
        lo = h * HEAD_DIM
        hi = lo + HEAD_DIM
        factor = scales[0, h] * (LOG2E / math.sqrt(HEAD_DIM))
        q = qs[0, lo:hi, :]
        x = [
            lax.dot_general(ks[j, lo:hi, :], q, tn, preferred_element_type=F32) * factor + biases[j]
            for j in range(3)
        ]
        top = jnp.max(jnp.maximum(jnp.maximum(x[0], x[1]), x[2]), axis=0, keepdims=True)
        e = [jnp.exp2(s - top) for s in x]
        inv = 1.0 / jnp.sum(e[0] + e[1] + e[2], axis=0, keepdims=True)
        o = sum(
            jnp.dot(vs[j, lo:hi, :], (e[j] * inv).astype(BF), preferred_element_type=F32)
            for j in range(3)
        )
        mix[0, lo:hi, :] = o.astype(BF)

    odd = frame % 2
    back = [0, 2, jnp.where(odd == 1, 1, -1), jnp.where(odd == 1, 3, 1), jnp.where(odd == 1, -1, 3)]
    allow = [(b >= 0) & (b <= PRIOR_SNAPSHOTS) & (frame - b >= 0) for b in back]
    shut = [jnp.where(a, 0.0, FAR).astype(F32) for a in allow]
    for h in range(HEADS):
        lo = h * HEAD_DIM
        hi = lo + HEAD_DIM
        factor = scales[1, h] * (LOG2E / math.sqrt(HEAD_DIM))
        q = qs[1, lo:hi, :].astype(F32)
        x = [
            jnp.sum(q * ks[3 + j, lo:hi, :].astype(F32), axis=0, keepdims=True) * factor + shut[j]
            for j in range(n_time)
        ]
        top = functools.reduce(jnp.maximum, x)
        e = [jnp.exp2(s - top) for s in x]
        inv = 1.0 / sum(e)
        o = sum(
            (e[j] * inv).astype(BF).astype(F32) * vs[3 + j, lo:hi, :].astype(F32)
            for j in range(n_time)
        )
        mix[1, lo:hi, :] = o.astype(BF)

    update = jnp.dot(final[0], mix[0], preferred_element_type=F32) + jnp.dot(
        final[1], mix[1], preferred_element_type=F32
    )
    update = update.T

    def sigma_of(lv):
        power = (jnp.full((1, width), lv, jnp.int32).astype(F32) + 1.0) / total_levels
        return sigma_low * jnp.exp(power * math.log(sigma_high / sigma_low))

    s, s_next = sigma_of(level), sigma_of(level - 1)
    state = state_ref[...].astype(F32)
    fresh = noise_ref[...].astype(F32)
    denoised = state / (1.0 + s * s) + s * lax.rsqrt(1.0 + s * s) * update
    stepped = denoised + s_next * (keep_share * (state - denoised) / s + fresh_share * fresh)
    out_ref[...] = jnp.where(level == 0, sigma_high * fresh, stepped).astype(BF)


def body(
    noisy_snapshot_stack,
    gaussian_perturbation,
    snapshot_noise_indices,
    partition_longitude_starts,
    latitude_patch_tally,
    normalizer_scaling,
    head_score_scales,
    local_projection_matrices,
    time_projection_matrices,
    final_projection_matrices,
):
    frames, rows, lon, width = noisy_snapshot_stack.shape
    assert frames == 1 and rows == 1
    n, nf = lax.axis_size("band"), lax.axis_size("frame")
    assert n % 2 == 0 and nf % 2 == 0
    band, frame = lax.axis_index("band"), lax.axis_index("frame")
    parity = frame % 2
    state = noisy_snapshot_stack.reshape(lon, width)
    noise = gaussian_perturbation.reshape(lon, width)

    chunk_a = jnp.concatenate([local_projection_matrices, final_projection_matrices[:width]], axis=1).T
    chunk_b = jnp.concatenate([time_projection_matrices, final_projection_matrices[width:]], axis=1).T
    own0 = jnp.where(parity == 0, chunk_a, chunk_b)
    own1 = jnp.where(parity == 0, chunk_b, chunk_a)

    ring, core = ring_pairs(nf, n), core_pairs(nf, n)
    half = n // 2
    chain0, chain1 = [own0], [own1]
    for h in range(half):
        chain0.append(lax.ppermute(chain0[-1], AXES, ring))
        if h < half - 1:
            chain1.append(lax.ppermute(chain1[-1], AXES, ring))
    swap0 = [lax.ppermute(c, AXES, core) for c in chain0[1:half]]
    swap1 = [lax.ppermute(c, AXES, core) for c in chain1[1:half]]
    swap_last = lax.ppermute(chain0[half], AXES, core)
    first = chain0 + swap1
    second = chain1 + [swap_last] + swap0

    above = shift_band(state, 1)
    below = shift_band(state, -1)
    two_back = shift_frame(state, 2)
    partner = lax.ppermute(state, AXES, core)
    partner_two = lax.ppermute(two_back, AXES, core)
    past = [two_back, partner, partner_two]
    if nf > 4:
        past.append(shift_frame(state, 3))

    pos = jnp.where(band % 2 == 0, band // 2, n - 1 - band // 2)
    away = jnp.array(list(range(0, -half - 1, -1)) + list(range(1, half)), jnp.int32)
    slot_pos = (pos + jnp.where(parity == 0, away, -away)) % n
    meta = jnp.concatenate(
        [
            ring_band(slot_pos, n),
            jnp.stack(
                [parity, partition_longitude_starts[0], snapshot_noise_indices[0], frame, band]
            ),
        ]
    ).astype(jnp.int32)

    smem = pl.BlockSpec(memory_space=pltpu.SMEM)
    vmem = pl.BlockSpec(memory_space=pltpu.VMEM)
    operands = [state, noise, above, below] + past + first + second
    n_time = 1 + len(past)
    out = pl.pallas_call(
        functools.partial(kernel, n, n_time, n, nf),
        out_shape=jax.ShapeDtypeStruct((lon, width), BF),
        in_specs=[smem] * 3 + [vmem] * (1 + len(operands)),
        out_specs=vmem,
        scratch_shapes=[
            pltpu.VMEM((2, 3 * width, width), BF),
            pltpu.VMEM((2, width, width), BF),
            pltpu.VMEM((2, width, lon), BF),
            pltpu.VMEM((3 + n_time, width, lon), BF),
            pltpu.VMEM((3 + n_time, width, lon), BF),
            pltpu.VMEM((2, width, lon), BF),
        ],
        compiler_params=pltpu.CompilerParams(vmem_limit_bytes=40 * 1024 * 1024),
    )(meta, head_score_scales, latitude_patch_tally, normalizer_scaling.reshape(1, width), *operands)
    return out.reshape(noisy_snapshot_stack.shape)


def solution(mesh):
    return jax.shard_map(
        body,
        mesh=mesh,
        in_specs=(
            P("frame", "band", None, None),
            P("frame", "band", None, None),
            P("frame"),
            P("frame"),
            P(),
            P(),
            P(),
            P(None, "band"),
            P(None, "band"),
            P(None, "band"),
        ),
        out_specs=P("frame", "band", None, None),
        check_vma=False,
    )
```

time: 160 us -> 59.9 us (0.37)
  waiting for transfers between devices: 93.8 us -> 7.85 us
  starting transfers between devices: 12.1 us -> 28.5 us
  between operations: 15.2 us -> 1.46 us
  other arithmetic: 14 us -> 1.07 us
  matrix products: 10.2 us -> 0 us
  Pallas kernels: 0 us -> 8.32 us
  local copies, waits for them, and re-layouts: 13.8 us -> 12.2 us
    all_gather x3 -> x0, waiting for transfers between devices: 91.7 us -> none  [the longest x1 43 us: body(): lax.all_gather(time_projection_matrices, 'band', axis=1, tiled=True)]
    ppermute x5 -> x19, starting transfers between devices: 12 us -> 28.5 us  [the longest x3 9.27 us: body(): chain1.append(lax.ppermute(chain1[-1], AXES, ring))]
    unnamed x13 -> x38, local copies, waits for them, and re-layouts: 0.17 us -> 11.2 us
    dot_general x5 -> x0, matrix products: 10.2 us -> none  [the longest x1 2.66 us: local_patch_mixer(): jnp.einsum('rwhqk,rwkhd->rwqhd', probs, content_vectors, preferred_elemen...]
    slice x29 -> x1, local copies, waits for them, and re-layouts: 9.88 us -> 0.92 us  [body(): final_projection_matrices[:width]]
    pallas_call x0 -> x1, Pallas kernels: none -> 8.32 us  [body(): pl.pallas_call(functools.partial(kernel, n, n_time, n, nf), out_shape=jax...]
    ppermute x5 -> x19, waiting for transfers between devices: 0.01 us -> 7.85 us  [the longest x4 5.51 us: body(): chain0.append(lax.ppermute(chain0[-1], AXES, ring))]
    concatenate x4 -> x0, other arithmetic: 2.87 us -> none  [the longest x1 1.24 us: extended(): jnp.concatenate([lax.ppermute(tail, axis, [(i, (i + 1) % count) for i in...]
  transfers between devices with their start and end apart: 8 -> 19, of which waited for: 3 -> 6; matrix products, arithmetic and copies ran while one was open for 22% -> 0% of each run, Pallas kernels for 0% -> 0%
where the time goes in v1:
time: 59.9 us; the launch traced here: 59.4 us
  starting transfers between devices  28.5 us (48%)
  local copies, waits for them, and re-layouts  12.2 us (20%)
  Pallas kernels  8.32 us (14%)
  waiting for transfers between devices  7.85 us (13%)
  between operations  1.46 us (2%)
  other arithmetic  1.07 us (2%)
    unnamed x38, local copies, waits for them, and re-layouts  11.2 us
    ppermute x3, starting transfers between devices, body(): chain1.append(lax.ppermute(chain1[-1], AXES, ring))  9.27 us
    ppermute x4, starting transfers between devices, body(): chain0.append(lax.ppermute(chain0[-1], AXES, ring))  8.81 us
    pallas_call x1, Pallas kernels, body(): pl.pallas_call(functools.partial(kernel, n, n_time, n, nf), out_shape=jax...  8.32 us
    ppermute x2, starting transfers between devices, shift_band(): lax.ppermute(block, 'band', [(i, i + hop) for i in range(n) if 0 <= i + h...  5.84 us
    ppermute x4, waiting for transfers between devices, body(): chain0.append(lax.ppermute(chain0[-1], AXES, ring))  5.51 us
    ppermute x1, starting transfers between devices, shift_frame(): return lax.ppermute(block, 'frame', [(i, i + hop) for i in range(nf - hop)])  3.39 us
  transfers between devices with their start and end apart: 19, of which 6 were waited for; matrix products, arithmetic and copies ran while one was open for 0% of the time, Pallas kernels for 0%

profile of v1, /device:TPU:0, one launch (start us, length us, event | category | flops | bytes accessed | tf_op | source)
XLA Modules:
  0.0 59.4 jit_solution(4218409845423025586)
XLA Ops:
  0.0 0.9 %fusion.2 = (bf16[512,64]{0,1:T(8,128)(2,1)S(1)}, bf16[512,64]{0,1:T(8,128)(2,1)S(1)}) fusion(bf16[1024,64]{0,1:T(8,128)(2,1)} %param.20), kind=kLoop, calls=%fused_computation.11 | loop fusion | bytes 262144 | tf_op jit(solution)/shard_map/slice | solution.py:209
  1.0 1.1 %select_bitcast_fusion = (bf16[256,512]{1,0:T(8,128)(2,1)S(1)}, bf16[256,512]{1,0:T(8,128)(2,1)S(1)}) fusion(pred[]{:T(512)S(6)} %eq.14, bf16[512,64]{0,1:T(8,128)(2,1)S(1)} %get-tuple-element.8, bf16[512,192]{0,1:T(8,128)(2,1)S(1)} %copy-done.16, bf16[512,64]{0,1:T(8,128)(2,1)S(1)} %get-tuple-element.7, bf16[512,192]{0,1:T(8,128)(2,1)} %param.18), kind=kLoop, calls=%fused_computation.2 | loop fusion | flops 1310720 | bytes 1048577 | tf_op jit(solution)/shard_map/jit(_where)/select_n | solution.py:212
  2.1 3.1 %collective-permute-start.5 = (bf16[256,512]{1,0:T(8,128)(2,1)S(1)}, bf16[256,512]{1,0:T(8,128)(2,1)S(1)}, u32[]{:S(2)}, u32[]{:S(2)}) collective-permute-start(bf16[256,512]{1,0:T(8,128)(2,1)S(1)} %get-tuple-element.6.rest_5_), channel_id=1, source_target_pairs={{0,2},{2,4},{4,6},{6,7},{7,5},{5,3},{3,1},{1,0},{8,9},{10,8},{12,1... | collective-permute-start | bytes 786440 | tf_op jit(solution)/shard_map/ppermute | solution.py:218
  5.1 1.6 %collective-permute-start.9 = (bf16[256,512]{1,0:T(8,128)(2,1)S(1)}, bf16[256,512]{1,0:T(8,128)(2,1)S(1)}, u32[]{:S(2)}, u32[]{:S(2)}) collective-permute-start(bf16[256,512]{1,0:T(8,128)(2,1)S(1)} %get-tuple-element.5.rest_13_), channel_id=1, source_target_pairs={{0,2},{2,4},{4,6},{6,7},{7,5},{5,3},{3,1},{1,0},{8,9},{10,8},{12,1... | collective-permute-start | bytes 786440 | tf_op jit(solution)/shard_map/ppermute | solution.py:220
  6.7 2.7 %collective-permute-done.5.rest_6_ = bf16[256,512]{1,0:T(8,128)(2,1)S(1)} collective-permute-done((bf16[256,512]{1,0:T(8,128)(2,1)S(1)}, bf16[256,512]{1,0:T(8,128)(2,1)S(1)}, u32[]{:S(2)}, u32[]{:S(2)}) %collective-permute-start.5) | collective-permute-done | bytes 262176 | tf_op jit(solution)/shard_map/ppermute | solution.py:218
  9.4 2.1 %collective-permute-start.6 = (bf16[256,512]{1,0:T(8,128)(2,1)S(1)}, bf16[256,512]{1,0:T(8,128)(2,1)S(1)}, u32[]{:S(2)}, u32[]{:S(2)}) collective-permute-start(bf16[256,512]{1,0:T(8,128)(2,1)S(1)} %collective-permute-done.5.rest_6_), channel_id=1, source_target_pairs={{0,2},{2,4},{4,6},{6,7},{7,5},{5,3},{3,1},{1,0},{8,9},{10,8},{12,1... | collective-permute-start | bytes 786440 | tf_op jit(solution)/shard_map/ppermute | solution.py:218
  12.2 2.1 %collective-permute-start.11 = (bf16[256,512]{1,0:T(8,128)(2,1)S(1)}, bf16[256,512]{1,0:T(8,128)(2,1)S(1)}, u32[]{:S(2)}, u32[]{:S(2)}) collective-permute-start(bf16[256,512]{1,0:T(8,128)(2,1)S(1)} %collective-permute-done.9.rest_14_), channel_id=1, source_target_pairs={{0,2},{2,4},{4,6},{6,7},{7,5},{5,3},{3,1},{1,0},{8,9},{10,8},{12,1... | collective-permute-start | bytes 786440 | tf_op jit(solution)/shard_map/ppermute | solution.py:220
  14.3 1.5 %collective-permute-done.6.rest_7_ = bf16[256,512]{1,0:T(8,128)(2,1)S(1)} collective-permute-done((bf16[256,512]{1,0:T(8,128)(2,1)S(1)}, bf16[256,512]{1,0:T(8,128)(2,1)S(1)}, u32[]{:S(2)}, u32[]{:S(2)}) %collective-permute-start.6) | collective-permute-done | bytes 262176 | tf_op jit(solution)/shard_map/ppermute | solution.py:218
  15.8 2.1 %collective-permute-start.7 = (bf16[256,512]{1,0:T(8,128)(2,1)S(1)}, bf16[256,512]{1,0:T(8,128)(2,1)S(1)}, u32[]{:S(2)}, u32[]{:S(2)}) collective-permute-start(bf16[256,512]{1,0:T(8,128)(2,1)S(1)} %collective-permute-done.6.rest_7_), channel_id=1, source_target_pairs={{0,2},{2,4},{4,6},{6,7},{7,5},{5,3},{3,1},{1,0},{8,9},{10,8},{12,1... | collective-permute-start | bytes 786440 | tf_op jit(solution)/shard_map/ppermute | solution.py:218
  17.9 3.4 %collective-permute-start.2 = (bf16[180,512]{1,0:T(8,128)(2,1)S(1)}, bf16[180,512]{1,0:T(8,128)(2,1)S(1)}, u32[]{:S(2)}, u32[]{:S(2)}) collective-permute-start(bf16[180,512]{1,0:T(8,128)(2,1)S(1)} %bitcast.12), channel_id=1, source_target_pairs={{0,16},{8,24},{1,17},{9,25},{2,18},{10,26},{3,19},{11,27},{4,20},{... | collective-permute-start | bytes 552968 | tf_op jit(solution)/shard_map/ppermute | solution.py:49
  21.3 1.3 %collective-permute-start.1 = (bf16[180,512]{1,0:T(8,128)(2,1)S(1)}, bf16[180,512]{1,0:T(8,128)(2,1)S(1)}, u32[]{:S(2)}, u32[]{:S(2)}) collective-permute-start(bf16[180,512]{1,0:T(8,128)(2,1)S(1)} %bitcast.13), channel_id=1, source_target_pairs={{1,0},{2,1},{3,2},{4,3},{5,4},{6,5},{7,6},{9,8},{10,9},{11,10},{12... | collective-permute-start | bytes 552968 | tf_op jit(solution)/shard_map/ppermute | solution.py:54
  23.3 4.5 %collective-permute-start = (bf16[180,512]{1,0:T(8,128)(2,1)S(1)}, bf16[180,512]{1,0:T(8,128)(2,1)S(1)}, u32[]{:S(2)}, u32[]{:S(2)}) collective-permute-start(bf16[180,512]{1,0:T(8,128)(2,1)S(1)} %bitcast.14), channel_id=1, source_target_pairs={{0,1},{1,2},{2,3},{3,4},{4,5},{5,6},{6,7},{8,9},{9,10},{10,11},{11... | collective-permute-start | bytes 552968 | tf_op jit(solution)/shard_map/ppermute | solution.py:54
  27.9 0.8 %collective-permute-done.1.rest_1_ = bf16[180,512]{1,0:T(8,128)(2,1)S(1)} collective-permute-done((bf16[180,512]{1,0:T(8,128)(2,1)S(1)}, bf16[180,512]{1,0:T(8,128)(2,1)S(1)}, u32[]{:S(2)}, u32[]{:S(2)}) %collective-permute-start.1) | collective-permute-done | bytes 184352 | tf_op jit(solution)/shard_map/ppermute | solution.py:54
  29.4 5.6 %collective-permute-start.13 = (bf16[256,512]{1,0:T(8,128)(2,1)S(1)}, bf16[256,512]{1,0:T(8,128)(2,1)S(1)}, u32[]{:S(2)}, u32[]{:S(2)}) collective-permute-start(bf16[256,512]{1,0:T(8,128)(2,1)S(1)} %collective-permute-done.11.rest_15_), channel_id=1, source_target_pairs={{0,2},{2,4},{4,6},{6,7},{7,5},{5,3},{3,1},{1,0},{8,9},{10,8},{12,1... | collective-permute-start | bytes 786440 | tf_op jit(solution)/shard_map/ppermute | solution.py:220
  35.0 1.6 %collective-permute-start.8 = (bf16[256,512]{1,0:T(8,128)(2,1)S(1)}, bf16[256,512]{1,0:T(8,128)(2,1)S(1)}, u32[]{:S(2)}, u32[]{:S(2)}) collective-permute-start(bf16[256,512]{1,0:T(8,128)(2,1)S(1)} %collective-permute-done.7.rest_8_), channel_id=1, source_target_pairs={{0,2},{2,4},{4,6},{6,7},{7,5},{5,3},{3,1},{1,0},{8,9},{10,8},{12,1... | collective-permute-start | bytes 786440 | tf_op jit(solution)/shard_map/ppermute | solution.py:218
  40.4 1.3 %collective-permute-done.8.rest_9_ = bf16[256,512]{1,0:T(8,128)(2,1)S(1)} collective-permute-done((bf16[256,512]{1,0:T(8,128)(2,1)S(1)}, bf16[256,512]{1,0:T(8,128)(2,1)S(1)}, u32[]{:S(2)}, u32[]{:S(2)}) %collective-permute-start.8) | collective-permute-done | bytes 262176 | tf_op jit(solution)/shard_map/ppermute | solution.py:218
  44.7 0.9 %copy-done.1 = bf16[1,1,180,512]{3,2,1,0:T(8,128)(2,1)S(1)} copy-done((bf16[1,1,180,512]{3,2,1,0:T(8,128)(2,1)S(1)}, bf16[1,1,180,512]{3,2,1,0:T(8,128)(2,1)}, u32[]{:S(2)}) %copy-start.1) | copy-done | bytes 184344
  45.6 0.9 %copy-done.2 = bf16[1,1,180,512]{3,2,1,0:T(8,128)(2,1)S(1)} copy-done((bf16[1,1,180,512]{3,2,1,0:T(8,128)(2,1)S(1)}, bf16[1,1,180,512]{3,2,1,0:T(8,128)(2,1)}, u32[]{:S(2)}) %copy-start.2) | copy-done | bytes 184344
  46.5 0.9 %copy-done.4 = bf16[180,512]{1,0:T(8,128)(2,1)S(1)} copy-done((bf16[180,512]{1,0:T(8,128)(2,1)S(1)}, bf16[180,512]{1,0:T(8,128)(2,1)}, u32[]{:S(2)}) %copy-start.4) | copy-done | bytes 184344
  47.4 0.9 %copy-done.6 = bf16[180,512]{1,0:T(8,128)(2,1)S(1)} copy-done((bf16[180,512]{1,0:T(8,128)(2,1)S(1)}, bf16[180,512]{1,0:T(8,128)(2,1)}, u32[]{:S(2)}) %copy-start.6) | copy-done | bytes 184344
  48.4 0.9 %copy-done.8 = bf16[180,512]{1,0:T(8,128)(2,1)S(1)} copy-done((bf16[180,512]{1,0:T(8,128)(2,1)S(1)}, bf16[180,512]{1,0:T(8,128)(2,1)}, u32[]{:S(2)}) %copy-start.8) | copy-done | bytes 184344
  49.3 0.9 %copy-done.10 = bf16[180,512]{1,0:T(8,128)(2,1)S(1)} copy-done((bf16[180,512]{1,0:T(8,128)(2,1)S(1)}, bf16[180,512]{1,0:T(8,128)(2,1)}, u32[]{:S(2)}) %copy-start.10) | copy-done | bytes 184344
  50.2 0.9 %copy-done.12 = bf16[180,512]{1,0:T(8,128)(2,1)S(1)} copy-done((bf16[180,512]{1,0:T(8,128)(2,1)S(1)}, bf16[180,512]{1,0:T(8,128)(2,1)}, u32[]{:S(2)}) %copy-start.12) | copy-done | bytes 184344
  51.1 8.3 %shard_map.109 = bf16[180,512]{1,0:T(8,128)(2,1)} custom-call(s32[13]{0:T(128)S(1)} %concatenate.9.meta, f32[2,8]{1,0:T(2,128)S(1)} %copy-done.14, s32[8]{0:T(128)S(1)} %copy-done.15, f32[1,512]{1,0:T(1,128)S(1)} %bitcast.17, bf16[180,512]{1,0:T(8,128)(2,1)S(1)} %bitcast.15, bf16[180,512]{1,0:T(8,128)(2,1)S(1)} %bitcast.16, bf16[180,512]{1,0:T(8,128)(2,1)S(1)} %copy-done.10, ...), custom_call_target="tpu_custom_call" | custom-call | tf_op jit(solution)/shard_map/pallas_call | solution.py:252
  (57 shorter events, 7.6 us)
Async XLA Ops:
  0.0 1.0 %copy-start.16 = (bf16[512,192]{0,1:T(8,128)(2,1)S(1)}, bf16[512,192]{0,1:T(8,128)(2,1)}, u32[]{:S(2)}) copy-start(bf16[512,192]{0,1:T(8,128)(2,1)} %param.19) | copy-start | bytes 589828
  1.0 10.5 %copy-start = (bf16[1,1,180,512]{3,2,1,0:T(8,128)(2,1)S(1)}, bf16[1,1,180,512]{3,2,1,0:T(8,128)(2,1)}, u32[]{:S(2)}) copy-start(bf16[1,1,180,512]{3,2,1,0:T(8,128)(2,1)} %param.11) | copy-start | bytes 552964
  2.1 7.4 %collective-permute-start.5 = (bf16[256,512]{1,0:T(8,128)(2,1)S(1)}, bf16[256,512]{1,0:T(8,128)(2,1)S(1)}, u32[]{:S(2)}, u32[]{:S(2)}) collective-permute-start(bf16[256,512]{1,0:T(8,128)(2,1)S(1)} %get-tuple-element.6.rest_5_), channel_id=1, source_target_pairs={{0,2},{2,4},{4,6},{6,7},{7,5},{5,3},{3,1},{1,0},{8,9},{10,8},{12,1... | collective-permute-start | bytes 786440 | tf_op jit(solution)/shard_map/ppermute | solution.py:218
  5.1 7.1 %collective-permute-start.9 = (bf16[256,512]{1,0:T(8,128)(2,1)S(1)}, bf16[256,512]{1,0:T(8,128)(2,1)S(1)}, u32[]{:S(2)}, u32[]{:S(2)}) collective-permute-start(bf16[256,512]{1,0:T(8,128)(2,1)S(1)} %get-tuple-element.5.rest_13_), channel_id=1, source_target_pairs={{0,2},{2,4},{4,6},{6,7},{7,5},{5,3},{3,1},{1,0},{8,9},{10,8},{12,1... | collective-permute-start | bytes 786440 | tf_op jit(solution)/shard_map/ppermute | solution.py:220
  9.4 6.4 %collective-permute-start.6 = (bf16[256,512]{1,0:T(8,128)(2,1)S(1)}, bf16[256,512]{1,0:T(8,128)(2,1)S(1)}, u32[]{:S(2)}, u32[]{:S(2)}) collective-permute-start(bf16[256,512]{1,0:T(8,128)(2,1)S(1)} %collective-permute-done.5.rest_6_), channel_id=1, source_target_pairs={{0,2},{2,4},{4,6},{6,7},{7,5},{5,3},{3,1},{1,0},{8,9},{10,8},{12,1... | collective-permute-start | bytes 786440 | tf_op jit(solution)/shard_map/ppermute | solution.py:218
  11.5 11.1 %collective-permute-start.3 = (bf16[180,512]{1,0:T(8,128)(2,1)S(1)}, bf16[180,512]{1,0:T(8,128)(2,1)S(1)}, u32[]{:S(2)}, u32[]{:S(2)}) collective-permute-start(bf16[180,512]{1,0:T(8,128)(2,1)S(1)} %bitcast.11), channel_id=1, source_target_pairs={{0,8},{1,9},{2,10},{3,11},{4,12},{5,13},{6,14},{7,15},{8,0},{9,1},... | collective-permute-start | bytes 552968 | tf_op jit(solution)/shard_map/ppermute | solution.py:230
  12.2 17.2 %collective-permute-start.11 = (bf16[256,512]{1,0:T(8,128)(2,1)S(1)}, bf16[256,512]{1,0:T(8,128)(2,1)S(1)}, u32[]{:S(2)}, u32[]{:S(2)}) collective-permute-start(bf16[256,512]{1,0:T(8,128)(2,1)S(1)} %collective-permute-done.9.rest_14_), channel_id=1, source_target_pairs={{0,2},{2,4},{4,6},{6,7},{7,5},{5,3},{3,1},{1,0},{8,9},{10,8},{12,1... | collective-permute-start | bytes 786440 | tf_op jit(solution)/shard_map/ppermute | solution.py:220
  15.8 19.2 %collective-permute-start.7 = (bf16[256,512]{1,0:T(8,128)(2,1)S(1)}, bf16[256,512]{1,0:T(8,128)(2,1)S(1)}, u32[]{:S(2)}, u32[]{:S(2)}) collective-permute-start(bf16[256,512]{1,0:T(8,128)(2,1)S(1)} %collective-permute-done.6.rest_7_), channel_id=1, source_target_pairs={{0,2},{2,4},{4,6},{6,7},{7,5},{5,3},{3,1},{1,0},{8,9},{10,8},{12,1... | collective-permute-start | bytes 786440 | tf_op jit(solution)/shard_map/ppermute | solution.py:218
  17.9 9.9 %collective-permute-start.2 = (bf16[180,512]{1,0:T(8,128)(2,1)S(1)}, bf16[180,512]{1,0:T(8,128)(2,1)S(1)}, u32[]{:S(2)}, u32[]{:S(2)}) collective-permute-start(bf16[180,512]{1,0:T(8,128)(2,1)S(1)} %bitcast.12), channel_id=1, source_target_pairs={{0,16},{8,24},{1,17},{9,25},{2,18},{10,26},{3,19},{11,27},{4,20},{... | collective-permute-start | bytes 552968 | tf_op jit(solution)/shard_map/ppermute | solution.py:49
  21.3 7.5 %collective-permute-start.1 = (bf16[180,512]{1,0:T(8,128)(2,1)S(1)}, bf16[180,512]{1,0:T(8,128)(2,1)S(1)}, u32[]{:S(2)}, u32[]{:S(2)}) collective-permute-start(bf16[180,512]{1,0:T(8,128)(2,1)S(1)} %bitcast.13), channel_id=1, source_target_pairs={{1,0},{2,1},{3,2},{4,3},{5,4},{6,5},{7,6},{9,8},{10,9},{11,10},{12... | collective-permute-start | bytes 552968 | tf_op jit(solution)/shard_map/ppermute | solution.py:54
  23.3 13.4 %collective-permute-start = (bf16[180,512]{1,0:T(8,128)(2,1)S(1)}, bf16[180,512]{1,0:T(8,128)(2,1)S(1)}, u32[]{:S(2)}, u32[]{:S(2)}) collective-permute-start(bf16[180,512]{1,0:T(8,128)(2,1)S(1)} %bitcast.14), channel_id=1, source_target_pairs={{0,1},{1,2},{2,3},{3,4},{4,5},{5,6},{6,7},{8,9},{9,10},{10,11},{11... | collective-permute-start | bytes 552968 | tf_op jit(solution)/shard_map/ppermute | solution.py:54
  27.8 11.7 %collective-permute-start.10 = (bf16[256,512]{1,0:T(8,128)(2,1)S(1)}, bf16[256,512]{1,0:T(8,128)(2,1)S(1)}, u32[]{:S(2)}, u32[]{:S(2)}) collective-permute-start(bf16[256,512]{1,0:T(8,128)(2,1)S(1)} %collective-permute-done.9.rest_14_), channel_id=1, source_target_pairs={{0,8},{1,9},{2,10},{3,11},{4,12},{5,13},{6,14},{7,15},{8,0},{9,1},... | collective-permute-start | bytes 786440 | tf_op jit(solution)/shard_map/ppermute | solution.py:222
  29.4 10.5 %collective-permute-start.16 = (bf16[256,512]{1,0:T(8,128)(2,1)S(1)}, bf16[256,512]{1,0:T(8,128)(2,1)S(1)}, u32[]{:S(2)}, u32[]{:S(2)}) collective-permute-start(bf16[256,512]{1,0:T(8,128)(2,1)S(1)} %collective-permute-done.5.rest_6_), channel_id=1, source_target_pairs={{0,8},{1,9},{2,10},{3,11},{4,12},{5,13},{6,14},{7,15},{8,0},{9,1},... | collective-permute-start | bytes 786440 | tf_op jit(solution)/shard_map/ppermute | solution.py:221
  29.4 10.6 %collective-permute-start.13 = (bf16[256,512]{1,0:T(8,128)(2,1)S(1)}, bf16[256,512]{1,0:T(8,128)(2,1)S(1)}, u32[]{:S(2)}, u32[]{:S(2)}) collective-permute-start(bf16[256,512]{1,0:T(8,128)(2,1)S(1)} %collective-permute-done.11.rest_15_), channel_id=1, source_target_pairs={{0,2},{2,4},{4,6},{6,7},{7,5},{5,3},{3,1},{1,0},{8,9},{10,8},{12,1... | collective-permute-start | bytes 786440 | tf_op jit(solution)/shard_map/ppermute | solution.py:220
  35.0 6.7 %collective-permute-start.8 = (bf16[256,512]{1,0:T(8,128)(2,1)S(1)}, bf16[256,512]{1,0:T(8,128)(2,1)S(1)}, u32[]{:S(2)}, u32[]{:S(2)}) collective-permute-start(bf16[256,512]{1,0:T(8,128)(2,1)S(1)} %collective-permute-done.7.rest_8_), channel_id=1, source_target_pairs={{0,2},{2,4},{4,6},{6,7},{7,5},{5,3},{3,1},{1,0},{8,9},{10,8},{12,1... | collective-permute-start | bytes 786440 | tf_op jit(solution)/shard_map/ppermute | solution.py:218
  37.3 1.4 %collective-permute-start.4 = (bf16[180,512]{1,0:T(8,128)(2,1)S(1)}, bf16[180,512]{1,0:T(8,128)(2,1)S(1)}, u32[]{:S(2)}, u32[]{:S(2)}) collective-permute-start(bf16[180,512]{1,0:T(8,128)(2,1)S(1)} %collective-permute-done.2.rest_2_), channel_id=1, source_target_pairs={{0,8},{1,9},{2,10},{3,11},{4,12},{5,13},{6,14},{7,15},{8,0},{9,1},... | collective-permute-start | bytes 552968 | tf_op jit(solution)/shard_map/ppermute | solution.py:231
  39.4 4.5 %collective-permute-start.12 = (bf16[256,512]{1,0:T(8,128)(2,1)S(1)}, bf16[256,512]{1,0:T(8,128)(2,1)S(1)}, u32[]{:S(2)}, u32[]{:S(2)}) collective-permute-start(bf16[256,512]{1,0:T(8,128)(2,1)S(1)} %collective-permute-done.11.rest_15_), channel_id=1, source_target_pairs={{0,8},{1,9},{2,10},{3,11},{4,12},{5,13},{6,14},{7,15},{8,0},{9,1},... | collective-permute-start | bytes 786440 | tf_op jit(solution)/shard_map/ppermute | solution.py:222
  39.6 4.4 %collective-permute-start.17 = (bf16[256,512]{1,0:T(8,128)(2,1)S(1)}, bf16[256,512]{1,0:T(8,128)(2,1)S(1)}, u32[]{:S(2)}, u32[]{:S(2)}) collective-permute-start(bf16[256,512]{1,0:T(8,128)(2,1)S(1)} %collective-permute-done.6.rest_7_), channel_id=1, source_target_pairs={{0,8},{1,9},{2,10},{3,11},{4,12},{5,13},{6,14},{7,15},{8,0},{9,1},... | collective-permute-start | bytes 786440 | tf_op jit(solution)/shard_map/ppermute | solution.py:221
  39.9 4.0 %collective-permute-start.18 = (bf16[256,512]{1,0:T(8,128)(2,1)S(1)}, bf16[256,512]{1,0:T(8,128)(2,1)}, u32[]{:S(2)}, u32[]{:S(2)}) collective-permute-start(bf16[256,512]{1,0:T(8,128)(2,1)S(1)} %collective-permute-done.7.rest_8_), channel_id=1, source_target_pairs={{0,8},{1,9},{2,10},{3,11},{4,12},{5,13},{6,14},{7,15},{8,0},{9,1},... | collective-permute-start | bytes 786440 | tf_op jit(solution)/shard_map/ppermute | solution.py:221
  40.1 3.9 %collective-permute-start.14 = (bf16[256,512]{1,0:T(8,128)(2,1)S(1)}, bf16[256,512]{1,0:T(8,128)(2,1)}, u32[]{:S(2)}, u32[]{:S(2)}) collective-permute-start(bf16[256,512]{1,0:T(8,128)(2,1)S(1)} %collective-permute-done.13.rest_16_), channel_id=1, source_target_pairs={{0,8},{1,9},{2,10},{3,11},{4,12},{5,13},{6,14},{7,15},{8,0},{9,1},... | collective-permute-start | bytes 786440 | tf_op jit(solution)/shard_map/ppermute | solution.py:222
  41.7 2.2 %collective-permute-start.15 = (bf16[256,512]{1,0:T(8,128)(2,1)S(1)}, bf16[256,512]{1,0:T(8,128)(2,1)}, u32[]{:S(2)}, u32[]{:S(2)}) collective-permute-start(bf16[256,512]{1,0:T(8,128)(2,1)S(1)} %collective-permute-done.8.rest_9_), channel_id=1, source_target_pairs={{0,8},{1,9},{2,10},{3,11},{4,12},{5,13},{6,14},{7,15},{8,0},{9,1},... | collective-permute-start | bytes 786440 | tf_op jit(solution)/shard_map/ppermute | solution.py:223
  44.7 0.9 %copy-start.1 = (bf16[1,1,180,512]{3,2,1,0:T(8,128)(2,1)S(1)}, bf16[1,1,180,512]{3,2,1,0:T(8,128)(2,1)}, u32[]{:S(2)}) copy-start(bf16[1,1,180,512]{3,2,1,0:T(8,128)(2,1)} %param.11) | copy-start | bytes 552964
  45.6 0.9 %copy-start.2 = (bf16[1,1,180,512]{3,2,1,0:T(8,128)(2,1)S(1)}, bf16[1,1,180,512]{3,2,1,0:T(8,128)(2,1)}, u32[]{:S(2)}) copy-start(bf16[1,1,180,512]{3,2,1,0:T(8,128)(2,1)} %param.12) | copy-start | bytes 552964
  49.3 0.9 %copy-start.10 = (bf16[180,512]{1,0:T(8,128)(2,1)S(1)}, bf16[180,512]{1,0:T(8,128)(2,1)}, u32[]{:S(2)}) copy-start(bf16[180,512]{1,0:T(8,128)(2,1)} %copy-done.9) | copy-start | bytes 552964
  (14 other events, 10.4 us)

commit v2 on v1

--- a/solution.py
+++ b/solution.py
@@ -20,14 +20,23 @@
 fresh_share = 0.6
 LOG2E = 1.4426950408889634
 FAR = -1e30
+TIE = 9
+LARGE = 60 * 1024 * 1024
 
 AXES = ("frame", "band")
 BF = jnp.bfloat16
 F32 = jnp.float32
 
 
-def ring_band(pos, n):
-    return jnp.where(pos < n // 2, 2 * pos, 2 * (n - 1 - pos) + 1)
+def slot_bands(band, parity, n):
+    even = lax.rem(band, 2) == 0
+    pos = jnp.where(even, band // 2, n - 1 - band // 2)
+    half = n // 2
+    bands = []
+    for away in [*range(0, half + 1), *range(-1, -half, -1)]:
+        p = lax.rem(pos + jnp.where(parity == 0, n - away, n + away), n)
+        bands.append(jnp.where(p < half, 2 * p, 2 * (n - 1 - p) + 1))
+    return bands
 
 
 def ring_pairs(nf, n):
@@ -40,18 +49,21 @@
     return pairs
 
 
-def core_pairs(nf, n):
-    return [(f * n + b, (f ^ 1) * n + b) for f in range(nf) for b in range(n)]
-
-
-def shift_frame(block, hop):
+def core_pairs(nf, n, first=0, stride=1):
+    return [(f * n + b, (f ^ 1) * n + b) for f in range(first, nf, stride) for b in range(n)]
+
+
+def rotate_frame(block, hop):
     nf = lax.axis_size("frame")
-    return lax.ppermute(block, "frame", [(i, i + hop) for i in range(nf - hop)])
-
-
-def shift_band(block, hop):
+    return lax.ppermute(block, "frame", [(i, (i + hop) % nf) for i in range(nf)])
+
+
+def exchange_bands(block, first):
     n = lax.axis_size("band")
-    return lax.ppermute(block, "band", [(i, i + hop) for i in range(n) if 0 <= i + hop < n])
+    pairs = []
+    for b in range(first, n - 1, 2):
+        pairs += [(b, b + 1), (b + 1, b)]
+    return lax.ppermute(block, "band", pairs)
 
 
 def unit_rows(block):
@@ -60,32 +72,32 @@
     return (shaped * lax.rsqrt(mean + epsilon)).reshape(block.shape)
 
 
+def norm_kernel(gain_ref, state_ref, normed_ref):
+    x = state_ref[...].astype(F32)
+    scale = lax.rsqrt(jnp.mean(x * x, axis=-1, keepdims=True) + epsilon)
+    normed_ref[...] = (x * scale * gain_ref[...]).astype(BF)
+
+
 def kernel(
-    slots, n_time, n_bands, total_levels,
-    meta, scales, tally, gain_ref, state_ref, noise_ref, *rest,
+    n_time, n_bands, total_levels,
+    meta, scales, tally, *rest,
 ):
-    space_refs = (state_ref,) + rest[:2]
-    time_refs = (state_ref,) + rest[2 : 1 + n_time]
-    rest = rest[1 + n_time :]
-    first, second = rest[:slots], rest[slots : 2 * slots]
-    out_ref = rest[2 * slots]
-    weights, final, qs, ks, vs, mix = rest[2 * slots + 1 :]
-    lon, width = state_ref.shape
-    parity, shift, level = meta[slots], meta[slots + 1], meta[slots + 2]
-    frame, band = meta[slots + 3], meta[slots + 4]
-    r3 = 3 * width // n_bands
+    slots, states = n_bands, 2 + n_time
+    normed, rest = rest[0], rest[1:]
+    mine, rest = rest[:slots], rest[slots:]
+    other, rest = rest[:slots], rest[slots:]
+    out_ref, weights, final, qs, ks, vs, mix = rest
+    lon, width = out_ref.shape
+    band, frame, shift, level = meta[0], meta[1], meta[2], meta[3]
+    parity = lax.rem(frame, 2)
     r1 = width // n_bands
-
-    for group, which in ((first, parity), (second, 1 - parity)):
-        for i, ref in enumerate(group):
-            b = meta[i]
-            weights[which, pl.ds(pl.multiple_of(b * r3, 16), r3), :] = ref[0:r3, :]
-            final[which, pl.ds(pl.multiple_of(b * r1, 16), r1), :] = ref[r3 : r3 + r1, :]
-
-    def normed(ref):
-        x = ref[...].astype(F32)
-        scale = lax.rsqrt(jnp.mean(x * x, axis=-1, keepdims=True) + epsilon)
-        return (x * scale * gain_ref[...]).astype(BF)
+    r3 = 3 * r1
+
+    bands = slot_bands(band, parity, n_bands)
+    for group, which in ((mine, parity), (other, 1 - parity)):
+        for b, ref in zip(bands, group):
+            weights[which, pl.ds(pl.multiple_of(b * r3, 16), r3), :] = ref[:r3, :]
+            final[which, pl.ds(pl.multiple_of(b * r1, 16), r1), :] = ref[r3:, :]
 
     nt = (((1,), (1,)), ((), ()))
 
@@ -94,18 +106,12 @@
             weights[which, part * width : (part + 1) * width, :], x, nt, preferred_element_type=F32
         )
 
-    own = normed(state_ref)
+    own = normed[0]
     qs[0] = unit_rows(proj(0, 0, own)).astype(BF)
-    for j, ref in enumerate(space_refs):
-        x = own if j == 0 else normed(ref)
+    for j in range(3):
+        x = normed[j]
         ks[j] = unit_rows(proj(0, 1, x)).astype(BF)
         vs[j] = proj(0, 2, x).astype(BF)
-    qs[1] = unit_rows(proj(1, 0, own)).astype(BF)
-    for j, ref in enumerate(time_refs):
-        x = own if j == 0 else normed(ref)
-        ks[3 + j] = unit_rows(proj(1, 1, x)).astype(BF)
-        vs[3 + j] = proj(1, 2, x).astype(BF)
-
     kcol = lax.broadcasted_iota(jnp.int32, (lon, lon), 0)
     qcol = lax.broadcasted_iota(jnp.int32, (lon, lon), 1)
 
@@ -118,8 +124,9 @@
         return w
 
     same = window(kcol) == window(qcol)
+    side = 1 - 2 * (band % 2)
     biases = []
-    for j, off in enumerate((0, -1, 1)):
+    for j, off in enumerate((0, side, -side)):
         row = band + off
         exists = (row >= 0) & (row < n_bands)
         limit = jnp.where(exists, tally[jnp.clip(row, 0, n_bands - 1)], 0)
@@ -146,6 +153,11 @@
         )
         mix[0, lo:hi, :] = o.astype(BF)
 
+    qs[1] = unit_rows(proj(1, 0, own)).astype(BF)
+    for j in range(n_time):
+        x = normed[j + 2 if j else 0]
+        ks[3 + j] = unit_rows(proj(1, 1, x)).astype(BF)
+        vs[3 + j] = proj(1, 2, x).astype(BF)
     odd = frame % 2
     back = [0, 2, jnp.where(odd == 1, 1, -1), jnp.where(odd == 1, 3, 1), jnp.where(odd == 1, -1, 3)]
     allow = [(b >= 0) & (b <= PRIOR_SNAPSHOTS) & (frame - b >= 0) for b in back]
@@ -178,8 +190,8 @@
         return sigma_low * jnp.exp(power * math.log(sigma_high / sigma_low))
 
     s, s_next = sigma_of(level), sigma_of(level - 1)
-    state = state_ref[...].astype(F32)
-    fresh = noise_ref[...].astype(F32)
+    state = normed[states].astype(F32)
+    fresh = normed[states + 1].astype(F32)
     denoised = state / (1.0 + s * s) + s * lax.rsqrt(1.0 + s * s) * update
     stepped = denoised + s_next * (keep_share * (state - denoised) / s + fresh_share * fresh)
     out_ref[...] = jnp.where(level == 0, sigma_high * fresh, stepped).astype(BF)
@@ -206,53 +218,57 @@
     state = noisy_snapshot_stack.reshape(lon, width)
     noise = gaussian_perturbation.reshape(lon, width)
 
+    smem = pl.BlockSpec(memory_space=pltpu.SMEM)
+    vmem = pl.BlockSpec(memory_space=pltpu.VMEM)
+    hbm = pl.BlockSpec(memory_space=pltpu.HBM)
+    gain = normalizer_scaling.reshape(1, width)
+    normed = pl.pallas_call(
+        norm_kernel,
+        out_shape=jax.ShapeDtypeStruct((lon, width), BF),
+        in_specs=[vmem, vmem],
+        out_specs=vmem,
+        compiler_params=pltpu.CompilerParams(vmem_limit_bytes=LARGE),
+        name="norm",
+    )(gain, state)
+
     chunk_a = jnp.concatenate([local_projection_matrices, final_projection_matrices[:width]], axis=1).T
     chunk_b = jnp.concatenate([time_projection_matrices, final_projection_matrices[width:]], axis=1).T
     own0 = jnp.where(parity == 0, chunk_a, chunk_b)
     own1 = jnp.where(parity == 0, chunk_b, chunk_a)
 
+    meta = jnp.stack(
+        [band, frame, partition_longitude_starts[0], snapshot_noise_indices[0]]
+    ).astype(jnp.int32)
     ring, core = ring_pairs(nf, n), core_pairs(nf, n)
     half = n // 2
     chain0, chain1 = [own0], [own1]
+    partners = exchange_bands(normed, 0)
+    others = exchange_bands(normed, 1)
+    two_back = rotate_frame(normed, 2)
     for h in range(half):
-        chain0.append(lax.ppermute(chain0[-1], AXES, ring))
+        a, b = chain0[-1], chain1[-1]
+        if h == 1:
+            a, meta = lax.optimization_barrier((a, meta))
+        chain0.append(lax.ppermute(a, AXES, ring))
         if h < half - 1:
-            chain1.append(lax.ppermute(chain1[-1], AXES, ring))
+            chain1.append(lax.ppermute(b, AXES, ring))
     swap0 = [lax.ppermute(c, AXES, core) for c in chain0[1:half]]
     swap1 = [lax.ppermute(c, AXES, core) for c in chain1[1:half]]
     swap_last = lax.ppermute(chain0[half], AXES, core)
-    first = chain0 + swap1
-    second = chain1 + [swap_last] + swap0
-
-    above = shift_band(state, 1)
-    below = shift_band(state, -1)
-    two_back = shift_frame(state, 2)
-    partner = lax.ppermute(state, AXES, core)
+    mine = chain0 + swap1
+    other = chain1 + [swap_last] + swap0
+    partner = lax.ppermute(normed, AXES, core)
     partner_two = lax.ppermute(two_back, AXES, core)
     past = [two_back, partner, partner_two]
     if nf > 4:
-        past.append(shift_frame(state, 3))
-
-    pos = jnp.where(band % 2 == 0, band // 2, n - 1 - band // 2)
-    away = jnp.array(list(range(0, -half - 1, -1)) + list(range(1, half)), jnp.int32)
-    slot_pos = (pos + jnp.where(parity == 0, away, -away)) % n
-    meta = jnp.concatenate(
-        [
-            ring_band(slot_pos, n),
-            jnp.stack(
-                [parity, partition_longitude_starts[0], snapshot_noise_indices[0], frame, band]
-            ),
-        ]
-    ).astype(jnp.int32)
-
-    smem = pl.BlockSpec(memory_space=pltpu.SMEM)
-    vmem = pl.BlockSpec(memory_space=pltpu.VMEM)
-    operands = [state, noise, above, below] + past + first + second
+        past.append(rotate_frame(normed, 3))
+
     n_time = 1 + len(past)
+    rows_in = jnp.stack([normed, partners, others, *past, state, noise])
     out = pl.pallas_call(
-        functools.partial(kernel, n, n_time, n, nf),
+        functools.partial(kernel, n_time, n, nf),
         out_shape=jax.ShapeDtypeStruct((lon, width), BF),
-        in_specs=[smem] * 3 + [vmem] * (1 + len(operands)),
+        in_specs=[smem] * 3 + [vmem] * (1 + 2 * n),
         out_specs=vmem,
         scratch_shapes=[
             pltpu.VMEM((2, 3 * width, width), BF),
@@ -262,8 +278,12 @@
             pltpu.VMEM((3 + n_time, width, lon), BF),
             pltpu.VMEM((2, width, lon), BF),
         ],
-        compiler_params=pltpu.CompilerParams(vmem_limit_bytes=40 * 1024 * 1024),
-    )(meta, head_score_scales, latitude_patch_tally, normalizer_scaling.reshape(1, width), *operands)
+        compiler_params=pltpu.CompilerParams(vmem_limit_bytes=20 * 1024 * 1024),
+        name="block",
+    )(
+        meta, head_score_scales, latitude_patch_tally,
+        rows_in, *mine, *other,
+    )
     return out.reshape(noisy_snapshot_stack.shape)
 
 

time: 59.9 us -> 44.2 us (0.74)
  local copies, waits for them, and re-layouts: 12.2 us -> 1.93 us
  starting transfers between devices: 28.5 us -> 20.7 us
  Pallas kernels: 8.32 us -> 9.83 us
  waiting for transfers between devices: 7.85 us -> 8.87 us
    unnamed x38 -> x15, local copies, waits for them, and re-layouts: 11.2 us -> 1.04 us
    ppermute x11, starting transfers between devices: 27.3 us -> 18.4 us  [the longest x4 7.86 us: body(): chain0.append(lax.ppermute(a, AXES, ring))]
    pallas_call x1 -> x2, Pallas kernels: 8.32 us -> 9.83 us  [the longest x1 8.05 us: body(): pl.pallas_call(functools.partial(kernel, n_time, n, nf), out_shape=jax.Sh...]
    ppermute x1, waiting for transfers between devices: 0.01 us -> 1.44 us  [body(): swap_last = lax.ppermute(chain0[half], AXES, core)]
    ppermute x1, waiting for transfers between devices: 0.75 us -> 0.01 us  [body(): partner_two = lax.ppermute(two_back, AXES, core)]
  transfers between devices with their start and end apart: 19 -> 19, of which waited for: 6 -> 6; matrix products, arithmetic and copies ran while one was open for 0% -> 3% of each run, Pallas kernels for 0% -> 4%
where the time goes in v2:
time: 44.2 us; the launch traced here: 44 us
  starting transfers between devices  20.7 us (47%)
  Pallas kernels  9.83 us (22%)
  waiting for transfers between devices  8.87 us (20%)
  local copies, waits for them, and re-layouts  1.93 us (4%)
  between operations  1.48 us (3%)
  other arithmetic  1.19 us (3%)
    pallas_call x1, Pallas kernels, body(): pl.pallas_call(functools.partial(kernel, n_time, n, nf), out_shape=jax.Sh...  8.05 us
    ppermute x4, starting transfers between devices, body(): chain0.append(lax.ppermute(a, AXES, ring))  7.86 us
    ppermute x3, starting transfers between devices, body(): chain1.append(lax.ppermute(b, AXES, ring))  7.81 us
    ppermute x4, waiting for transfers between devices, body(): chain0.append(lax.ppermute(a, AXES, ring))  6.07 us
    ppermute x1, starting transfers between devices, rotate_frame(): lax.ppermute(block, 'frame', [(i, (i + hop) % nf) for i in range(nf)])  2 us
    pallas_call x1, Pallas kernels, body(): pl.pallas_call(norm_kernel, out_shape=jax.ShapeDtypeStruct((lon, width),...  1.78 us
    ppermute x1, waiting for transfers between devices, body(): swap_last = lax.ppermute(chain0[half], AXES, core)  1.44 us
    ppermute x3, waiting for transfers between devices, body(): chain1.append(lax.ppermute(b, AXES, ring))  1.34 us
  transfers between devices with their start and end apart: 19, of which 6 were waited for; matrix products, arithmetic and copies ran while one was open for 3% of the time, Pallas kernels for 4%

profile of v2, /device:TPU:0, one launch (start us, length us, event | category | flops | bytes accessed | tf_op | source)
XLA Modules:
  0.0 44.0 jit_solution(13376974392788173076)
XLA Ops:
  0.0 0.9 %fusion = (bf16[512,64]{0,1:T(8,128)(2,1)S(1)}, bf16[512,64]{0,1:T(8,128)(2,1)S(1)}) fusion(bf16[1024,64]{0,1:T(8,128)(2,1)} %param.19), kind=kLoop, calls=%fused_computation.13 | loop fusion | bytes 262144 | tf_op jit(solution)/shard_map/slice | solution.py:234
  0.9 1.1 %select_bitcast_fusion = (bf16[256,512]{1,0:T(8,128)(2,1)S(1)}, bf16[256,512]{1,0:T(8,128)(2,1)S(1)}) fusion(pred[]{:T(512)S(6)} %eq.6, bf16[512,64]{0,1:T(8,128)(2,1)S(1)} %get-tuple-element.12, bf16[512,192]{0,1:T(8,128)(2,1)} %param.18, bf16[512,64]{0,1:T(8,128)(2,1)S(1)} %get-tuple-element.11, bf16[512,192]{0,1:T(8,128)(2,1)} %param.17), kind=kLoop, calls=%fused_computation.2 | loop fusion | flops 1310720 | bytes 1048577 | tf_op jit(solution)/shard_map/jit(_where)/select_n | solution.py:237
  2.0 3.1 %collective-permute-start = (bf16[256,512]{1,0:T(8,128)(2,1)S(1)}, bf16[256,512]{1,0:T(8,128)(2,1)S(1)}, u32[]{:S(2)}, u32[]{:S(2)}) collective-permute-start(bf16[256,512]{1,0:T(8,128)(2,1)S(1)} %get-tuple-element.10.rest_1_), channel_id=1, source_target_pairs={{0,2},{2,4},{4,6},{6,7},{7,5},{5,3},{3,1},{1,0},{8,9},{10,8},{12,1... | collective-permute-start | bytes 786440 | tf_op jit(solution)/shard_map/ppermute | solution.py:252
  5.1 1.8 %norm.1 = bf16[180,512]{1,0:T(8,128)(2,1)} custom-call(f32[1,512]{1,0:T(1,128)} %bitcast.26, bf16[180,512]{1,0:T(8,128)(2,1)} %bitcast.25), custom_call_target="tpu_custom_call" | custom-call | tf_op jit(solution)/shard_map/norm/pallas_call | solution.py:225
  6.9 0.7 %collective-permute-start.2 = (bf16[180,512]{1,0:T(8,128)(2,1)}, bf16[180,512]{1,0:T(8,128)(2,1)S(1)}, u32[]{:S(2)}, u32[]{:S(2)}) collective-permute-start(bf16[180,512]{1,0:T(8,128)(2,1)} %norm.1), channel_id=1, source_target_pairs={{1,2},{2,1},{3,4},{4,3},{5,6},{6,5},{9,10},{10,9},{11,12},{12,11},... | collective-permute-start | bytes 552968 | tf_op jit(solution)/shard_map/ppermute | solution.py:66
  7.6 2.0 %collective-permute-start.3 = (bf16[180,512]{1,0:T(8,128)(2,1)}, bf16[180,512]{1,0:T(8,128)(2,1)S(1)}, u32[]{:S(2)}, u32[]{:S(2)}) collective-permute-start(bf16[180,512]{1,0:T(8,128)(2,1)} %norm.1), channel_id=1, source_target_pairs={{0,16},{8,24},{16,0},{24,8},{1,17},{9,25},{17,1},{25,9},{2,18},{10... | collective-permute-start | bytes 552968 | tf_op jit(solution)/shard_map/ppermute | solution.py:58
  9.6 4.3 %collective-permute-start.9 = (bf16[256,512]{1,0:T(8,128)(2,1)S(1)}, bf16[256,512]{1,0:T(8,128)(2,1)S(1)}, u32[]{:S(2)}, u32[]{:S(2)}) collective-permute-start(bf16[256,512]{1,0:T(8,128)(2,1)S(1)} %get-tuple-element.9.rest_9_), channel_id=1, source_target_pairs={{0,2},{2,4},{4,6},{6,7},{7,5},{5,3},{3,1},{1,0},{8,9},{10,8},{12,1... | collective-permute-start | bytes 786440 | tf_op jit(solution)/shard_map/ppermute | solution.py:254
  15.2 1.6 %collective-permute-start.6 = (bf16[256,512]{1,0:T(8,128)(2,1)S(1)}, bf16[256,512]{1,0:T(8,128)(2,1)S(1)}, u32[]{:S(2)}, u32[]{:S(2)}) collective-permute-start(bf16[256,512]{1,0:T(8,128)(2,1)S(1)} %collective-permute-done.rest_2_), channel_id=1, source_target_pairs={{0,2},{2,4},{4,6},{6,7},{7,5},{5,3},{3,1},{1,0},{8,9},{10,8},{12,1... | collective-permute-start | bytes 786440 | tf_op jit(solution)/shard_map/ppermute | solution.py:252
  16.8 0.9 %bitcast_dynamic-update-slice_fusion.7 = bf16[8,180,512]{2,1,0:T(8,128)(2,1)S(1)} fusion(bf16[180,512]{1,0:T(8,128)(2,1)} %norm.1), kind=kLoop, calls=%fused_computation.11 | loop fusion | bytes 372736
  17.9 0.5 %collective-permute-start.5 = (bf16[180,512]{1,0:T(8,128)(2,1)S(1)}, bf16[180,512]{1,0:T(8,128)(2,1)S(1)}, u32[]{:S(2)}, u32[]{:S(2)}) collective-permute-start(bf16[180,512]{1,0:T(8,128)(2,1)S(1)} %collective-permute-done.3), channel_id=1, source_target_pairs={{0,8},{1,9},{2,10},{3,11},{4,12},{5,13},{6,14},{7,15},{8,0},{9,1},... | collective-permute-start | bytes 552968 | tf_op jit(solution)/shard_map/ppermute | solution.py:261
  18.4 1.8 %collective-permute-start.11 = (bf16[256,512]{1,0:T(8,128)(2,1)S(1)}, bf16[256,512]{1,0:T(8,128)(2,1)S(1)}, u32[]{:S(2)}, u32[]{:S(2)}) collective-permute-start(bf16[256,512]{1,0:T(8,128)(2,1)S(1)} %collective-permute-done.9.rest_10_), channel_id=1, source_target_pairs={{0,2},{2,4},{4,6},{6,7},{7,5},{5,3},{3,1},{1,0},{8,9},{10,8},{12,1... | collective-permute-start | bytes 786440 | tf_op jit(solution)/shard_map/ppermute | solution.py:254
  20.2 1.4 %collective-permute-done.6.rest_3_ = bf16[256,512]{1,0:T(8,128)(2,1)S(1)} collective-permute-done((bf16[256,512]{1,0:T(8,128)(2,1)S(1)}, bf16[256,512]{1,0:T(8,128)(2,1)S(1)}, u32[]{:S(2)}, u32[]{:S(2)}) %collective-permute-start.6) | collective-permute-done | bytes 262176 | tf_op jit(solution)/shard_map/ppermute | solution.py:252
  21.6 1.6 %collective-permute-start.7 = (bf16[256,512]{1,0:T(8,128)(2,1)S(1)}, bf16[256,512]{1,0:T(8,128)(2,1)S(1)}, u32[]{:S(2)}, u32[]{:S(2)}) collective-permute-start(bf16[256,512]{1,0:T(8,128)(2,1)S(1)} %collective-permute-done.6.rest_3_), channel_id=1, source_target_pairs={{0,2},{2,4},{4,6},{6,7},{7,5},{5,3},{3,1},{1,0},{8,9},{10,8},{12,1... | collective-permute-start | bytes 786440 | tf_op jit(solution)/shard_map/ppermute | solution.py:252
  23.3 1.0 %collective-permute-start.10 = (bf16[256,512]{1,0:T(8,128)(2,1)S(1)}, bf16[256,512]{1,0:T(8,128)(2,1)S(1)}, u32[]{:S(2)}, u32[]{:S(2)}) collective-permute-start(bf16[256,512]{1,0:T(8,128)(2,1)S(1)} %collective-permute-done.9.rest_10_), channel_id=1, source_target_pairs={{0,8},{1,9},{2,10},{3,11},{4,12},{5,13},{6,14},{7,15},{8,0},{9,1},... | collective-permute-start | bytes 786440 | tf_op jit(solution)/shard_map/ppermute | solution.py:256
  24.3 0.1 collective-permute-start.16
  24.4 0.4 %collective-permute-done.11.rest_11_ = bf16[256,512]{1,0:T(8,128)(2,1)S(1)} collective-permute-done((bf16[256,512]{1,0:T(8,128)(2,1)S(1)}, bf16[256,512]{1,0:T(8,128)(2,1)S(1)}, u32[]{:S(2)}, u32[]{:S(2)}) %collective-permute-start.11) | collective-permute-done | bytes 262176 | tf_op jit(solution)/shard_map/ppermute | solution.py:254
  24.8 1.7 %collective-permute-start.13 = (bf16[256,512]{1,0:T(8,128)(2,1)S(1)}, bf16[256,512]{1,0:T(8,128)(2,1)S(1)}, u32[]{:S(2)}, u32[]{:S(2)}) collective-permute-start(bf16[256,512]{1,0:T(8,128)(2,1)S(1)} %collective-permute-done.11.rest_11_), channel_id=1, source_target_pairs={{0,2},{2,4},{4,6},{6,7},{7,5},{5,3},{3,1},{1,0},{8,9},{10,8},{12,1... | collective-permute-start | bytes 786440 | tf_op jit(solution)/shard_map/ppermute | solution.py:254
  26.6 1.4 %collective-permute-done.7.rest_4_ = bf16[256,512]{1,0:T(8,128)(2,1)S(1)} collective-permute-done((bf16[256,512]{1,0:T(8,128)(2,1)S(1)}, bf16[256,512]{1,0:T(8,128)(2,1)S(1)}, u32[]{:S(2)}, u32[]{:S(2)}) %collective-permute-start.7) | collective-permute-done | bytes 262176 | tf_op jit(solution)/shard_map/ppermute | solution.py:252
  28.0 1.6 %collective-permute-start.8 = (bf16[256,512]{1,0:T(8,128)(2,1)S(1)}, bf16[256,512]{1,0:T(8,128)(2,1)S(1)}, u32[]{:S(2)}, u32[]{:S(2)}) collective-permute-start(bf16[256,512]{1,0:T(8,128)(2,1)S(1)} %collective-permute-done.7.rest_4_), channel_id=1, source_target_pairs={{0,2},{2,4},{4,6},{6,7},{7,5},{5,3},{3,1},{1,0},{8,9},{10,8},{12,1... | collective-permute-start | bytes 786440 | tf_op jit(solution)/shard_map/ppermute | solution.py:252
  29.7 0.5 %collective-permute-start.17 = (bf16[256,512]{1,0:T(8,128)(2,1)S(1)}, bf16[256,512]{1,0:T(8,128)(2,1)S(1)}, u32[]{:S(2)}, u32[]{:S(2)}) collective-permute-start(bf16[256,512]{1,0:T(8,128)(2,1)S(1)} %collective-permute-done.6.rest_3_), channel_id=1, source_target_pairs={{0,8},{1,9},{2,10},{3,11},{4,12},{5,13},{6,14},{7,15},{8,0},{9,1},... | collective-permute-start | bytes 786440 | tf_op jit(solution)/shard_map/ppermute | solution.py:255
  30.3 0.9 %collective-permute-done.13.rest_12_ = bf16[256,512]{1,0:T(8,128)(2,1)S(1)} collective-permute-done((bf16[256,512]{1,0:T(8,128)(2,1)S(1)}, bf16[256,512]{1,0:T(8,128)(2,1)S(1)}, u32[]{:S(2)}, u32[]{:S(2)}) %collective-permute-start.13) | collective-permute-done | bytes 262176 | tf_op jit(solution)/shard_map/ppermute | solution.py:254
  31.2 3.2 %collective-permute-done.8.rest_5_ = bf16[256,512]{1,0:T(8,128)(2,1)S(1)} collective-permute-done((bf16[256,512]{1,0:T(8,128)(2,1)S(1)}, bf16[256,512]{1,0:T(8,128)(2,1)S(1)}, u32[]{:S(2)}, u32[]{:S(2)}) %collective-permute-start.8) | collective-permute-done | bytes 262176 | tf_op jit(solution)/shard_map/ppermute | solution.py:252
  34.5 1.4 %collective-permute-done.15.rest_13_ = bf16[256,512]{1,0:T(8,128)(2,1)S(1)} collective-permute-done((bf16[256,512]{1,0:T(8,128)(2,1)S(1)}, bf16[256,512]{1,0:T(8,128)(2,1)S(1)}, u32[]{:S(2)}, u32[]{:S(2)}) %collective-permute-start.15) | collective-permute-done | bytes 262176 | tf_op jit(solution)/shard_map/ppermute | solution.py:257
  35.9 8.0 %block.1 = bf16[180,512]{1,0:T(8,128)(2,1)} custom-call(s32[4]{0:T(128)S(1)} %pad_add_fusion.meta, f32[2,8]{1,0:T(2,128)S(1)} %copy-done, s32[8]{0:T(128)S(1)} %copy-done.1, bf16[8,180,512]{2,1,0:T(8,128)(2,1)S(1)} %bitcast_dynamic-update-slice_fusion.rest_0_, bf16[256,512]{1,0:T(8,128)(2,1)S(1)} %get-tuple-element.10.rest_1_, ...), custom_call_target="tpu_custom_call" | custom-call | tf_op jit(solution)/shard_map/block/pallas_call | solution.py:268
  (35 shorter events, 0.5 us)
Async XLA Ops:
  2.0 32.4 %copy-start.2 = (bf16[1,1,180,512]{3,2,1,0:T(8,128)(2,1)S(1)}, bf16[1,1,180,512]{3,2,1,0:T(8,128)(2,1)}, u32[]{:S(2)}) copy-start(bf16[1,1,180,512]{3,2,1,0:T(8,128)(2,1)} %param.10) | copy-start | bytes 552964
  2.0 13.2 %collective-permute-start = (bf16[256,512]{1,0:T(8,128)(2,1)S(1)}, bf16[256,512]{1,0:T(8,128)(2,1)S(1)}, u32[]{:S(2)}, u32[]{:S(2)}) collective-permute-start(bf16[256,512]{1,0:T(8,128)(2,1)S(1)} %get-tuple-element.10.rest_1_), channel_id=1, source_target_pairs={{0,2},{2,4},{4,6},{6,7},{7,5},{5,3},{3,1},{1,0},{8,9},{10,8},{12,1... | collective-permute-start | bytes 786440 | tf_op jit(solution)/shard_map/ppermute | solution.py:252
  5.1 29.3 %copy-start.3 = (bf16[1,1,180,512]{3,2,1,0:T(8,128)(2,1)S(1)}, bf16[1,1,180,512]{3,2,1,0:T(8,128)(2,1)}, u32[]{:S(2)}) copy-start(bf16[1,1,180,512]{3,2,1,0:T(8,128)(2,1)} %param.11) | copy-start | bytes 552964
  6.9 10.9 %collective-permute-start.1 = (bf16[180,512]{1,0:T(8,128)(2,1)}, bf16[180,512]{1,0:T(8,128)(2,1)S(1)}, u32[]{:S(2)}, u32[]{:S(2)}) collective-permute-start(bf16[180,512]{1,0:T(8,128)(2,1)} %norm.1), channel_id=1, source_target_pairs={{0,1},{1,0},{2,3},{3,2},{4,5},{5,4},{6,7},{7,6},{8,9},{9,8},{10,11... | collective-permute-start | bytes 552968 | tf_op jit(solution)/shard_map/ppermute | solution.py:66
  6.9 16.3 %collective-permute-start.2 = (bf16[180,512]{1,0:T(8,128)(2,1)}, bf16[180,512]{1,0:T(8,128)(2,1)S(1)}, u32[]{:S(2)}, u32[]{:S(2)}) collective-permute-start(bf16[180,512]{1,0:T(8,128)(2,1)} %norm.1), channel_id=1, source_target_pairs={{1,2},{2,1},{3,4},{4,3},{5,6},{6,5},{9,10},{10,9},{11,12},{12,11},... | collective-permute-start | bytes 552968 | tf_op jit(solution)/shard_map/ppermute | solution.py:66
  7.6 10.3 %collective-permute-start.3 = (bf16[180,512]{1,0:T(8,128)(2,1)}, bf16[180,512]{1,0:T(8,128)(2,1)S(1)}, u32[]{:S(2)}, u32[]{:S(2)}) collective-permute-start(bf16[180,512]{1,0:T(8,128)(2,1)} %norm.1), channel_id=1, source_target_pairs={{0,16},{8,24},{16,0},{24,8},{1,17},{9,25},{17,1},{25,9},{2,18},{10... | collective-permute-start | bytes 552968 | tf_op jit(solution)/shard_map/ppermute | solution.py:58
  9.6 8.8 %collective-permute-start.9 = (bf16[256,512]{1,0:T(8,128)(2,1)S(1)}, bf16[256,512]{1,0:T(8,128)(2,1)S(1)}, u32[]{:S(2)}, u32[]{:S(2)}) collective-permute-start(bf16[256,512]{1,0:T(8,128)(2,1)S(1)} %get-tuple-element.9.rest_9_), channel_id=1, source_target_pairs={{0,2},{2,4},{4,6},{6,7},{7,5},{5,3},{3,1},{1,0},{8,9},{10,8},{12,1... | collective-permute-start | bytes 786440 | tf_op jit(solution)/shard_map/ppermute | solution.py:254
  15.2 20.7 %copy-start = (f32[2,8]{1,0:T(2,128)S(1)}, f32[2,8]{1,0:T(2,128)}, u32[]{:S(2)}) copy-start(f32[2,8]{1,0:T(2,128)} %scales.1) | copy-start | bytes 196
  15.2 20.7 %copy-start.1 = (s32[8]{0:T(128)S(1)}, s32[8]{0:T(128)}, u32[]{:S(2)}) copy-start(s32[8]{0:T(128)} %tally.1) | copy-start | bytes 100
  15.2 6.4 %collective-permute-start.6 = (bf16[256,512]{1,0:T(8,128)(2,1)S(1)}, bf16[256,512]{1,0:T(8,128)(2,1)S(1)}, u32[]{:S(2)}, u32[]{:S(2)}) collective-permute-start(bf16[256,512]{1,0:T(8,128)(2,1)S(1)} %collective-permute-done.rest_2_), channel_id=1, source_target_pairs={{0,2},{2,4},{4,6},{6,7},{7,5},{5,3},{3,1},{1,0},{8,9},{10,8},{12,1... | collective-permute-start | bytes 786440 | tf_op jit(solution)/shard_map/ppermute | solution.py:252
  17.8 6.5 %collective-permute-start.4 = (bf16[180,512]{1,0:T(8,128)(2,1)}, bf16[180,512]{1,0:T(8,128)(2,1)S(1)}, u32[]{:S(2)}, u32[]{:S(2)}) collective-permute-start(bf16[180,512]{1,0:T(8,128)(2,1)} %norm.1), channel_id=1, source_target_pairs={{0,8},{1,9},{2,10},{3,11},{4,12},{5,13},{6,14},{7,15},{8,0},{9,1},... | collective-permute-start | bytes 552968 | tf_op jit(solution)/shard_map/ppermute | solution.py:260
  17.9 11.7 %collective-permute-start.5 = (bf16[180,512]{1,0:T(8,128)(2,1)S(1)}, bf16[180,512]{1,0:T(8,128)(2,1)S(1)}, u32[]{:S(2)}, u32[]{:S(2)}) collective-permute-start(bf16[180,512]{1,0:T(8,128)(2,1)S(1)} %collective-permute-done.3), channel_id=1, source_target_pairs={{0,8},{1,9},{2,10},{3,11},{4,12},{5,13},{6,14},{7,15},{8,0},{9,1},... | collective-permute-start | bytes 552968 | tf_op jit(solution)/shard_map/ppermute | solution.py:261
  18.4 6.4 %collective-permute-start.11 = (bf16[256,512]{1,0:T(8,128)(2,1)S(1)}, bf16[256,512]{1,0:T(8,128)(2,1)S(1)}, u32[]{:S(2)}, u32[]{:S(2)}) collective-permute-start(bf16[256,512]{1,0:T(8,128)(2,1)S(1)} %collective-permute-done.9.rest_10_), channel_id=1, source_target_pairs={{0,2},{2,4},{4,6},{6,7},{7,5},{5,3},{3,1},{1,0},{8,9},{10,8},{12,1... | collective-permute-start | bytes 786440 | tf_op jit(solution)/shard_map/ppermute | solution.py:254
  21.6 6.4 %collective-permute-start.7 = (bf16[256,512]{1,0:T(8,128)(2,1)S(1)}, bf16[256,512]{1,0:T(8,128)(2,1)S(1)}, u32[]{:S(2)}, u32[]{:S(2)}) collective-permute-start(bf16[256,512]{1,0:T(8,128)(2,1)S(1)} %collective-permute-done.6.rest_3_), channel_id=1, source_target_pairs={{0,2},{2,4},{4,6},{6,7},{7,5},{5,3},{3,1},{1,0},{8,9},{10,8},{12,1... | collective-permute-start | bytes 786440 | tf_op jit(solution)/shard_map/ppermute | solution.py:252
  23.3 6.5 %collective-permute-start.10 = (bf16[256,512]{1,0:T(8,128)(2,1)S(1)}, bf16[256,512]{1,0:T(8,128)(2,1)S(1)}, u32[]{:S(2)}, u32[]{:S(2)}) collective-permute-start(bf16[256,512]{1,0:T(8,128)(2,1)S(1)} %collective-permute-done.9.rest_10_), channel_id=1, source_target_pairs={{0,8},{1,9},{2,10},{3,11},{4,12},{5,13},{6,14},{7,15},{8,0},{9,1},... | collective-permute-start | bytes 786440 | tf_op jit(solution)/shard_map/ppermute | solution.py:256
  24.3 5.9 %collective-permute-start.16 = (bf16[256,512]{1,0:T(8,128)(2,1)S(1)}, bf16[256,512]{1,0:T(8,128)(2,1)S(1)}, u32[]{:S(2)}, u32[]{:S(2)}) collective-permute-start(bf16[256,512]{1,0:T(8,128)(2,1)S(1)} %collective-permute-done.rest_2_), channel_id=1, source_target_pairs={{0,8},{1,9},{2,10},{3,11},{4,12},{5,13},{6,14},{7,15},{8,0},{9,1},... | collective-permute-start | bytes 786440 | tf_op jit(solution)/shard_map/ppermute | solution.py:255
  24.8 6.4 %collective-permute-start.13 = (bf16[256,512]{1,0:T(8,128)(2,1)S(1)}, bf16[256,512]{1,0:T(8,128)(2,1)S(1)}, u32[]{:S(2)}, u32[]{:S(2)}) collective-permute-start(bf16[256,512]{1,0:T(8,128)(2,1)S(1)} %collective-permute-done.11.rest_11_), channel_id=1, source_target_pairs={{0,2},{2,4},{4,6},{6,7},{7,5},{5,3},{3,1},{1,0},{8,9},{10,8},{12,1... | collective-permute-start | bytes 786440 | tf_op jit(solution)/shard_map/ppermute | solution.py:254
  28.0 6.4 %collective-permute-start.8 = (bf16[256,512]{1,0:T(8,128)(2,1)S(1)}, bf16[256,512]{1,0:T(8,128)(2,1)S(1)}, u32[]{:S(2)}, u32[]{:S(2)}) collective-permute-start(bf16[256,512]{1,0:T(8,128)(2,1)S(1)} %collective-permute-done.7.rest_4_), channel_id=1, source_target_pairs={{0,2},{2,4},{4,6},{6,7},{7,5},{5,3},{3,1},{1,0},{8,9},{10,8},{12,1... | collective-permute-start | bytes 786440 | tf_op jit(solution)/shard_map/ppermute | solution.py:252
  29.6 4.8 %collective-permute-start.12 = (bf16[256,512]{1,0:T(8,128)(2,1)S(1)}, bf16[256,512]{1,0:T(8,128)(2,1)S(1)}, u32[]{:S(2)}, u32[]{:S(2)}) collective-permute-start(bf16[256,512]{1,0:T(8,128)(2,1)S(1)} %collective-permute-done.11.rest_11_), channel_id=1, source_target_pairs={{0,8},{1,9},{2,10},{3,11},{4,12},{5,13},{6,14},{7,15},{8,0},{9,1},... | collective-permute-start | bytes 786440 | tf_op jit(solution)/shard_map/ppermute | solution.py:256
  29.7 4.7 %collective-permute-start.17 = (bf16[256,512]{1,0:T(8,128)(2,1)S(1)}, bf16[256,512]{1,0:T(8,128)(2,1)S(1)}, u32[]{:S(2)}, u32[]{:S(2)}) collective-permute-start(bf16[256,512]{1,0:T(8,128)(2,1)S(1)} %collective-permute-done.6.rest_3_), channel_id=1, source_target_pairs={{0,8},{1,9},{2,10},{3,11},{4,12},{5,13},{6,14},{7,15},{8,0},{9,1},... | collective-permute-start | bytes 786440 | tf_op jit(solution)/shard_map/ppermute | solution.py:255
  30.2 4.3 %collective-permute-start.18 = (bf16[256,512]{1,0:T(8,128)(2,1)S(1)}, bf16[256,512]{1,0:T(8,128)(2,1)S(1)}, u32[]{:S(2)}, u32[]{:S(2)}) collective-permute-start(bf16[256,512]{1,0:T(8,128)(2,1)S(1)} %collective-permute-done.7.rest_4_), channel_id=1, source_target_pairs={{0,8},{1,9},{2,10},{3,11},{4,12},{5,13},{6,14},{7,15},{8,0},{9,1},... | collective-permute-start | bytes 786440 | tf_op jit(solution)/shard_map/ppermute | solution.py:255
  31.2 3.3 %collective-permute-start.14 = (bf16[256,512]{1,0:T(8,128)(2,1)S(1)}, bf16[256,512]{1,0:T(8,128)(2,1)S(1)}, u32[]{:S(2)}, u32[]{:S(2)}) collective-permute-start(bf16[256,512]{1,0:T(8,128)(2,1)S(1)} %collective-permute-done.13.rest_12_), channel_id=1, source_target_pairs={{0,8},{1,9},{2,10},{3,11},{4,12},{5,13},{6,14},{7,15},{8,0},{9,1},... | collective-permute-start | bytes 786440 | tf_op jit(solution)/shard_map/ppermute | solution.py:256
  34.4 1.5 %collective-permute-start.15 = (bf16[256,512]{1,0:T(8,128)(2,1)S(1)}, bf16[256,512]{1,0:T(8,128)(2,1)S(1)}, u32[]{:S(2)}, u32[]{:S(2)}) collective-permute-start(bf16[256,512]{1,0:T(8,128)(2,1)S(1)} %collective-permute-done.8.rest_5_), channel_id=1, source_target_pairs={{0,8},{1,9},{2,10},{3,11},{4,12},{5,13},{6,14},{7,15},{8,0},{9,1},... | collective-permute-start | bytes 786440 | tf_op jit(solution)/shard_map/ppermute | solution.py:257

commit v3 on v2

--- a/solution.py
+++ b/solution.py
@@ -72,10 +72,11 @@
     return (shaped * lax.rsqrt(mean + epsilon)).reshape(block.shape)
 
 
-def norm_kernel(gain_ref, state_ref, normed_ref):
-    x = state_ref[...].astype(F32)
-    scale = lax.rsqrt(jnp.mean(x * x, axis=-1, keepdims=True) + epsilon)
-    normed_ref[...] = (x * scale * gain_ref[...]).astype(BF)
+def norm_kernel(gain_ref, rows_ref, normed_ref):
+    for j in range(rows_ref.shape[0]):
+        x = rows_ref[j].astype(F32)
+        scale = lax.rsqrt(jnp.mean(x * x, axis=-1, keepdims=True) + epsilon)
+        normed_ref[j] = (x * scale * gain_ref[...]).astype(BF)
 
 
 def kernel(
@@ -83,7 +84,7 @@
     meta, scales, tally, *rest,
 ):
     slots, states = n_bands, 2 + n_time
-    normed, rest = rest[0], rest[1:]
+    normed, late, rest = rest[0], rest[1], rest[2:]
     mine, rest = rest[:slots], rest[slots:]
     other, rest = rest[:slots], rest[slots:]
     out_ref, weights, final, qs, ks, vs, mix = rest
@@ -135,6 +136,18 @@
             seen = seen | (kcol == qcol)
         biases.append(jnp.where(seen, 0.0, FAR).astype(F32))
     tn = (((0,), (0,)), ((), ()))
+    def time_part(i):
+        j, part = i // 2, 1 + i % 2
+        if j == n_time:
+            qs[1] = unit_rows(proj(1, 0, normed[0])).astype(BF)
+            return
+        out = proj(1, part, normed[j + 2 if j else 0])
+        if part == 1:
+            ks[3 + j] = unit_rows(out).astype(BF)
+        else:
+            vs[3 + j] = out.astype(BF)
+
+    todo = 2 * n_time + 1
     for h in range(HEADS):
         lo = h * HEAD_DIM
         hi = lo + HEAD_DIM
@@ -144,20 +157,17 @@
             lax.dot_general(ks[j, lo:hi, :], q, tn, preferred_element_type=F32) * factor + biases[j]
             for j in range(3)
         ]
+        for i in range(h * todo // HEADS, (h + 1) * todo // HEADS):
+            time_part(i)
         top = jnp.max(jnp.maximum(jnp.maximum(x[0], x[1]), x[2]), axis=0, keepdims=True)
         e = [jnp.exp2(s - top) for s in x]
         inv = 1.0 / jnp.sum(e[0] + e[1] + e[2], axis=0, keepdims=True)
         o = sum(
-            jnp.dot(vs[j, lo:hi, :], (e[j] * inv).astype(BF), preferred_element_type=F32)
+            jnp.dot(vs[j, lo:hi, :], e[j].astype(BF), preferred_element_type=F32)
             for j in range(3)
         )
-        mix[0, lo:hi, :] = o.astype(BF)
-
-    qs[1] = unit_rows(proj(1, 0, own)).astype(BF)
-    for j in range(n_time):
-        x = normed[j + 2 if j else 0]
-        ks[3 + j] = unit_rows(proj(1, 1, x)).astype(BF)
-        vs[3 + j] = proj(1, 2, x).astype(BF)
+        mix[0, lo:hi, :] = (o * inv).astype(BF)
+
     odd = frame % 2
     back = [0, 2, jnp.where(odd == 1, 1, -1), jnp.where(odd == 1, 3, 1), jnp.where(odd == 1, -1, 3)]
     allow = [(b >= 0) & (b <= PRIOR_SNAPSHOTS) & (frame - b >= 0) for b in back]
@@ -190,8 +200,8 @@
         return sigma_low * jnp.exp(power * math.log(sigma_high / sigma_low))
 
     s, s_next = sigma_of(level), sigma_of(level - 1)
-    state = normed[states].astype(F32)
-    fresh = normed[states + 1].astype(F32)
+    state = late[0].astype(F32)
+    fresh = late[1].astype(F32)
     denoised = state / (1.0 + s * s) + s * lax.rsqrt(1.0 + s * s) * update
     stepped = denoised + s_next * (keep_share * (state - denoised) / s + fresh_share * fresh)
     out_ref[...] = jnp.where(level == 0, sigma_high * fresh, stepped).astype(BF)
@@ -221,16 +231,6 @@
     smem = pl.BlockSpec(memory_space=pltpu.SMEM)
     vmem = pl.BlockSpec(memory_space=pltpu.VMEM)
     hbm = pl.BlockSpec(memory_space=pltpu.HBM)
-    gain = normalizer_scaling.reshape(1, width)
-    normed = pl.pallas_call(
-        norm_kernel,
-        out_shape=jax.ShapeDtypeStruct((lon, width), BF),
-        in_specs=[vmem, vmem],
-        out_specs=vmem,
-        compiler_params=pltpu.CompilerParams(vmem_limit_bytes=LARGE),
-        name="norm",
-    )(gain, state)
-
     chunk_a = jnp.concatenate([local_projection_matrices, final_projection_matrices[:width]], axis=1).T
     chunk_b = jnp.concatenate([time_projection_matrices, final_projection_matrices[width:]], axis=1).T
     own0 = jnp.where(parity == 0, chunk_a, chunk_b)
@@ -242,9 +242,9 @@
     ring, core = ring_pairs(nf, n), core_pairs(nf, n)
     half = n // 2
     chain0, chain1 = [own0], [own1]
-    partners = exchange_bands(normed, 0)
-    others = exchange_bands(normed, 1)
-    two_back = rotate_frame(normed, 2)
+    partners = exchange_bands(state, 0)
+    others = exchange_bands(state, 1)
+    two_back = rotate_frame(state, 2)
     for h in range(half):
         a, b = chain0[-1], chain1[-1]
         if h == 1:
@@ -257,18 +257,27 @@
     swap_last = lax.ppermute(chain0[half], AXES, core)
     mine = chain0 + swap1
     other = chain1 + [swap_last] + swap0
-    partner = lax.ppermute(normed, AXES, core)
+    partner = lax.ppermute(state, AXES, core)
     partner_two = lax.ppermute(two_back, AXES, core)
     past = [two_back, partner, partner_two]
     if nf > 4:
-        past.append(rotate_frame(normed, 3))
+        past.append(rotate_frame(state, 3))
 
     n_time = 1 + len(past)
-    rows_in = jnp.stack([normed, partners, others, *past, state, noise])
+    gathered = jnp.stack([state, partners, others, *past])
+    normed = pl.pallas_call(
+        norm_kernel,
+        out_shape=jax.ShapeDtypeStruct(gathered.shape, BF),
+        in_specs=[vmem, vmem],
+        out_specs=vmem,
+        compiler_params=pltpu.CompilerParams(vmem_limit_bytes=8 * 1024 * 1024),
+        name="norm",
+    )(normalizer_scaling.reshape(1, width), gathered)
+    late = jnp.stack([state, noise])
     out = pl.pallas_call(
         functools.partial(kernel, n_time, n, nf),
         out_shape=jax.ShapeDtypeStruct((lon, width), BF),
-        in_specs=[smem] * 3 + [vmem] * (1 + 2 * n),
+        in_specs=[smem] * 3 + [vmem] * (2 + 2 * n),
         out_specs=vmem,
         scratch_shapes=[
             pltpu.VMEM((2, 3 * width, width), BF),
@@ -282,7 +291,7 @@
         name="block",
     )(
         meta, head_score_scales, latitude_patch_tally,
-        rows_in, *mine, *other,
+        normed, late, *mine, *other,
     )
     return out.reshape(noisy_snapshot_stack.shape)
 

time: 44.2 us -> 41.8 us (0.946)
  starting transfers between devices: 20.7 us -> 25 us
  waiting for transfers between devices: 8.87 us -> 4.81 us
  Pallas kernels: 9.83 us -> 7.99 us
  local copies, waits for them, and re-layouts: 1.93 us -> 1.04 us
    ppermute x4, waiting for transfers between devices: 6.07 us -> 2.44 us  [body(): chain0.append(lax.ppermute(a, AXES, ring))]
    pallas_call x1, Pallas kernels: 1.78 us -> 0.45 us  [body(): pl.pallas_call(norm_kernel, out_shape=jax.ShapeDtypeStruct(gathered.shape...]
    ppermute x1, starting transfers between devices: 0.49 us -> 1.81 us  [body(): partner_two = lax.ppermute(two_back, AXES, core)]
    ppermute x1, starting transfers between devices: 0.07 us -> 1.34 us  [body(): partner = lax.ppermute(state, AXES, core)]
    ppermute x1, waiting for transfers between devices: 0.01 us -> 1.04 us  [body(): partner_two = lax.ppermute(two_back, AXES, core)]
    ppermute x4, starting transfers between devices: 7.86 us -> 8.81 us  [body(): chain0.append(lax.ppermute(a, AXES, ring))]
    unnamed x15, local copies, waits for them, and re-layouts: 1.04 us -> 0.09 us
    ppermute x1, starting transfers between devices: 0.01 us -> 0.86 us  [body(): swap_last = lax.ppermute(chain0[half], AXES, core)]
  transfers between devices with their start and end apart: 19 -> 19, of which waited for: 6 -> 6; matrix products, arithmetic and copies ran while one was open for 3% -> 0% of each run, Pallas kernels for 4% -> 1%
where the time goes in v3:
time: 41.8 us; the launch traced here: 41.6 us
  starting transfers between devices  25 us (60%)
  Pallas kernels  7.99 us (19%)
  waiting for transfers between devices  4.81 us (12%)
  between operations  1.48 us (4%)
  other arithmetic  1.23 us (3%)
  local copies, waits for them, and re-layouts  1.04 us (2%)
    ppermute x4, starting transfers between devices, body(): chain0.append(lax.ppermute(a, AXES, ring))  8.81 us
    ppermute x3, starting transfers between devices, body(): chain1.append(lax.ppermute(b, AXES, ring))  7.98 us
    pallas_call x1, Pallas kernels, body(): pl.pallas_call(functools.partial(kernel, n_time, n, nf), out_shape=jax.Sh...  7.54 us
    ppermute x4, waiting for transfers between devices, body(): chain0.append(lax.ppermute(a, AXES, ring))  2.44 us
    ppermute x1, starting transfers between devices, rotate_frame(): lax.ppermute(block, 'frame', [(i, (i + hop) % nf) for i in range(nf)])  2 us
    ppermute x1, starting transfers between devices, body(): partner_two = lax.ppermute(two_back, AXES, core)  1.81 us
    ppermute x1, starting transfers between devices, body(): partner = lax.ppermute(state, AXES, core)  1.34 us
    select_n x1, other arithmetic, body(): own1 = jnp.where(parity == 0, chunk_b, chunk_a)  1.12 us
  transfers between devices with their start and end apart: 19, of which 6 were waited for; matrix products, arithmetic and copies ran while one was open for 0% of the time, Pallas kernels for 1%

profile of v3, /device:TPU:0, one launch (start us, length us, event | category | flops | bytes accessed | tf_op | source)
XLA Modules:
  0.0 41.6 jit_solution(6438810857555138786)
XLA Ops:
  0.0 0.9 %fusion = (bf16[512,64]{0,1:T(8,128)(2,1)S(1)}, bf16[512,64]{0,1:T(8,128)(2,1)S(1)}) fusion(bf16[1024,64]{0,1:T(8,128)(2,1)} %param.19), kind=kLoop, calls=%fused_computation.12 | loop fusion | bytes 262144 | tf_op jit(solution)/shard_map/slice | solution.py:234
  0.9 1.1 %select_bitcast_fusion = (bf16[256,512]{1,0:T(8,128)(2,1)S(1)}, bf16[256,512]{1,0:T(8,128)(2,1)S(1)}) fusion(pred[]{:T(512)S(6)} %eq.6, bf16[512,64]{0,1:T(8,128)(2,1)S(1)} %get-tuple-element.12, bf16[512,192]{0,1:T(8,128)(2,1)} %param.18, bf16[512,64]{0,1:T(8,128)(2,1)S(1)} %get-tuple-element.11, bf16[512,192]{0,1:T(8,128)(2,1)} %param.17), kind=kLoop, calls=%fused_computation.3 | loop fusion | flops 1310720 | bytes 1048577 | tf_op jit(solution)/shard_map/jit(_where)/select_n | solution.py:237
  2.1 3.1 %collective-permute-start = (bf16[256,512]{1,0:T(8,128)(2,1)S(1)}, bf16[256,512]{1,0:T(8,128)(2,1)S(1)}, u32[]{:S(2)}, u32[]{:S(2)}) collective-permute-start(bf16[256,512]{1,0:T(8,128)(2,1)S(1)} %get-tuple-element.10.rest_2_), channel_id=1, source_target_pairs={{0,2},{2,4},{4,6},{6,7},{7,5},{5,3},{3,1},{1,0},{8,9},{10,8},{12,1... | collective-permute-start | bytes 786440 | tf_op jit(solution)/shard_map/ppermute | solution.py:252
  5.1 1.6 %collective-permute-start.9 = (bf16[256,512]{1,0:T(8,128)(2,1)S(1)}, bf16[256,512]{1,0:T(8,128)(2,1)S(1)}, u32[]{:S(2)}, u32[]{:S(2)}) collective-permute-start(bf16[256,512]{1,0:T(8,128)(2,1)S(1)} %get-tuple-element.9.rest_10_), channel_id=1, source_target_pairs={{0,2},{2,4},{4,6},{6,7},{7,5},{5,3},{3,1},{1,0},{8,9},{10,8},{12,1... | collective-permute-start | bytes 786440 | tf_op jit(solution)/shard_map/ppermute | solution.py:254
  8.1 1.3 %collective-permute-done.rest_3_ = bf16[256,512]{1,0:T(8,128)(2,1)S(1)} collective-permute-done((bf16[256,512]{1,0:T(8,128)(2,1)S(1)}, bf16[256,512]{1,0:T(8,128)(2,1)S(1)}, u32[]{:S(2)}, u32[]{:S(2)}) %collective-permute-start) | collective-permute-done | bytes 262176 | tf_op jit(solution)/shard_map/ppermute | solution.py:252
  9.4 2.1 %collective-permute-start.6 = (bf16[256,512]{1,0:T(8,128)(2,1)S(1)}, bf16[256,512]{1,0:T(8,128)(2,1)S(1)}, u32[]{:S(2)}, u32[]{:S(2)}) collective-permute-start(bf16[256,512]{1,0:T(8,128)(2,1)S(1)} %collective-permute-done.rest_3_), channel_id=1, source_target_pairs={{0,2},{2,4},{4,6},{6,7},{7,5},{5,3},{3,1},{1,0},{8,9},{10,8},{12,1... | collective-permute-start | bytes 786440 | tf_op jit(solution)/shard_map/ppermute | solution.py:252
  11.5 0.7 %collective-permute-start.2 = (bf16[180,512]{1,0:T(8,128)(2,1)S(1)}, bf16[180,512]{1,0:T(8,128)(2,1)S(1)}, u32[]{:S(2)}, u32[]{:S(2)}) collective-permute-start(bf16[180,512]{1,0:T(8,128)(2,1)S(1)} %bitcast.24), channel_id=1, source_target_pairs={{1,2},{2,1},{3,4},{4,3},{5,6},{6,5},{9,10},{10,9},{11,12},{12,11},... | collective-permute-start | bytes 552968 | tf_op jit(solution)/shard_map/ppermute | solution.py:66
  12.2 2.0 %collective-permute-start.3 = (bf16[180,512]{1,0:T(8,128)(2,1)S(1)}, bf16[180,512]{1,0:T(8,128)(2,1)S(1)}, u32[]{:S(2)}, u32[]{:S(2)}) collective-permute-start(bf16[180,512]{1,0:T(8,128)(2,1)S(1)} %bitcast.25), channel_id=1, source_target_pairs={{0,16},{8,24},{16,0},{24,8},{1,17},{9,25},{17,1},{25,9},{2,18},{10... | collective-permute-start | bytes 552968 | tf_op jit(solution)/shard_map/ppermute | solution.py:58
  14.2 4.3 %collective-permute-start.11 = (bf16[256,512]{1,0:T(8,128)(2,1)S(1)}, bf16[256,512]{1,0:T(8,128)(2,1)S(1)}, u32[]{:S(2)}, u32[]{:S(2)}) collective-permute-start(bf16[256,512]{1,0:T(8,128)(2,1)S(1)} %collective-permute-done.9.rest_11_), channel_id=1, source_target_pairs={{0,2},{2,4},{4,6},{6,7},{7,5},{5,3},{3,1},{1,0},{8,9},{10,8},{12,1... | collective-permute-start | bytes 786440 | tf_op jit(solution)/shard_map/ppermute | solution.py:254
  18.5 1.6 %collective-permute-start.7 = (bf16[256,512]{1,0:T(8,128)(2,1)S(1)}, bf16[256,512]{1,0:T(8,128)(2,1)S(1)}, u32[]{:S(2)}, u32[]{:S(2)}) collective-permute-start(bf16[256,512]{1,0:T(8,128)(2,1)S(1)} %collective-permute-done.6.rest_4_), channel_id=1, source_target_pairs={{0,2},{2,4},{4,6},{6,7},{7,5},{5,3},{3,1},{1,0},{8,9},{10,8},{12,1... | collective-permute-start | bytes 786440 | tf_op jit(solution)/shard_map/ppermute | solution.py:252
  20.2 1.3 %collective-permute-start.4 = (bf16[180,512]{1,0:T(8,128)(2,1)S(1)}, bf16[180,512]{1,0:T(8,128)(2,1)S(1)}, u32[]{:S(2)}, u32[]{:S(2)}) collective-permute-start(bf16[180,512]{1,0:T(8,128)(2,1)S(1)} %bitcast.27), channel_id=1, source_target_pairs={{0,8},{1,9},{2,10},{3,11},{4,12},{5,13},{6,14},{7,15},{8,0},{9,1},... | collective-permute-start | bytes 552968 | tf_op jit(solution)/shard_map/ppermute | solution.py:260
  21.6 0.5 %collective-permute-start.16 = (bf16[256,512]{1,0:T(8,128)(2,1)S(1)}, bf16[256,512]{1,0:T(8,128)(2,1)S(1)}, u32[]{:S(2)}, u32[]{:S(2)}) collective-permute-start(bf16[256,512]{1,0:T(8,128)(2,1)S(1)} %collective-permute-done.rest_3_), channel_id=1, source_target_pairs={{0,8},{1,9},{2,10},{3,11},{4,12},{5,13},{6,14},{7,15},{8,0},{9,1},... | collective-permute-start | bytes 786440 | tf_op jit(solution)/shard_map/ppermute | solution.py:255
  22.1 0.7 %collective-permute-done.11.rest_12_ = bf16[256,512]{1,0:T(8,128)(2,1)S(1)} collective-permute-done((bf16[256,512]{1,0:T(8,128)(2,1)S(1)}, bf16[256,512]{1,0:T(8,128)(2,1)S(1)}, u32[]{:S(2)}, u32[]{:S(2)}) %collective-permute-start.11) | collective-permute-done | bytes 262176 | tf_op jit(solution)/shard_map/ppermute | solution.py:254
  22.8 2.1 %collective-permute-start.13 = (bf16[256,512]{1,0:T(8,128)(2,1)S(1)}, bf16[256,512]{1,0:T(8,128)(2,1)S(1)}, u32[]{:S(2)}, u32[]{:S(2)}) collective-permute-start(bf16[256,512]{1,0:T(8,128)(2,1)S(1)} %collective-permute-done.11.rest_12_), channel_id=1, source_target_pairs={{0,2},{2,4},{4,6},{6,7},{7,5},{5,3},{3,1},{1,0},{8,9},{10,8},{12,1... | collective-permute-start | bytes 786440 | tf_op jit(solution)/shard_map/ppermute | solution.py:254
  24.9 0.7 %collective-permute-done.7.rest_5_ = bf16[256,512]{1,0:T(8,128)(2,1)S(1)} collective-permute-done((bf16[256,512]{1,0:T(8,128)(2,1)S(1)}, bf16[256,512]{1,0:T(8,128)(2,1)S(1)}, u32[]{:S(2)}, u32[]{:S(2)}) %collective-permute-start.7) | collective-permute-done | bytes 262176 | tf_op jit(solution)/shard_map/ppermute | solution.py:252
  25.6 2.1 %collective-permute-start.8 = (bf16[256,512]{1,0:T(8,128)(2,1)S(1)}, bf16[256,512]{1,0:T(8,128)(2,1)S(1)}, u32[]{:S(2)}, u32[]{:S(2)}) collective-permute-start(bf16[256,512]{1,0:T(8,128)(2,1)S(1)} %collective-permute-done.7.rest_5_), channel_id=1, source_target_pairs={{0,2},{2,4},{4,6},{6,7},{7,5},{5,3},{3,1},{1,0},{8,9},{10,8},{12,1... | collective-permute-start | bytes 786440 | tf_op jit(solution)/shard_map/ppermute | solution.py:252
  27.7 1.8 %collective-permute-start.5 = (bf16[180,512]{1,0:T(8,128)(2,1)S(1)}, bf16[180,512]{1,0:T(8,128)(2,1)S(1)}, u32[]{:S(2)}, u32[]{:S(2)}) collective-permute-start(bf16[180,512]{1,0:T(8,128)(2,1)S(1)} %collective-permute-done.3), channel_id=1, source_target_pairs={{0,8},{1,9},{2,10},{3,11},{4,12},{5,13},{6,14},{7,15},{8,0},{9,1},... | collective-permute-start | bytes 552968 | tf_op jit(solution)/shard_map/ppermute | solution.py:261
  29.6 1.0 %collective-permute-done.5 = bf16[180,512]{1,0:T(8,128)(2,1)S(1)} collective-permute-done((bf16[180,512]{1,0:T(8,128)(2,1)S(1)}, bf16[180,512]{1,0:T(8,128)(2,1)S(1)}, u32[]{:S(2)}, u32[]{:S(2)}) %collective-permute-start.5) | collective-permute-done | bytes 184352 | tf_op jit(solution)/shard_map/ppermute | solution.py:261
  30.6 0.4 collective-permute-start.12
  31.1 0.4 collective-permute-start.18
  32.0 0.9 %collective-permute-start.15 = (bf16[256,512]{1,0:T(8,128)(2,1)S(1)}, bf16[256,512]{1,0:T(8,128)(2,1)S(1)}, u32[]{:S(2)}, u32[]{:S(2)}) collective-permute-start(bf16[256,512]{1,0:T(8,128)(2,1)S(1)} %collective-permute-done.8.rest_6_), channel_id=1, source_target_pairs={{0,8},{1,9},{2,10},{3,11},{4,12},{5,13},{6,14},{7,15},{8,0},{9,1},... | collective-permute-start | bytes 786440 | tf_op jit(solution)/shard_map/ppermute | solution.py:257
  33.0 0.5 %norm.1.rest_0_ = bf16[6,180,512]{2,1,0:T(8,128)(2,1)S(1)} custom-call(f32[1,512]{1,0:T(1,128)S(1)} %bitcast.22, bf16[6,180,512]{2,1,0:T(8,128)(2,1)S(1)} %bitcast_dynamic-update-slice_fusion.rows_ref), custom_call_target="tpu_custom_call" | custom-call | tf_op jit(solution)/shard_map/norm/pallas_call | solution.py:268
  33.5 0.6 %collective-permute-done.15.rest_14_ = bf16[256,512]{1,0:T(8,128)(2,1)S(1)} collective-permute-done((bf16[256,512]{1,0:T(8,128)(2,1)S(1)}, bf16[256,512]{1,0:T(8,128)(2,1)S(1)}, u32[]{:S(2)}, u32[]{:S(2)}) %collective-permute-start.15) | collective-permute-done | bytes 262176 | tf_op jit(solution)/shard_map/ppermute | solution.py:257
  34.0 7.5 %block.1 = bf16[180,512]{1,0:T(8,128)(2,1)} custom-call(s32[4]{0:T(128)S(1)} %pad_add_fusion.meta, f32[2,8]{1,0:T(2,128)S(1)} %copy-done.1, s32[8]{0:T(128)S(1)} %copy-done.2, bf16[6,180,512]{2,1,0:T(8,128)(2,1)S(1)} %norm.1.rest_0_, bf16[2,180,512]{2,1,0:T(8,128)(2,1)S(1)} %pad_maximum_fusion.rest_1_, bf16[256,512]{1,0:T(8,128)(2,1)S(1)} %get-tuple-element.10.rest_2_, ...), custom_call_target="tpu_custom_call" | custom-call | tf_op jit(solution)/shard_map/block/pallas_call | solution.py:277
  (36 shorter events, 1.0 us)
Async XLA Ops:
  0.0 11.5 %copy-start.3 = (bf16[1,1,180,512]{3,2,1,0:T(8,128)(2,1)S(1)}, bf16[1,1,180,512]{3,2,1,0:T(8,128)(2,1)}, u32[]{:S(2)}) copy-start(bf16[1,1,180,512]{3,2,1,0:T(8,128)(2,1)} %param.10) | copy-start | bytes 552964
  0.0 20.1 %copy-start.4 = (bf16[1,1,180,512]{3,2,1,0:T(8,128)(2,1)S(1)}, bf16[1,1,180,512]{3,2,1,0:T(8,128)(2,1)}, u32[]{:S(2)}) copy-start(bf16[1,1,180,512]{3,2,1,0:T(8,128)(2,1)} %param.11) | copy-start | bytes 552964
  2.1 7.4 %collective-permute-start = (bf16[256,512]{1,0:T(8,128)(2,1)S(1)}, bf16[256,512]{1,0:T(8,128)(2,1)S(1)}, u32[]{:S(2)}, u32[]{:S(2)}) collective-permute-start(bf16[256,512]{1,0:T(8,128)(2,1)S(1)} %get-tuple-element.10.rest_2_), channel_id=1, source_target_pairs={{0,2},{2,4},{4,6},{6,7},{7,5},{5,3},{3,1},{1,0},{8,9},{10,8},{12,1... | collective-permute-start | bytes 786440 | tf_op jit(solution)/shard_map/ppermute | solution.py:252
  5.1 9.1 %collective-permute-start.9 = (bf16[256,512]{1,0:T(8,128)(2,1)S(1)}, bf16[256,512]{1,0:T(8,128)(2,1)S(1)}, u32[]{:S(2)}, u32[]{:S(2)}) collective-permute-start(bf16[256,512]{1,0:T(8,128)(2,1)S(1)} %get-tuple-element.9.rest_10_), channel_id=1, source_target_pairs={{0,2},{2,4},{4,6},{6,7},{7,5},{5,3},{3,1},{1,0},{8,9},{10,8},{12,1... | collective-permute-start | bytes 786440 | tf_op jit(solution)/shard_map/ppermute | solution.py:254
  9.4 9.1 %collective-permute-start.6 = (bf16[256,512]{1,0:T(8,128)(2,1)S(1)}, bf16[256,512]{1,0:T(8,128)(2,1)S(1)}, u32[]{:S(2)}, u32[]{:S(2)}) collective-permute-start(bf16[256,512]{1,0:T(8,128)(2,1)S(1)} %collective-permute-done.rest_3_), channel_id=1, source_target_pairs={{0,2},{2,4},{4,6},{6,7},{7,5},{5,3},{3,1},{1,0},{8,9},{10,8},{12,1... | collective-permute-start | bytes 786440 | tf_op jit(solution)/shard_map/ppermute | solution.py:252
  11.5 8.7 %collective-permute-start.1 = (bf16[180,512]{1,0:T(8,128)(2,1)S(1)}, bf16[180,512]{1,0:T(8,128)(2,1)S(1)}, u32[]{:S(2)}, u32[]{:S(2)}) collective-permute-start(bf16[180,512]{1,0:T(8,128)(2,1)S(1)} %bitcast.23), channel_id=1, source_target_pairs={{0,1},{1,0},{2,3},{3,2},{4,5},{5,4},{6,7},{7,6},{8,9},{9,8},{10,11... | collective-permute-start | bytes 552968 | tf_op jit(solution)/shard_map/ppermute | solution.py:66
  11.5 10.0 %collective-permute-start.2 = (bf16[180,512]{1,0:T(8,128)(2,1)S(1)}, bf16[180,512]{1,0:T(8,128)(2,1)S(1)}, u32[]{:S(2)}, u32[]{:S(2)}) collective-permute-start(bf16[180,512]{1,0:T(8,128)(2,1)S(1)} %bitcast.24), channel_id=1, source_target_pairs={{1,2},{2,1},{3,4},{4,3},{5,6},{6,5},{9,10},{10,9},{11,12},{12,11},... | collective-permute-start | bytes 552968 | tf_op jit(solution)/shard_map/ppermute | solution.py:66
  12.2 9.4 %collective-permute-start.3 = (bf16[180,512]{1,0:T(8,128)(2,1)S(1)}, bf16[180,512]{1,0:T(8,128)(2,1)S(1)}, u32[]{:S(2)}, u32[]{:S(2)}) collective-permute-start(bf16[180,512]{1,0:T(8,128)(2,1)S(1)} %bitcast.25), channel_id=1, source_target_pairs={{0,16},{8,24},{16,0},{24,8},{1,17},{9,25},{17,1},{25,9},{2,18},{10... | collective-permute-start | bytes 552968 | tf_op jit(solution)/shard_map/ppermute | solution.py:58
  14.2 8.6 %collective-permute-start.11 = (bf16[256,512]{1,0:T(8,128)(2,1)S(1)}, bf16[256,512]{1,0:T(8,128)(2,1)S(1)}, u32[]{:S(2)}, u32[]{:S(2)}) collective-permute-start(bf16[256,512]{1,0:T(8,128)(2,1)S(1)} %collective-permute-done.9.rest_11_), channel_id=1, source_target_pairs={{0,2},{2,4},{4,6},{6,7},{7,5},{5,3},{3,1},{1,0},{8,9},{10,8},{12,1... | collective-permute-start | bytes 786440 | tf_op jit(solution)/shard_map/ppermute | solution.py:254
  18.5 7.1 %collective-permute-start.7 = (bf16[256,512]{1,0:T(8,128)(2,1)S(1)}, bf16[256,512]{1,0:T(8,128)(2,1)S(1)}, u32[]{:S(2)}, u32[]{:S(2)}) collective-permute-start(bf16[256,512]{1,0:T(8,128)(2,1)S(1)} %collective-permute-done.6.rest_4_), channel_id=1, source_target_pairs={{0,2},{2,4},{4,6},{6,7},{7,5},{5,3},{3,1},{1,0},{8,9},{10,8},{12,1... | collective-permute-start | bytes 786440 | tf_op jit(solution)/shard_map/ppermute | solution.py:252
  20.2 12.8 %copy-start = (f32[512]{0:T(512)S(1)}, f32[512]{0:T(512)}, u32[]{:S(2)}) copy-start(f32[512]{0:T(512)} %param.15) | copy-start | bytes 6148
  20.2 7.6 %collective-permute-start.4 = (bf16[180,512]{1,0:T(8,128)(2,1)S(1)}, bf16[180,512]{1,0:T(8,128)(2,1)S(1)}, u32[]{:S(2)}, u32[]{:S(2)}) collective-permute-start(bf16[180,512]{1,0:T(8,128)(2,1)S(1)} %bitcast.27), channel_id=1, source_target_pairs={{0,8},{1,9},{2,10},{3,11},{4,12},{5,13},{6,14},{7,15},{8,0},{9,1},... | collective-permute-start | bytes 552968 | tf_op jit(solution)/shard_map/ppermute | solution.py:260
  21.6 9.4 %collective-permute-start.10 = (bf16[256,512]{1,0:T(8,128)(2,1)S(1)}, bf16[256,512]{1,0:T(8,128)(2,1)S(1)}, u32[]{:S(2)}, u32[]{:S(2)}) collective-permute-start(bf16[256,512]{1,0:T(8,128)(2,1)S(1)} %collective-permute-done.9.rest_11_), channel_id=1, source_target_pairs={{0,8},{1,9},{2,10},{3,11},{4,12},{5,13},{6,14},{7,15},{8,0},{9,1},... | collective-permute-start | bytes 786440 | tf_op jit(solution)/shard_map/ppermute | solution.py:256
  21.6 9.5 %collective-permute-start.16 = (bf16[256,512]{1,0:T(8,128)(2,1)S(1)}, bf16[256,512]{1,0:T(8,128)(2,1)S(1)}, u32[]{:S(2)}, u32[]{:S(2)}) collective-permute-start(bf16[256,512]{1,0:T(8,128)(2,1)S(1)} %collective-permute-done.rest_3_), channel_id=1, source_target_pairs={{0,8},{1,9},{2,10},{3,11},{4,12},{5,13},{6,14},{7,15},{8,0},{9,1},... | collective-permute-start | bytes 786440 | tf_op jit(solution)/shard_map/ppermute | solution.py:255
  22.8 8.7 %collective-permute-start.13 = (bf16[256,512]{1,0:T(8,128)(2,1)S(1)}, bf16[256,512]{1,0:T(8,128)(2,1)S(1)}, u32[]{:S(2)}, u32[]{:S(2)}) collective-permute-start(bf16[256,512]{1,0:T(8,128)(2,1)S(1)} %collective-permute-done.11.rest_12_), channel_id=1, source_target_pairs={{0,2},{2,4},{4,6},{6,7},{7,5},{5,3},{3,1},{1,0},{8,9},{10,8},{12,1... | collective-permute-start | bytes 786440 | tf_op jit(solution)/shard_map/ppermute | solution.py:254
  25.6 6.4 %collective-permute-start.8 = (bf16[256,512]{1,0:T(8,128)(2,1)S(1)}, bf16[256,512]{1,0:T(8,128)(2,1)S(1)}, u32[]{:S(2)}, u32[]{:S(2)}) collective-permute-start(bf16[256,512]{1,0:T(8,128)(2,1)S(1)} %collective-permute-done.7.rest_5_), channel_id=1, source_target_pairs={{0,2},{2,4},{4,6},{6,7},{7,5},{5,3},{3,1},{1,0},{8,9},{10,8},{12,1... | collective-permute-start | bytes 786440 | tf_op jit(solution)/shard_map/ppermute | solution.py:252
  27.7 2.9 %collective-permute-start.5 = (bf16[180,512]{1,0:T(8,128)(2,1)S(1)}, bf16[180,512]{1,0:T(8,128)(2,1)S(1)}, u32[]{:S(2)}, u32[]{:S(2)}) collective-permute-start(bf16[180,512]{1,0:T(8,128)(2,1)S(1)} %collective-permute-done.3), channel_id=1, source_target_pairs={{0,8},{1,9},{2,10},{3,11},{4,12},{5,13},{6,14},{7,15},{8,0},{9,1},... | collective-permute-start | bytes 552968 | tf_op jit(solution)/shard_map/ppermute | solution.py:261
  30.6 2.8 %collective-permute-start.12 = (bf16[256,512]{1,0:T(8,128)(2,1)S(1)}, bf16[256,512]{1,0:T(8,128)(2,1)S(1)}, u32[]{:S(2)}, u32[]{:S(2)}) collective-permute-start(bf16[256,512]{1,0:T(8,128)(2,1)S(1)} %collective-permute-done.11.rest_12_), channel_id=1, source_target_pairs={{0,8},{1,9},{2,10},{3,11},{4,12},{5,13},{6,14},{7,15},{8,0},{9,1},... | collective-permute-start | bytes 786440 | tf_op jit(solution)/shard_map/ppermute | solution.py:256
  31.0 2.4 %collective-permute-start.17 = (bf16[256,512]{1,0:T(8,128)(2,1)S(1)}, bf16[256,512]{1,0:T(8,128)(2,1)S(1)}, u32[]{:S(2)}, u32[]{:S(2)}) collective-permute-start(bf16[256,512]{1,0:T(8,128)(2,1)S(1)} %collective-permute-done.6.rest_4_), channel_id=1, source_target_pairs={{0,8},{1,9},{2,10},{3,11},{4,12},{5,13},{6,14},{7,15},{8,0},{9,1},... | collective-permute-start | bytes 786440 | tf_op jit(solution)/shard_map/ppermute | solution.py:255
  31.1 2.3 %collective-permute-start.18 = (bf16[256,512]{1,0:T(8,128)(2,1)S(1)}, bf16[256,512]{1,0:T(8,128)(2,1)S(1)}, u32[]{:S(2)}, u32[]{:S(2)}) collective-permute-start(bf16[256,512]{1,0:T(8,128)(2,1)S(1)} %collective-permute-done.7.rest_5_), channel_id=1, source_target_pairs={{0,8},{1,9},{2,10},{3,11},{4,12},{5,13},{6,14},{7,15},{8,0},{9,1},... | collective-permute-start | bytes 786440 | tf_op jit(solution)/shard_map/ppermute | solution.py:255
  31.5 1.9 %collective-permute-start.14 = (bf16[256,512]{1,0:T(8,128)(2,1)S(1)}, bf16[256,512]{1,0:T(8,128)(2,1)S(1)}, u32[]{:S(2)}, u32[]{:S(2)}) collective-permute-start(bf16[256,512]{1,0:T(8,128)(2,1)S(1)} %collective-permute-done.13.rest_13_), channel_id=1, source_target_pairs={{0,8},{1,9},{2,10},{3,11},{4,12},{5,13},{6,14},{7,15},{8,0},{9,1},... | collective-permute-start | bytes 786440 | tf_op jit(solution)/shard_map/ppermute | solution.py:256
  32.0 2.0 %collective-permute-start.15 = (bf16[256,512]{1,0:T(8,128)(2,1)S(1)}, bf16[256,512]{1,0:T(8,128)(2,1)S(1)}, u32[]{:S(2)}, u32[]{:S(2)}) collective-permute-start(bf16[256,512]{1,0:T(8,128)(2,1)S(1)} %collective-permute-done.8.rest_6_), channel_id=1, source_target_pairs={{0,8},{1,9},{2,10},{3,11},{4,12},{5,13},{6,14},{7,15},{8,0},{9,1},... | collective-permute-start | bytes 786440 | tf_op jit(solution)/shard_map/ppermute | solution.py:257
  32.9 1.1 %copy-start.1 = (f32[2,8]{1,0:T(2,128)S(1)}, f32[2,8]{1,0:T(2,128)}, u32[]{:S(2)}) copy-start(f32[2,8]{1,0:T(2,128)} %scales.1) | copy-start | bytes 196
  32.9 1.1 %copy-start.2 = (s32[8]{0:T(128)S(1)}, s32[8]{0:T(128)}, u32[]{:S(2)}) copy-start(s32[8]{0:T(128)} %tally.1) | copy-start | bytes 100

commit v4 on v3

--- a/solution.py
+++ b/solution.py
@@ -148,16 +148,28 @@
             vs[3 + j] = out.astype(BF)
 
     todo = 2 * n_time + 1
-    for h in range(HEADS):
-        lo = h * HEAD_DIM
-        hi = lo + HEAD_DIM
-        factor = scales[0, h] * (LOG2E / math.sqrt(HEAD_DIM))
-        q = qs[0, lo:hi, :]
+    pairs = HEADS // 2
+    wide = [jnp.concatenate([b, b], axis=1) for b in biases]
+    first_half = lax.broadcasted_iota(jnp.int32, (1, 2 * lon), 1) < lon
+    blank = jnp.zeros((HEAD_DIM, lon), BF)
+    for h in range(pairs):
+        lo = 2 * h * HEAD_DIM
+        mid = lo + HEAD_DIM
+        hi = mid + HEAD_DIM
+        base = LOG2E / math.sqrt(HEAD_DIM)
+        factor = jnp.where(first_half, scales[0, 2 * h] * base, scales[0, 2 * h + 1] * base)
+        q = jnp.concatenate(
+            [
+                jnp.concatenate([qs[0, lo:mid, :], blank], axis=1),
+                jnp.concatenate([blank, qs[0, mid:hi, :]], axis=1),
+            ],
+            axis=0,
+        )
         x = [
-            lax.dot_general(ks[j, lo:hi, :], q, tn, preferred_element_type=F32) * factor + biases[j]
+            lax.dot_general(ks[j, lo:hi, :], q, tn, preferred_element_type=F32) * factor + wide[j]
             for j in range(3)
         ]
-        for i in range(h * todo // HEADS, (h + 1) * todo // HEADS):
+        for i in range(h * todo // pairs, (h + 1) * todo // pairs):
             time_part(i)
         top = jnp.max(jnp.maximum(jnp.maximum(x[0], x[1]), x[2]), axis=0, keepdims=True)
         e = [jnp.exp2(s - top) for s in x]
@@ -166,7 +178,9 @@
             jnp.dot(vs[j, lo:hi, :], e[j].astype(BF), preferred_element_type=F32)
             for j in range(3)
         )
-        mix[0, lo:hi, :] = (o * inv).astype(BF)
+        o = o * inv
+        mix[0, lo:mid, :] = o[:HEAD_DIM, :lon].astype(BF)
+        mix[0, mid:hi, :] = o[HEAD_DIM:, lon:].astype(BF)
 
     odd = frame % 2
     back = [0, 2, jnp.where(odd == 1, 1, -1), jnp.where(odd == 1, 3, 1), jnp.where(odd == 1, -1, 3)]

time: 41.8 us -> 40.9 us (0.978)
  Pallas kernels: 7.99 us -> 7.15 us
    pallas_call x1, Pallas kernels: 7.54 us -> 6.69 us  [body(): pl.pallas_call(functools.partial(kernel, n_time, n, nf), out_shape=jax.Sh...]
where the time goes in v4:
time: 40.9 us; the launch traced here: 40.7 us
  starting transfers between devices  25 us (61%)
  Pallas kernels  7.15 us (17%)
  waiting for transfers between devices  4.81 us (12%)
  between operations  1.48 us (4%)
  other arithmetic  1.23 us (3%)
  local copies, waits for them, and re-layouts  1.04 us (3%)
    ppermute x4, starting transfers between devices, body(): chain0.append(lax.ppermute(a, AXES, ring))  8.81 us
    ppermute x3, starting transfers between devices, body(): chain1.append(lax.ppermute(b, AXES, ring))  7.98 us
    pallas_call x1, Pallas kernels, body(): pl.pallas_call(functools.partial(kernel, n_time, n, nf), out_shape=jax.Sh...  6.69 us
    ppermute x4, waiting for transfers between devices, body(): chain0.append(lax.ppermute(a, AXES, ring))  2.44 us
    ppermute x1, starting transfers between devices, rotate_frame(): lax.ppermute(block, 'frame', [(i, (i + hop) % nf) for i in range(nf)])  2 us
    ppermute x1, starting transfers between devices, body(): partner_two = lax.ppermute(two_back, AXES, core)  1.81 us
    ppermute x1, starting transfers between devices, body(): partner = lax.ppermute(state, AXES, core)  1.34 us
    select_n x1, other arithmetic, body(): own1 = jnp.where(parity == 0, chunk_b, chunk_a)  1.12 us
  transfers between devices with their start and end apart: 19, of which 6 were waited for; matrix products, arithmetic and copies ran while one was open for 0% of the time, Pallas kernels for 1%

profile of v4, /device:TPU:0, one launch (start us, length us, event | category | flops | bytes accessed | tf_op | source)
XLA Modules:
  0.0 40.7 jit_solution(9508781996591143525)
XLA Ops:
  0.0 0.9 %fusion = (bf16[512,64]{0,1:T(8,128)(2,1)S(1)}, bf16[512,64]{0,1:T(8,128)(2,1)S(1)}) fusion(bf16[1024,64]{0,1:T(8,128)(2,1)} %param.19), kind=kLoop, calls=%fused_computation.12 | loop fusion | bytes 262144 | tf_op jit(solution)/shard_map/slice | solution.py:248
  0.9 1.1 %select_bitcast_fusion = (bf16[256,512]{1,0:T(8,128)(2,1)S(1)}, bf16[256,512]{1,0:T(8,128)(2,1)S(1)}) fusion(pred[]{:T(512)S(6)} %eq.6, bf16[512,64]{0,1:T(8,128)(2,1)S(1)} %get-tuple-element.12, bf16[512,192]{0,1:T(8,128)(2,1)} %param.18, bf16[512,64]{0,1:T(8,128)(2,1)S(1)} %get-tuple-element.11, bf16[512,192]{0,1:T(8,128)(2,1)} %param.17), kind=kLoop, calls=%fused_computation.3 | loop fusion | flops 1310720 | bytes 1048577 | tf_op jit(solution)/shard_map/jit(_where)/select_n | solution.py:251
  2.1 3.1 %collective-permute-start = (bf16[256,512]{1,0:T(8,128)(2,1)S(1)}, bf16[256,512]{1,0:T(8,128)(2,1)S(1)}, u32[]{:S(2)}, u32[]{:S(2)}) collective-permute-start(bf16[256,512]{1,0:T(8,128)(2,1)S(1)} %get-tuple-element.10.rest_2_), channel_id=1, source_target_pairs={{0,2},{2,4},{4,6},{6,7},{7,5},{5,3},{3,1},{1,0},{8,9},{10,8},{12,1... | collective-permute-start | bytes 786440 | tf_op jit(solution)/shard_map/ppermute | solution.py:266
  5.1 1.6 %collective-permute-start.9 = (bf16[256,512]{1,0:T(8,128)(2,1)S(1)}, bf16[256,512]{1,0:T(8,128)(2,1)S(1)}, u32[]{:S(2)}, u32[]{:S(2)}) collective-permute-start(bf16[256,512]{1,0:T(8,128)(2,1)S(1)} %get-tuple-element.9.rest_10_), channel_id=1, source_target_pairs={{0,2},{2,4},{4,6},{6,7},{7,5},{5,3},{3,1},{1,0},{8,9},{10,8},{12,1... | collective-permute-start | bytes 786440 | tf_op jit(solution)/shard_map/ppermute | solution.py:268
  8.1 1.3 %collective-permute-done.rest_3_ = bf16[256,512]{1,0:T(8,128)(2,1)S(1)} collective-permute-done((bf16[256,512]{1,0:T(8,128)(2,1)S(1)}, bf16[256,512]{1,0:T(8,128)(2,1)S(1)}, u32[]{:S(2)}, u32[]{:S(2)}) %collective-permute-start) | collective-permute-done | bytes 262176 | tf_op jit(solution)/shard_map/ppermute | solution.py:266
  9.4 2.1 %collective-permute-start.6 = (bf16[256,512]{1,0:T(8,128)(2,1)S(1)}, bf16[256,512]{1,0:T(8,128)(2,1)S(1)}, u32[]{:S(2)}, u32[]{:S(2)}) collective-permute-start(bf16[256,512]{1,0:T(8,128)(2,1)S(1)} %collective-permute-done.rest_3_), channel_id=1, source_target_pairs={{0,2},{2,4},{4,6},{6,7},{7,5},{5,3},{3,1},{1,0},{8,9},{10,8},{12,1... | collective-permute-start | bytes 786440 | tf_op jit(solution)/shard_map/ppermute | solution.py:266
  11.5 0.7 %collective-permute-start.2 = (bf16[180,512]{1,0:T(8,128)(2,1)S(1)}, bf16[180,512]{1,0:T(8,128)(2,1)S(1)}, u32[]{:S(2)}, u32[]{:S(2)}) collective-permute-start(bf16[180,512]{1,0:T(8,128)(2,1)S(1)} %bitcast.24), channel_id=1, source_target_pairs={{1,2},{2,1},{3,4},{4,3},{5,6},{6,5},{9,10},{10,9},{11,12},{12,11},... | collective-permute-start | bytes 552968 | tf_op jit(solution)/shard_map/ppermute | solution.py:66
  12.2 2.0 %collective-permute-start.3 = (bf16[180,512]{1,0:T(8,128)(2,1)S(1)}, bf16[180,512]{1,0:T(8,128)(2,1)S(1)}, u32[]{:S(2)}, u32[]{:S(2)}) collective-permute-start(bf16[180,512]{1,0:T(8,128)(2,1)S(1)} %bitcast.25), channel_id=1, source_target_pairs={{0,16},{8,24},{16,0},{24,8},{1,17},{9,25},{17,1},{25,9},{2,18},{10... | collective-permute-start | bytes 552968 | tf_op jit(solution)/shard_map/ppermute | solution.py:58
  14.2 4.3 %collective-permute-start.11 = (bf16[256,512]{1,0:T(8,128)(2,1)S(1)}, bf16[256,512]{1,0:T(8,128)(2,1)S(1)}, u32[]{:S(2)}, u32[]{:S(2)}) collective-permute-start(bf16[256,512]{1,0:T(8,128)(2,1)S(1)} %collective-permute-done.9.rest_11_), channel_id=1, source_target_pairs={{0,2},{2,4},{4,6},{6,7},{7,5},{5,3},{3,1},{1,0},{8,9},{10,8},{12,1... | collective-permute-start | bytes 786440 | tf_op jit(solution)/shard_map/ppermute | solution.py:268
  18.5 1.6 %collective-permute-start.7 = (bf16[256,512]{1,0:T(8,128)(2,1)S(1)}, bf16[256,512]{1,0:T(8,128)(2,1)S(1)}, u32[]{:S(2)}, u32[]{:S(2)}) collective-permute-start(bf16[256,512]{1,0:T(8,128)(2,1)S(1)} %collective-permute-done.6.rest_4_), channel_id=1, source_target_pairs={{0,2},{2,4},{4,6},{6,7},{7,5},{5,3},{3,1},{1,0},{8,9},{10,8},{12,1... | collective-permute-start | bytes 786440 | tf_op jit(solution)/shard_map/ppermute | solution.py:266
  20.2 1.3 %collective-permute-start.4 = (bf16[180,512]{1,0:T(8,128)(2,1)S(1)}, bf16[180,512]{1,0:T(8,128)(2,1)S(1)}, u32[]{:S(2)}, u32[]{:S(2)}) collective-permute-start(bf16[180,512]{1,0:T(8,128)(2,1)S(1)} %bitcast.27), channel_id=1, source_target_pairs={{0,8},{1,9},{2,10},{3,11},{4,12},{5,13},{6,14},{7,15},{8,0},{9,1},... | collective-permute-start | bytes 552968 | tf_op jit(solution)/shard_map/ppermute | solution.py:274
  21.6 0.5 %collective-permute-start.16 = (bf16[256,512]{1,0:T(8,128)(2,1)S(1)}, bf16[256,512]{1,0:T(8,128)(2,1)S(1)}, u32[]{:S(2)}, u32[]{:S(2)}) collective-permute-start(bf16[256,512]{1,0:T(8,128)(2,1)S(1)} %collective-permute-done.rest_3_), channel_id=1, source_target_pairs={{0,8},{1,9},{2,10},{3,11},{4,12},{5,13},{6,14},{7,15},{8,0},{9,1},... | collective-permute-start | bytes 786440 | tf_op jit(solution)/shard_map/ppermute | solution.py:269
  22.1 0.7 %collective-permute-done.11.rest_12_ = bf16[256,512]{1,0:T(8,128)(2,1)S(1)} collective-permute-done((bf16[256,512]{1,0:T(8,128)(2,1)S(1)}, bf16[256,512]{1,0:T(8,128)(2,1)S(1)}, u32[]{:S(2)}, u32[]{:S(2)}) %collective-permute-start.11) | collective-permute-done | bytes 262176 | tf_op jit(solution)/shard_map/ppermute | solution.py:268
  22.8 2.1 %collective-permute-start.13 = (bf16[256,512]{1,0:T(8,128)(2,1)S(1)}, bf16[256,512]{1,0:T(8,128)(2,1)S(1)}, u32[]{:S(2)}, u32[]{:S(2)}) collective-permute-start(bf16[256,512]{1,0:T(8,128)(2,1)S(1)} %collective-permute-done.11.rest_12_), channel_id=1, source_target_pairs={{0,2},{2,4},{4,6},{6,7},{7,5},{5,3},{3,1},{1,0},{8,9},{10,8},{12,1... | collective-permute-start | bytes 786440 | tf_op jit(solution)/shard_map/ppermute | solution.py:268
  24.9 0.7 %collective-permute-done.7.rest_5_ = bf16[256,512]{1,0:T(8,128)(2,1)S(1)} collective-permute-done((bf16[256,512]{1,0:T(8,128)(2,1)S(1)}, bf16[256,512]{1,0:T(8,128)(2,1)S(1)}, u32[]{:S(2)}, u32[]{:S(2)}) %collective-permute-start.7) | collective-permute-done | bytes 262176 | tf_op jit(solution)/shard_map/ppermute | solution.py:266
  25.6 2.1 %collective-permute-start.8 = (bf16[256,512]{1,0:T(8,128)(2,1)S(1)}, bf16[256,512]{1,0:T(8,128)(2,1)S(1)}, u32[]{:S(2)}, u32[]{:S(2)}) collective-permute-start(bf16[256,512]{1,0:T(8,128)(2,1)S(1)} %collective-permute-done.7.rest_5_), channel_id=1, source_target_pairs={{0,2},{2,4},{4,6},{6,7},{7,5},{5,3},{3,1},{1,0},{8,9},{10,8},{12,1... | collective-permute-start | bytes 786440 | tf_op jit(solution)/shard_map/ppermute | solution.py:266
  27.7 1.8 %collective-permute-start.5 = (bf16[180,512]{1,0:T(8,128)(2,1)S(1)}, bf16[180,512]{1,0:T(8,128)(2,1)S(1)}, u32[]{:S(2)}, u32[]{:S(2)}) collective-permute-start(bf16[180,512]{1,0:T(8,128)(2,1)S(1)} %collective-permute-done.3), channel_id=1, source_target_pairs={{0,8},{1,9},{2,10},{3,11},{4,12},{5,13},{6,14},{7,15},{8,0},{9,1},... | collective-permute-start | bytes 552968 | tf_op jit(solution)/shard_map/ppermute | solution.py:275
  29.6 1.0 %collective-permute-done.5 = bf16[180,512]{1,0:T(8,128)(2,1)S(1)} collective-permute-done((bf16[180,512]{1,0:T(8,128)(2,1)S(1)}, bf16[180,512]{1,0:T(8,128)(2,1)S(1)}, u32[]{:S(2)}, u32[]{:S(2)}) %collective-permute-start.5) | collective-permute-done | bytes 184352 | tf_op jit(solution)/shard_map/ppermute | solution.py:275
  30.6 0.4 collective-permute-start.12
  31.1 0.4 collective-permute-start.18
  32.0 0.9 %collective-permute-start.15 = (bf16[256,512]{1,0:T(8,128)(2,1)S(1)}, bf16[256,512]{1,0:T(8,128)(2,1)S(1)}, u32[]{:S(2)}, u32[]{:S(2)}) collective-permute-start(bf16[256,512]{1,0:T(8,128)(2,1)S(1)} %collective-permute-done.8.rest_6_), channel_id=1, source_target_pairs={{0,8},{1,9},{2,10},{3,11},{4,12},{5,13},{6,14},{7,15},{8,0},{9,1},... | collective-permute-start | bytes 786440 | tf_op jit(solution)/shard_map/ppermute | solution.py:271
  33.0 0.5 %norm.1.rest_0_ = bf16[6,180,512]{2,1,0:T(8,128)(2,1)S(1)} custom-call(f32[1,512]{1,0:T(1,128)S(1)} %bitcast.22, bf16[6,180,512]{2,1,0:T(8,128)(2,1)S(1)} %bitcast_dynamic-update-slice_fusion.rows_ref), custom_call_target="tpu_custom_call" | custom-call | tf_op jit(solution)/shard_map/norm/pallas_call | solution.py:282
  33.5 0.6 %collective-permute-done.15.rest_14_ = bf16[256,512]{1,0:T(8,128)(2,1)S(1)} collective-permute-done((bf16[256,512]{1,0:T(8,128)(2,1)S(1)}, bf16[256,512]{1,0:T(8,128)(2,1)S(1)}, u32[]{:S(2)}, u32[]{:S(2)}) %collective-permute-start.15) | collective-permute-done | bytes 262176 | tf_op jit(solution)/shard_map/ppermute | solution.py:271
  34.0 6.7 %block.1 = bf16[180,512]{1,0:T(8,128)(2,1)} custom-call(s32[4]{0:T(128)S(1)} %pad_add_fusion.meta, f32[2,8]{1,0:T(2,128)S(1)} %copy-done.1, s32[8]{0:T(128)S(1)} %copy-done.2, bf16[6,180,512]{2,1,0:T(8,128)(2,1)S(1)} %norm.1.rest_0_, bf16[2,180,512]{2,1,0:T(8,128)(2,1)S(1)} %pad_maximum_fusion.rest_1_, bf16[256,512]{1,0:T(8,128)(2,1)S(1)} %get-tuple-element.10.rest_2_, ...), custom_call_target="tpu_custom_call" | custom-call | tf_op jit(solution)/shard_map/block/pallas_call | solution.py:291
  (36 shorter events, 1.0 us)
Async XLA Ops:
  0.0 11.5 %copy-start.3 = (bf16[1,1,180,512]{3,2,1,0:T(8,128)(2,1)S(1)}, bf16[1,1,180,512]{3,2,1,0:T(8,128)(2,1)}, u32[]{:S(2)}) copy-start(bf16[1,1,180,512]{3,2,1,0:T(8,128)(2,1)} %param.10) | copy-start | bytes 552964
  0.0 20.1 %copy-start.4 = (bf16[1,1,180,512]{3,2,1,0:T(8,128)(2,1)S(1)}, bf16[1,1,180,512]{3,2,1,0:T(8,128)(2,1)}, u32[]{:S(2)}) copy-start(bf16[1,1,180,512]{3,2,1,0:T(8,128)(2,1)} %param.11) | copy-start | bytes 552964
  2.1 7.4 %collective-permute-start = (bf16[256,512]{1,0:T(8,128)(2,1)S(1)}, bf16[256,512]{1,0:T(8,128)(2,1)S(1)}, u32[]{:S(2)}, u32[]{:S(2)}) collective-permute-start(bf16[256,512]{1,0:T(8,128)(2,1)S(1)} %get-tuple-element.10.rest_2_), channel_id=1, source_target_pairs={{0,2},{2,4},{4,6},{6,7},{7,5},{5,3},{3,1},{1,0},{8,9},{10,8},{12,1... | collective-permute-start | bytes 786440 | tf_op jit(solution)/shard_map/ppermute | solution.py:266
  5.1 9.1 %collective-permute-start.9 = (bf16[256,512]{1,0:T(8,128)(2,1)S(1)}, bf16[256,512]{1,0:T(8,128)(2,1)S(1)}, u32[]{:S(2)}, u32[]{:S(2)}) collective-permute-start(bf16[256,512]{1,0:T(8,128)(2,1)S(1)} %get-tuple-element.9.rest_10_), channel_id=1, source_target_pairs={{0,2},{2,4},{4,6},{6,7},{7,5},{5,3},{3,1},{1,0},{8,9},{10,8},{12,1... | collective-permute-start | bytes 786440 | tf_op jit(solution)/shard_map/ppermute | solution.py:268
  9.4 9.1 %collective-permute-start.6 = (bf16[256,512]{1,0:T(8,128)(2,1)S(1)}, bf16[256,512]{1,0:T(8,128)(2,1)S(1)}, u32[]{:S(2)}, u32[]{:S(2)}) collective-permute-start(bf16[256,512]{1,0:T(8,128)(2,1)S(1)} %collective-permute-done.rest_3_), channel_id=1, source_target_pairs={{0,2},{2,4},{4,6},{6,7},{7,5},{5,3},{3,1},{1,0},{8,9},{10,8},{12,1... | collective-permute-start | bytes 786440 | tf_op jit(solution)/shard_map/ppermute | solution.py:266
  11.5 8.7 %collective-permute-start.1 = (bf16[180,512]{1,0:T(8,128)(2,1)S(1)}, bf16[180,512]{1,0:T(8,128)(2,1)S(1)}, u32[]{:S(2)}, u32[]{:S(2)}) collective-permute-start(bf16[180,512]{1,0:T(8,128)(2,1)S(1)} %bitcast.23), channel_id=1, source_target_pairs={{0,1},{1,0},{2,3},{3,2},{4,5},{5,4},{6,7},{7,6},{8,9},{9,8},{10,11... | collective-permute-start | bytes 552968 | tf_op jit(solution)/shard_map/ppermute | solution.py:66
  11.5 10.0 %collective-permute-start.2 = (bf16[180,512]{1,0:T(8,128)(2,1)S(1)}, bf16[180,512]{1,0:T(8,128)(2,1)S(1)}, u32[]{:S(2)}, u32[]{:S(2)}) collective-permute-start(bf16[180,512]{1,0:T(8,128)(2,1)S(1)} %bitcast.24), channel_id=1, source_target_pairs={{1,2},{2,1},{3,4},{4,3},{5,6},{6,5},{9,10},{10,9},{11,12},{12,11},... | collective-permute-start | bytes 552968 | tf_op jit(solution)/shard_map/ppermute | solution.py:66
  12.2 9.4 %collective-permute-start.3 = (bf16[180,512]{1,0:T(8,128)(2,1)S(1)}, bf16[180,512]{1,0:T(8,128)(2,1)S(1)}, u32[]{:S(2)}, u32[]{:S(2)}) collective-permute-start(bf16[180,512]{1,0:T(8,128)(2,1)S(1)} %bitcast.25), channel_id=1, source_target_pairs={{0,16},{8,24},{16,0},{24,8},{1,17},{9,25},{17,1},{25,9},{2,18},{10... | collective-permute-start | bytes 552968 | tf_op jit(solution)/shard_map/ppermute | solution.py:58
  14.2 8.6 %collective-permute-start.11 = (bf16[256,512]{1,0:T(8,128)(2,1)S(1)}, bf16[256,512]{1,0:T(8,128)(2,1)S(1)}, u32[]{:S(2)}, u32[]{:S(2)}) collective-permute-start(bf16[256,512]{1,0:T(8,128)(2,1)S(1)} %collective-permute-done.9.rest_11_), channel_id=1, source_target_pairs={{0,2},{2,4},{4,6},{6,7},{7,5},{5,3},{3,1},{1,0},{8,9},{10,8},{12,1... | collective-permute-start | bytes 786440 | tf_op jit(solution)/shard_map/ppermute | solution.py:268
  18.5 7.1 %collective-permute-start.7 = (bf16[256,512]{1,0:T(8,128)(2,1)S(1)}, bf16[256,512]{1,0:T(8,128)(2,1)S(1)}, u32[]{:S(2)}, u32[]{:S(2)}) collective-permute-start(bf16[256,512]{1,0:T(8,128)(2,1)S(1)} %collective-permute-done.6.rest_4_), channel_id=1, source_target_pairs={{0,2},{2,4},{4,6},{6,7},{7,5},{5,3},{3,1},{1,0},{8,9},{10,8},{12,1... | collective-permute-start | bytes 786440 | tf_op jit(solution)/shard_map/ppermute | solution.py:266
  20.2 12.8 %copy-start = (f32[512]{0:T(512)S(1)}, f32[512]{0:T(512)}, u32[]{:S(2)}) copy-start(f32[512]{0:T(512)} %param.15) | copy-start | bytes 6148
  20.2 7.6 %collective-permute-start.4 = (bf16[180,512]{1,0:T(8,128)(2,1)S(1)}, bf16[180,512]{1,0:T(8,128)(2,1)S(1)}, u32[]{:S(2)}, u32[]{:S(2)}) collective-permute-start(bf16[180,512]{1,0:T(8,128)(2,1)S(1)} %bitcast.27), channel_id=1, source_target_pairs={{0,8},{1,9},{2,10},{3,11},{4,12},{5,13},{6,14},{7,15},{8,0},{9,1},... | collective-permute-start | bytes 552968 | tf_op jit(solution)/shard_map/ppermute | solution.py:274
  21.6 9.4 %collective-permute-start.10 = (bf16[256,512]{1,0:T(8,128)(2,1)S(1)}, bf16[256,512]{1,0:T(8,128)(2,1)S(1)}, u32[]{:S(2)}, u32[]{:S(2)}) collective-permute-start(bf16[256,512]{1,0:T(8,128)(2,1)S(1)} %collective-permute-done.9.rest_11_), channel_id=1, source_target_pairs={{0,8},{1,9},{2,10},{3,11},{4,12},{5,13},{6,14},{7,15},{8,0},{9,1},... | collective-permute-start | bytes 786440 | tf_op jit(solution)/shard_map/ppermute | solution.py:270
  21.6 9.5 %collective-permute-start.16 = (bf16[256,512]{1,0:T(8,128)(2,1)S(1)}, bf16[256,512]{1,0:T(8,128)(2,1)S(1)}, u32[]{:S(2)}, u32[]{:S(2)}) collective-permute-start(bf16[256,512]{1,0:T(8,128)(2,1)S(1)} %collective-permute-done.rest_3_), channel_id=1, source_target_pairs={{0,8},{1,9},{2,10},{3,11},{4,12},{5,13},{6,14},{7,15},{8,0},{9,1},... | collective-permute-start | bytes 786440 | tf_op jit(solution)/shard_map/ppermute | solution.py:269
  22.8 8.7 %collective-permute-start.13 = (bf16[256,512]{1,0:T(8,128)(2,1)S(1)}, bf16[256,512]{1,0:T(8,128)(2,1)S(1)}, u32[]{:S(2)}, u32[]{:S(2)}) collective-permute-start(bf16[256,512]{1,0:T(8,128)(2,1)S(1)} %collective-permute-done.11.rest_12_), channel_id=1, source_target_pairs={{0,2},{2,4},{4,6},{6,7},{7,5},{5,3},{3,1},{1,0},{8,9},{10,8},{12,1... | collective-permute-start | bytes 786440 | tf_op jit(solution)/shard_map/ppermute | solution.py:268
  25.6 6.4 %collective-permute-start.8 = (bf16[256,512]{1,0:T(8,128)(2,1)S(1)}, bf16[256,512]{1,0:T(8,128)(2,1)S(1)}, u32[]{:S(2)}, u32[]{:S(2)}) collective-permute-start(bf16[256,512]{1,0:T(8,128)(2,1)S(1)} %collective-permute-done.7.rest_5_), channel_id=1, source_target_pairs={{0,2},{2,4},{4,6},{6,7},{7,5},{5,3},{3,1},{1,0},{8,9},{10,8},{12,1... | collective-permute-start | bytes 786440 | tf_op jit(solution)/shard_map/ppermute | solution.py:266
  27.7 2.9 %collective-permute-start.5 = (bf16[180,512]{1,0:T(8,128)(2,1)S(1)}, bf16[180,512]{1,0:T(8,128)(2,1)S(1)}, u32[]{:S(2)}, u32[]{:S(2)}) collective-permute-start(bf16[180,512]{1,0:T(8,128)(2,1)S(1)} %collective-permute-done.3), channel_id=1, source_target_pairs={{0,8},{1,9},{2,10},{3,11},{4,12},{5,13},{6,14},{7,15},{8,0},{9,1},... | collective-permute-start | bytes 552968 | tf_op jit(solution)/shard_map/ppermute | solution.py:275
  30.6 2.8 %collective-permute-start.12 = (bf16[256,512]{1,0:T(8,128)(2,1)S(1)}, bf16[256,512]{1,0:T(8,128)(2,1)S(1)}, u32[]{:S(2)}, u32[]{:S(2)}) collective-permute-start(bf16[256,512]{1,0:T(8,128)(2,1)S(1)} %collective-permute-done.11.rest_12_), channel_id=1, source_target_pairs={{0,8},{1,9},{2,10},{3,11},{4,12},{5,13},{6,14},{7,15},{8,0},{9,1},... | collective-permute-start | bytes 786440 | tf_op jit(solution)/shard_map/ppermute | solution.py:270
  31.0 2.4 %collective-permute-start.17 = (bf16[256,512]{1,0:T(8,128)(2,1)S(1)}, bf16[256,512]{1,0:T(8,128)(2,1)S(1)}, u32[]{:S(2)}, u32[]{:S(2)}) collective-permute-start(bf16[256,512]{1,0:T(8,128)(2,1)S(1)} %collective-permute-done.6.rest_4_), channel_id=1, source_target_pairs={{0,8},{1,9},{2,10},{3,11},{4,12},{5,13},{6,14},{7,15},{8,0},{9,1},... | collective-permute-start | bytes 786440 | tf_op jit(solution)/shard_map/ppermute | solution.py:269
  31.1 2.3 %collective-permute-start.18 = (bf16[256,512]{1,0:T(8,128)(2,1)S(1)}, bf16[256,512]{1,0:T(8,128)(2,1)S(1)}, u32[]{:S(2)}, u32[]{:S(2)}) collective-permute-start(bf16[256,512]{1,0:T(8,128)(2,1)S(1)} %collective-permute-done.7.rest_5_), channel_id=1, source_target_pairs={{0,8},{1,9},{2,10},{3,11},{4,12},{5,13},{6,14},{7,15},{8,0},{9,1},... | collective-permute-start | bytes 786440 | tf_op jit(solution)/shard_map/ppermute | solution.py:269
  31.5 1.9 %collective-permute-start.14 = (bf16[256,512]{1,0:T(8,128)(2,1)S(1)}, bf16[256,512]{1,0:T(8,128)(2,1)S(1)}, u32[]{:S(2)}, u32[]{:S(2)}) collective-permute-start(bf16[256,512]{1,0:T(8,128)(2,1)S(1)} %collective-permute-done.13.rest_13_), channel_id=1, source_target_pairs={{0,8},{1,9},{2,10},{3,11},{4,12},{5,13},{6,14},{7,15},{8,0},{9,1},... | collective-permute-start | bytes 786440 | tf_op jit(solution)/shard_map/ppermute | solution.py:270
  32.0 2.0 %collective-permute-start.15 = (bf16[256,512]{1,0:T(8,128)(2,1)S(1)}, bf16[256,512]{1,0:T(8,128)(2,1)S(1)}, u32[]{:S(2)}, u32[]{:S(2)}) collective-permute-start(bf16[256,512]{1,0:T(8,128)(2,1)S(1)} %collective-permute-done.8.rest_6_), channel_id=1, source_target_pairs={{0,8},{1,9},{2,10},{3,11},{4,12},{5,13},{6,14},{7,15},{8,0},{9,1},... | collective-permute-start | bytes 786440 | tf_op jit(solution)/shard_map/ppermute | solution.py:271
  32.9 1.1 %copy-start.1 = (f32[2,8]{1,0:T(2,128)S(1)}, f32[2,8]{1,0:T(2,128)}, u32[]{:S(2)}) copy-start(f32[2,8]{1,0:T(2,128)} %scales.1) | copy-start | bytes 196
  32.9 1.1 %copy-start.2 = (s32[8]{0:T(128)S(1)}, s32[8]{0:T(128)}, u32[]{:S(2)}) copy-start(s32[8]{0:T(128)} %tally.1) | copy-start | bytes 100

commit v5 on v4

--- a/solution.py
+++ b/solution.py
@@ -113,8 +113,8 @@
         x = normed[j]
         ks[j] = unit_rows(proj(0, 1, x)).astype(BF)
         vs[j] = proj(0, 2, x).astype(BF)
-    kcol = lax.broadcasted_iota(jnp.int32, (lon, lon), 0)
-    qcol = lax.broadcasted_iota(jnp.int32, (lon, lon), 1)
+    kcol = lax.broadcasted_iota(jnp.int32, (lon, 1), 0)
+    qcol = lax.broadcasted_iota(jnp.int32, (1, lon), 1)
 
     def window(col):
         c = col - shift
@@ -204,10 +204,10 @@
         )
         mix[1, lo:hi, :] = o.astype(BF)
 
-    update = jnp.dot(final[0], mix[0], preferred_element_type=F32) + jnp.dot(
-        final[1], mix[1], preferred_element_type=F32
+    update = sum(
+        lax.dot_general(mix[w], final[w], (((0,), (1,)), ((), ())), preferred_element_type=F32)
+        for w in (0, 1)
     )
-    update = update.T
 
     def sigma_of(lv):
         power = (jnp.full((1, width), lv, jnp.int32).astype(F32) + 1.0) / total_levels

time: 40.9 us -> 40.7 us (level)
  no operation moved by 1% of the time
where the time goes in v5:
time: 40.7 us; the launch traced here: 40.5 us
  starting transfers between devices  25 us (61%)
  Pallas kernels  6.9 us (17%)
  waiting for transfers between devices  4.81 us (12%)
  between operations  1.48 us (4%)
  other arithmetic  1.23 us (3%)
  local copies, waits for them, and re-layouts  1.04 us (3%)
    ppermute x4, starting transfers between devices, body(): chain0.append(lax.ppermute(a, AXES, ring))  8.81 us
    ppermute x3, starting transfers between devices, body(): chain1.append(lax.ppermute(b, AXES, ring))  7.98 us
    pallas_call x1, Pallas kernels, body(): pl.pallas_call(functools.partial(kernel, n_time, n, nf), out_shape=jax.Sh...  6.45 us
    ppermute x4, waiting for transfers between devices, body(): chain0.append(lax.ppermute(a, AXES, ring))  2.44 us
    ppermute x1, starting transfers between devices, rotate_frame(): lax.ppermute(block, 'frame', [(i, (i + hop) % nf) for i in range(nf)])  2 us
    ppermute x1, starting transfers between devices, body(): partner_two = lax.ppermute(two_back, AXES, core)  1.81 us
    ppermute x1, starting transfers between devices, body(): partner = lax.ppermute(state, AXES, core)  1.34 us
    select_n x1, other arithmetic, body(): own1 = jnp.where(parity == 0, chunk_b, chunk_a)  1.12 us
  transfers between devices with their start and end apart: 19, of which 6 were waited for; matrix products, arithmetic and copies ran while one was open for 0% of the time, Pallas kernels for 1%

profile of v5, /device:TPU:0, one launch (start us, length us, event | category | flops | bytes accessed | tf_op | source)
XLA Modules:
  0.0 40.5 jit_solution(8552200819435915824)
XLA Ops:
  0.0 0.9 %fusion = (bf16[512,64]{0,1:T(8,128)(2,1)S(1)}, bf16[512,64]{0,1:T(8,128)(2,1)S(1)}) fusion(bf16[1024,64]{0,1:T(8,128)(2,1)} %param.19), kind=kLoop, calls=%fused_computation.12 | loop fusion | bytes 262144 | tf_op jit(solution)/shard_map/slice | solution.py:248
  0.9 1.1 %select_bitcast_fusion = (bf16[256,512]{1,0:T(8,128)(2,1)S(1)}, bf16[256,512]{1,0:T(8,128)(2,1)S(1)}) fusion(pred[]{:T(512)S(6)} %eq.6, bf16[512,64]{0,1:T(8,128)(2,1)S(1)} %get-tuple-element.12, bf16[512,192]{0,1:T(8,128)(2,1)} %param.18, bf16[512,64]{0,1:T(8,128)(2,1)S(1)} %get-tuple-element.11, bf16[512,192]{0,1:T(8,128)(2,1)} %param.17), kind=kLoop, calls=%fused_computation.3 | loop fusion | flops 1310720 | bytes 1048577 | tf_op jit(solution)/shard_map/jit(_where)/select_n | solution.py:251
  2.1 3.1 %collective-permute-start = (bf16[256,512]{1,0:T(8,128)(2,1)S(1)}, bf16[256,512]{1,0:T(8,128)(2,1)S(1)}, u32[]{:S(2)}, u32[]{:S(2)}) collective-permute-start(bf16[256,512]{1,0:T(8,128)(2,1)S(1)} %get-tuple-element.10.rest_2_), channel_id=1, source_target_pairs={{0,2},{2,4},{4,6},{6,7},{7,5},{5,3},{3,1},{1,0},{8,9},{10,8},{12,1... | collective-permute-start | bytes 786440 | tf_op jit(solution)/shard_map/ppermute | solution.py:266
  5.1 1.6 %collective-permute-start.9 = (bf16[256,512]{1,0:T(8,128)(2,1)S(1)}, bf16[256,512]{1,0:T(8,128)(2,1)S(1)}, u32[]{:S(2)}, u32[]{:S(2)}) collective-permute-start(bf16[256,512]{1,0:T(8,128)(2,1)S(1)} %get-tuple-element.9.rest_10_), channel_id=1, source_target_pairs={{0,2},{2,4},{4,6},{6,7},{7,5},{5,3},{3,1},{1,0},{8,9},{10,8},{12,1... | collective-permute-start | bytes 786440 | tf_op jit(solution)/shard_map/ppermute | solution.py:268
  8.1 1.3 %collective-permute-done.rest_3_ = bf16[256,512]{1,0:T(8,128)(2,1)S(1)} collective-permute-done((bf16[256,512]{1,0:T(8,128)(2,1)S(1)}, bf16[256,512]{1,0:T(8,128)(2,1)S(1)}, u32[]{:S(2)}, u32[]{:S(2)}) %collective-permute-start) | collective-permute-done | bytes 262176 | tf_op jit(solution)/shard_map/ppermute | solution.py:266
  9.4 2.1 %collective-permute-start.6 = (bf16[256,512]{1,0:T(8,128)(2,1)S(1)}, bf16[256,512]{1,0:T(8,128)(2,1)S(1)}, u32[]{:S(2)}, u32[]{:S(2)}) collective-permute-start(bf16[256,512]{1,0:T(8,128)(2,1)S(1)} %collective-permute-done.rest_3_), channel_id=1, source_target_pairs={{0,2},{2,4},{4,6},{6,7},{7,5},{5,3},{3,1},{1,0},{8,9},{10,8},{12,1... | collective-permute-start | bytes 786440 | tf_op jit(solution)/shard_map/ppermute | solution.py:266
  11.5 0.7 %collective-permute-start.2 = (bf16[180,512]{1,0:T(8,128)(2,1)S(1)}, bf16[180,512]{1,0:T(8,128)(2,1)S(1)}, u32[]{:S(2)}, u32[]{:S(2)}) collective-permute-start(bf16[180,512]{1,0:T(8,128)(2,1)S(1)} %bitcast.24), channel_id=1, source_target_pairs={{1,2},{2,1},{3,4},{4,3},{5,6},{6,5},{9,10},{10,9},{11,12},{12,11},... | collective-permute-start | bytes 552968 | tf_op jit(solution)/shard_map/ppermute | solution.py:66
  12.2 2.0 %collective-permute-start.3 = (bf16[180,512]{1,0:T(8,128)(2,1)S(1)}, bf16[180,512]{1,0:T(8,128)(2,1)S(1)}, u32[]{:S(2)}, u32[]{:S(2)}) collective-permute-start(bf16[180,512]{1,0:T(8,128)(2,1)S(1)} %bitcast.25), channel_id=1, source_target_pairs={{0,16},{8,24},{16,0},{24,8},{1,17},{9,25},{17,1},{25,9},{2,18},{10... | collective-permute-start | bytes 552968 | tf_op jit(solution)/shard_map/ppermute | solution.py:58
  14.2 4.3 %collective-permute-start.11 = (bf16[256,512]{1,0:T(8,128)(2,1)S(1)}, bf16[256,512]{1,0:T(8,128)(2,1)S(1)}, u32[]{:S(2)}, u32[]{:S(2)}) collective-permute-start(bf16[256,512]{1,0:T(8,128)(2,1)S(1)} %collective-permute-done.9.rest_11_), channel_id=1, source_target_pairs={{0,2},{2,4},{4,6},{6,7},{7,5},{5,3},{3,1},{1,0},{8,9},{10,8},{12,1... | collective-permute-start | bytes 786440 | tf_op jit(solution)/shard_map/ppermute | solution.py:268
  18.5 1.6 %collective-permute-start.7 = (bf16[256,512]{1,0:T(8,128)(2,1)S(1)}, bf16[256,512]{1,0:T(8,128)(2,1)S(1)}, u32[]{:S(2)}, u32[]{:S(2)}) collective-permute-start(bf16[256,512]{1,0:T(8,128)(2,1)S(1)} %collective-permute-done.6.rest_4_), channel_id=1, source_target_pairs={{0,2},{2,4},{4,6},{6,7},{7,5},{5,3},{3,1},{1,0},{8,9},{10,8},{12,1... | collective-permute-start | bytes 786440 | tf_op jit(solution)/shard_map/ppermute | solution.py:266
  20.2 1.3 %collective-permute-start.4 = (bf16[180,512]{1,0:T(8,128)(2,1)S(1)}, bf16[180,512]{1,0:T(8,128)(2,1)S(1)}, u32[]{:S(2)}, u32[]{:S(2)}) collective-permute-start(bf16[180,512]{1,0:T(8,128)(2,1)S(1)} %bitcast.27), channel_id=1, source_target_pairs={{0,8},{1,9},{2,10},{3,11},{4,12},{5,13},{6,14},{7,15},{8,0},{9,1},... | collective-permute-start | bytes 552968 | tf_op jit(solution)/shard_map/ppermute | solution.py:274
  21.6 0.5 %collective-permute-start.16 = (bf16[256,512]{1,0:T(8,128)(2,1)S(1)}, bf16[256,512]{1,0:T(8,128)(2,1)S(1)}, u32[]{:S(2)}, u32[]{:S(2)}) collective-permute-start(bf16[256,512]{1,0:T(8,128)(2,1)S(1)} %collective-permute-done.rest_3_), channel_id=1, source_target_pairs={{0,8},{1,9},{2,10},{3,11},{4,12},{5,13},{6,14},{7,15},{8,0},{9,1},... | collective-permute-start | bytes 786440 | tf_op jit(solution)/shard_map/ppermute | solution.py:269
  22.1 0.7 %collective-permute-done.11.rest_12_ = bf16[256,512]{1,0:T(8,128)(2,1)S(1)} collective-permute-done((bf16[256,512]{1,0:T(8,128)(2,1)S(1)}, bf16[256,512]{1,0:T(8,128)(2,1)S(1)}, u32[]{:S(2)}, u32[]{:S(2)}) %collective-permute-start.11) | collective-permute-done | bytes 262176 | tf_op jit(solution)/shard_map/ppermute | solution.py:268
  22.8 2.1 %collective-permute-start.13 = (bf16[256,512]{1,0:T(8,128)(2,1)S(1)}, bf16[256,512]{1,0:T(8,128)(2,1)S(1)}, u32[]{:S(2)}, u32[]{:S(2)}) collective-permute-start(bf16[256,512]{1,0:T(8,128)(2,1)S(1)} %collective-permute-done.11.rest_12_), channel_id=1, source_target_pairs={{0,2},{2,4},{4,6},{6,7},{7,5},{5,3},{3,1},{1,0},{8,9},{10,8},{12,1... | collective-permute-start | bytes 786440 | tf_op jit(solution)/shard_map/ppermute | solution.py:268
  24.9 0.7 %collective-permute-done.7.rest_5_ = bf16[256,512]{1,0:T(8,128)(2,1)S(1)} collective-permute-done((bf16[256,512]{1,0:T(8,128)(2,1)S(1)}, bf16[256,512]{1,0:T(8,128)(2,1)S(1)}, u32[]{:S(2)}, u32[]{:S(2)}) %collective-permute-start.7) | collective-permute-done | bytes 262176 | tf_op jit(solution)/shard_map/ppermute | solution.py:266
  25.6 2.1 %collective-permute-start.8 = (bf16[256,512]{1,0:T(8,128)(2,1)S(1)}, bf16[256,512]{1,0:T(8,128)(2,1)S(1)}, u32[]{:S(2)}, u32[]{:S(2)}) collective-permute-start(bf16[256,512]{1,0:T(8,128)(2,1)S(1)} %collective-permute-done.7.rest_5_), channel_id=1, source_target_pairs={{0,2},{2,4},{4,6},{6,7},{7,5},{5,3},{3,1},{1,0},{8,9},{10,8},{12,1... | collective-permute-start | bytes 786440 | tf_op jit(solution)/shard_map/ppermute | solution.py:266
  27.7 1.8 %collective-permute-start.5 = (bf16[180,512]{1,0:T(8,128)(2,1)S(1)}, bf16[180,512]{1,0:T(8,128)(2,1)S(1)}, u32[]{:S(2)}, u32[]{:S(2)}) collective-permute-start(bf16[180,512]{1,0:T(8,128)(2,1)S(1)} %collective-permute-done.3), channel_id=1, source_target_pairs={{0,8},{1,9},{2,10},{3,11},{4,12},{5,13},{6,14},{7,15},{8,0},{9,1},... | collective-permute-start | bytes 552968 | tf_op jit(solution)/shard_map/ppermute | solution.py:275
  29.6 1.0 %collective-permute-done.5 = bf16[180,512]{1,0:T(8,128)(2,1)S(1)} collective-permute-done((bf16[180,512]{1,0:T(8,128)(2,1)S(1)}, bf16[180,512]{1,0:T(8,128)(2,1)S(1)}, u32[]{:S(2)}, u32[]{:S(2)}) %collective-permute-start.5) | collective-permute-done | bytes 184352 | tf_op jit(solution)/shard_map/ppermute | solution.py:275
  30.6 0.4 collective-permute-start.12
  31.1 0.4 collective-permute-start.18
  32.0 0.9 %collective-permute-start.15 = (bf16[256,512]{1,0:T(8,128)(2,1)S(1)}, bf16[256,512]{1,0:T(8,128)(2,1)S(1)}, u32[]{:S(2)}, u32[]{:S(2)}) collective-permute-start(bf16[256,512]{1,0:T(8,128)(2,1)S(1)} %collective-permute-done.8.rest_6_), channel_id=1, source_target_pairs={{0,8},{1,9},{2,10},{3,11},{4,12},{5,13},{6,14},{7,15},{8,0},{9,1},... | collective-permute-start | bytes 786440 | tf_op jit(solution)/shard_map/ppermute | solution.py:271
  33.0 0.5 %norm.1.rest_0_ = bf16[6,180,512]{2,1,0:T(8,128)(2,1)S(1)} custom-call(f32[1,512]{1,0:T(1,128)S(1)} %bitcast.22, bf16[6,180,512]{2,1,0:T(8,128)(2,1)S(1)} %bitcast_dynamic-update-slice_fusion.rows_ref), custom_call_target="tpu_custom_call" | custom-call | tf_op jit(solution)/shard_map/norm/pallas_call | solution.py:282
  33.5 0.6 %collective-permute-done.15.rest_14_ = bf16[256,512]{1,0:T(8,128)(2,1)S(1)} collective-permute-done((bf16[256,512]{1,0:T(8,128)(2,1)S(1)}, bf16[256,512]{1,0:T(8,128)(2,1)S(1)}, u32[]{:S(2)}, u32[]{:S(2)}) %collective-permute-start.15) | collective-permute-done | bytes 262176 | tf_op jit(solution)/shard_map/ppermute | solution.py:271
  34.0 6.5 %block.1 = bf16[180,512]{1,0:T(8,128)(2,1)} custom-call(s32[4]{0:T(128)S(1)} %pad_add_fusion.meta, f32[2,8]{1,0:T(2,128)S(1)} %copy-done.1, s32[8]{0:T(128)S(1)} %copy-done.2, bf16[6,180,512]{2,1,0:T(8,128)(2,1)S(1)} %norm.1.rest_0_, bf16[2,180,512]{2,1,0:T(8,128)(2,1)S(1)} %pad_maximum_fusion.rest_1_, bf16[256,512]{1,0:T(8,128)(2,1)S(1)} %get-tuple-element.10.rest_2_, ...), custom_call_target="tpu_custom_call" | custom-call | tf_op jit(solution)/shard_map/block/pallas_call | solution.py:291
  (36 shorter events, 1.0 us)
Async XLA Ops:
  0.0 11.5 %copy-start.3 = (bf16[1,1,180,512]{3,2,1,0:T(8,128)(2,1)S(1)}, bf16[1,1,180,512]{3,2,1,0:T(8,128)(2,1)}, u32[]{:S(2)}) copy-start(bf16[1,1,180,512]{3,2,1,0:T(8,128)(2,1)} %param.10) | copy-start | bytes 552964
  0.0 20.1 %copy-start.4 = (bf16[1,1,180,512]{3,2,1,0:T(8,128)(2,1)S(1)}, bf16[1,1,180,512]{3,2,1,0:T(8,128)(2,1)}, u32[]{:S(2)}) copy-start(bf16[1,1,180,512]{3,2,1,0:T(8,128)(2,1)} %param.11) | copy-start | bytes 552964
  2.1 7.4 %collective-permute-start = (bf16[256,512]{1,0:T(8,128)(2,1)S(1)}, bf16[256,512]{1,0:T(8,128)(2,1)S(1)}, u32[]{:S(2)}, u32[]{:S(2)}) collective-permute-start(bf16[256,512]{1,0:T(8,128)(2,1)S(1)} %get-tuple-element.10.rest_2_), channel_id=1, source_target_pairs={{0,2},{2,4},{4,6},{6,7},{7,5},{5,3},{3,1},{1,0},{8,9},{10,8},{12,1... | collective-permute-start | bytes 786440 | tf_op jit(solution)/shard_map/ppermute | solution.py:266
  5.1 9.1 %collective-permute-start.9 = (bf16[256,512]{1,0:T(8,128)(2,1)S(1)}, bf16[256,512]{1,0:T(8,128)(2,1)S(1)}, u32[]{:S(2)}, u32[]{:S(2)}) collective-permute-start(bf16[256,512]{1,0:T(8,128)(2,1)S(1)} %get-tuple-element.9.rest_10_), channel_id=1, source_target_pairs={{0,2},{2,4},{4,6},{6,7},{7,5},{5,3},{3,1},{1,0},{8,9},{10,8},{12,1... | collective-permute-start | bytes 786440 | tf_op jit(solution)/shard_map/ppermute | solution.py:268
  9.4 9.1 %collective-permute-start.6 = (bf16[256,512]{1,0:T(8,128)(2,1)S(1)}, bf16[256,512]{1,0:T(8,128)(2,1)S(1)}, u32[]{:S(2)}, u32[]{:S(2)}) collective-permute-start(bf16[256,512]{1,0:T(8,128)(2,1)S(1)} %collective-permute-done.rest_3_), channel_id=1, source_target_pairs={{0,2},{2,4},{4,6},{6,7},{7,5},{5,3},{3,1},{1,0},{8,9},{10,8},{12,1... | collective-permute-start | bytes 786440 | tf_op jit(solution)/shard_map/ppermute | solution.py:266
  11.5 8.7 %collective-permute-start.1 = (bf16[180,512]{1,0:T(8,128)(2,1)S(1)}, bf16[180,512]{1,0:T(8,128)(2,1)S(1)}, u32[]{:S(2)}, u32[]{:S(2)}) collective-permute-start(bf16[180,512]{1,0:T(8,128)(2,1)S(1)} %bitcast.23), channel_id=1, source_target_pairs={{0,1},{1,0},{2,3},{3,2},{4,5},{5,4},{6,7},{7,6},{8,9},{9,8},{10,11... | collective-permute-start | bytes 552968 | tf_op jit(solution)/shard_map/ppermute | solution.py:66
  11.5 10.0 %collective-permute-start.2 = (bf16[180,512]{1,0:T(8,128)(2,1)S(1)}, bf16[180,512]{1,0:T(8,128)(2,1)S(1)}, u32[]{:S(2)}, u32[]{:S(2)}) collective-permute-start(bf16[180,512]{1,0:T(8,128)(2,1)S(1)} %bitcast.24), channel_id=1, source_target_pairs={{1,2},{2,1},{3,4},{4,3},{5,6},{6,5},{9,10},{10,9},{11,12},{12,11},... | collective-permute-start | bytes 552968 | tf_op jit(solution)/shard_map/ppermute | solution.py:66
  12.2 9.4 %collective-permute-start.3 = (bf16[180,512]{1,0:T(8,128)(2,1)S(1)}, bf16[180,512]{1,0:T(8,128)(2,1)S(1)}, u32[]{:S(2)}, u32[]{:S(2)}) collective-permute-start(bf16[180,512]{1,0:T(8,128)(2,1)S(1)} %bitcast.25), channel_id=1, source_target_pairs={{0,16},{8,24},{16,0},{24,8},{1,17},{9,25},{17,1},{25,9},{2,18},{10... | collective-permute-start | bytes 552968 | tf_op jit(solution)/shard_map/ppermute | solution.py:58
  14.2 8.6 %collective-permute-start.11 = (bf16[256,512]{1,0:T(8,128)(2,1)S(1)}, bf16[256,512]{1,0:T(8,128)(2,1)S(1)}, u32[]{:S(2)}, u32[]{:S(2)}) collective-permute-start(bf16[256,512]{1,0:T(8,128)(2,1)S(1)} %collective-permute-done.9.rest_11_), channel_id=1, source_target_pairs={{0,2},{2,4},{4,6},{6,7},{7,5},{5,3},{3,1},{1,0},{8,9},{10,8},{12,1... | collective-permute-start | bytes 786440 | tf_op jit(solution)/shard_map/ppermute | solution.py:268
  18.5 7.1 %collective-permute-start.7 = (bf16[256,512]{1,0:T(8,128)(2,1)S(1)}, bf16[256,512]{1,0:T(8,128)(2,1)S(1)}, u32[]{:S(2)}, u32[]{:S(2)}) collective-permute-start(bf16[256,512]{1,0:T(8,128)(2,1)S(1)} %collective-permute-done.6.rest_4_), channel_id=1, source_target_pairs={{0,2},{2,4},{4,6},{6,7},{7,5},{5,3},{3,1},{1,0},{8,9},{10,8},{12,1... | collective-permute-start | bytes 786440 | tf_op jit(solution)/shard_map/ppermute | solution.py:266
  20.2 12.8 %copy-start = (f32[512]{0:T(512)S(1)}, f32[512]{0:T(512)}, u32[]{:S(2)}) copy-start(f32[512]{0:T(512)} %param.15) | copy-start | bytes 6148
  20.2 7.6 %collective-permute-start.4 = (bf16[180,512]{1,0:T(8,128)(2,1)S(1)}, bf16[180,512]{1,0:T(8,128)(2,1)S(1)}, u32[]{:S(2)}, u32[]{:S(2)}) collective-permute-start(bf16[180,512]{1,0:T(8,128)(2,1)S(1)} %bitcast.27), channel_id=1, source_target_pairs={{0,8},{1,9},{2,10},{3,11},{4,12},{5,13},{6,14},{7,15},{8,0},{9,1},... | collective-permute-start | bytes 552968 | tf_op jit(solution)/shard_map/ppermute | solution.py:274
  21.6 9.4 %collective-permute-start.10 = (bf16[256,512]{1,0:T(8,128)(2,1)S(1)}, bf16[256,512]{1,0:T(8,128)(2,1)S(1)}, u32[]{:S(2)}, u32[]{:S(2)}) collective-permute-start(bf16[256,512]{1,0:T(8,128)(2,1)S(1)} %collective-permute-done.9.rest_11_), channel_id=1, source_target_pairs={{0,8},{1,9},{2,10},{3,11},{4,12},{5,13},{6,14},{7,15},{8,0},{9,1},... | collective-permute-start | bytes 786440 | tf_op jit(solution)/shard_map/ppermute | solution.py:270
  21.6 9.5 %collective-permute-start.16 = (bf16[256,512]{1,0:T(8,128)(2,1)S(1)}, bf16[256,512]{1,0:T(8,128)(2,1)S(1)}, u32[]{:S(2)}, u32[]{:S(2)}) collective-permute-start(bf16[256,512]{1,0:T(8,128)(2,1)S(1)} %collective-permute-done.rest_3_), channel_id=1, source_target_pairs={{0,8},{1,9},{2,10},{3,11},{4,12},{5,13},{6,14},{7,15},{8,0},{9,1},... | collective-permute-start | bytes 786440 | tf_op jit(solution)/shard_map/ppermute | solution.py:269
  22.8 8.7 %collective-permute-start.13 = (bf16[256,512]{1,0:T(8,128)(2,1)S(1)}, bf16[256,512]{1,0:T(8,128)(2,1)S(1)}, u32[]{:S(2)}, u32[]{:S(2)}) collective-permute-start(bf16[256,512]{1,0:T(8,128)(2,1)S(1)} %collective-permute-done.11.rest_12_), channel_id=1, source_target_pairs={{0,2},{2,4},{4,6},{6,7},{7,5},{5,3},{3,1},{1,0},{8,9},{10,8},{12,1... | collective-permute-start | bytes 786440 | tf_op jit(solution)/shard_map/ppermute | solution.py:268
  25.6 6.4 %collective-permute-start.8 = (bf16[256,512]{1,0:T(8,128)(2,1)S(1)}, bf16[256,512]{1,0:T(8,128)(2,1)S(1)}, u32[]{:S(2)}, u32[]{:S(2)}) collective-permute-start(bf16[256,512]{1,0:T(8,128)(2,1)S(1)} %collective-permute-done.7.rest_5_), channel_id=1, source_target_pairs={{0,2},{2,4},{4,6},{6,7},{7,5},{5,3},{3,1},{1,0},{8,9},{10,8},{12,1... | collective-permute-start | bytes 786440 | tf_op jit(solution)/shard_map/ppermute | solution.py:266
  27.7 2.9 %collective-permute-start.5 = (bf16[180,512]{1,0:T(8,128)(2,1)S(1)}, bf16[180,512]{1,0:T(8,128)(2,1)S(1)}, u32[]{:S(2)}, u32[]{:S(2)}) collective-permute-start(bf16[180,512]{1,0:T(8,128)(2,1)S(1)} %collective-permute-done.3), channel_id=1, source_target_pairs={{0,8},{1,9},{2,10},{3,11},{4,12},{5,13},{6,14},{7,15},{8,0},{9,1},... | collective-permute-start | bytes 552968 | tf_op jit(solution)/shard_map/ppermute | solution.py:275
  30.6 2.8 %collective-permute-start.12 = (bf16[256,512]{1,0:T(8,128)(2,1)S(1)}, bf16[256,512]{1,0:T(8,128)(2,1)S(1)}, u32[]{:S(2)}, u32[]{:S(2)}) collective-permute-start(bf16[256,512]{1,0:T(8,128)(2,1)S(1)} %collective-permute-done.11.rest_12_), channel_id=1, source_target_pairs={{0,8},{1,9},{2,10},{3,11},{4,12},{5,13},{6,14},{7,15},{8,0},{9,1},... | collective-permute-start | bytes 786440 | tf_op jit(solution)/shard_map/ppermute | solution.py:270
  31.0 2.4 %collective-permute-start.17 = (bf16[256,512]{1,0:T(8,128)(2,1)S(1)}, bf16[256,512]{1,0:T(8,128)(2,1)S(1)}, u32[]{:S(2)}, u32[]{:S(2)}) collective-permute-start(bf16[256,512]{1,0:T(8,128)(2,1)S(1)} %collective-permute-done.6.rest_4_), channel_id=1, source_target_pairs={{0,8},{1,9},{2,10},{3,11},{4,12},{5,13},{6,14},{7,15},{8,0},{9,1},... | collective-permute-start | bytes 786440 | tf_op jit(solution)/shard_map/ppermute | solution.py:269
  31.1 2.3 %collective-permute-start.18 = (bf16[256,512]{1,0:T(8,128)(2,1)S(1)}, bf16[256,512]{1,0:T(8,128)(2,1)S(1)}, u32[]{:S(2)}, u32[]{:S(2)}) collective-permute-start(bf16[256,512]{1,0:T(8,128)(2,1)S(1)} %collective-permute-done.7.rest_5_), channel_id=1, source_target_pairs={{0,8},{1,9},{2,10},{3,11},{4,12},{5,13},{6,14},{7,15},{8,0},{9,1},... | collective-permute-start | bytes 786440 | tf_op jit(solution)/shard_map/ppermute | solution.py:269
  31.5 1.9 %collective-permute-start.14 = (bf16[256,512]{1,0:T(8,128)(2,1)S(1)}, bf16[256,512]{1,0:T(8,128)(2,1)S(1)}, u32[]{:S(2)}, u32[]{:S(2)}) collective-permute-start(bf16[256,512]{1,0:T(8,128)(2,1)S(1)} %collective-permute-done.13.rest_13_), channel_id=1, source_target_pairs={{0,8},{1,9},{2,10},{3,11},{4,12},{5,13},{6,14},{7,15},{8,0},{9,1},... | collective-permute-start | bytes 786440 | tf_op jit(solution)/shard_map/ppermute | solution.py:270
  32.0 2.0 %collective-permute-start.15 = (bf16[256,512]{1,0:T(8,128)(2,1)S(1)}, bf16[256,512]{1,0:T(8,128)(2,1)S(1)}, u32[]{:S(2)}, u32[]{:S(2)}) collective-permute-start(bf16[256,512]{1,0:T(8,128)(2,1)S(1)} %collective-permute-done.8.rest_6_), channel_id=1, source_target_pairs={{0,8},{1,9},{2,10},{3,11},{4,12},{5,13},{6,14},{7,15},{8,0},{9,1},... | collective-permute-start | bytes 786440 | tf_op jit(solution)/shard_map/ppermute | solution.py:271
  32.9 1.1 %copy-start.1 = (f32[2,8]{1,0:T(2,128)S(1)}, f32[2,8]{1,0:T(2,128)}, u32[]{:S(2)}) copy-start(f32[2,8]{1,0:T(2,128)} %scales.1) | copy-start | bytes 196
  32.9 1.1 %copy-start.2 = (s32[8]{0:T(128)S(1)}, s32[8]{0:T(128)}, u32[]{:S(2)}) copy-start(s32[8]{0:T(128)} %tally.1) | copy-start | bytes 100

commit v6 on v5

--- a/solution.py
+++ b/solution.py
@@ -186,23 +186,21 @@
     back = [0, 2, jnp.where(odd == 1, 1, -1), jnp.where(odd == 1, 3, 1), jnp.where(odd == 1, -1, 3)]
     allow = [(b >= 0) & (b <= PRIOR_SNAPSHOTS) & (frame - b >= 0) for b in back]
     shut = [jnp.where(a, 0.0, FAR).astype(F32) for a in allow]
-    for h in range(HEADS):
-        lo = h * HEAD_DIM
-        hi = lo + HEAD_DIM
-        factor = scales[1, h] * (LOG2E / math.sqrt(HEAD_DIM))
-        q = qs[1, lo:hi, :].astype(F32)
-        x = [
-            jnp.sum(q * ks[3 + j, lo:hi, :].astype(F32), axis=0, keepdims=True) * factor + shut[j]
-            for j in range(n_time)
-        ]
-        top = functools.reduce(jnp.maximum, x)
-        e = [jnp.exp2(s - top) for s in x]
-        inv = 1.0 / sum(e)
-        o = sum(
-            (e[j] * inv).astype(BF).astype(F32) * vs[3 + j, lo:hi, :].astype(F32)
-            for j in range(n_time)
-        )
-        mix[1, lo:hi, :] = o.astype(BF)
+    def by_head(block):
+        return block.astype(F32).reshape(HEADS, HEAD_DIM, lon)
+
+    base = LOG2E / math.sqrt(HEAD_DIM)
+    factor = jnp.concatenate([jnp.full((1, lon), scales[1, h] * base) for h in range(HEADS)], axis=0)
+    q = by_head(qs[1])
+    x = [jnp.sum(q * by_head(ks[3 + j]), axis=1) * factor + shut[j] for j in range(n_time)]
+    top = functools.reduce(jnp.maximum, x)
+    e = [jnp.exp2(s - top) for s in x]
+    inv = 1.0 / sum(e)
+    o = sum(
+        (e[j] * inv).astype(BF).astype(F32)[:, None, :] * by_head(vs[3 + j])
+        for j in range(n_time)
+    )
+    mix[1] = o.reshape(HEADS * HEAD_DIM, lon).astype(BF)
 
     update = sum(
         lax.dot_general(mix[w], final[w], (((0,), (1,)), ((), ())), preferred_element_type=F32)

time: 40.7 us -> 40.6 us (level)
  no operation moved by 1% of the time
where the time goes in v6:
time: 40.6 us; the launch traced here: 40.4 us
  starting transfers between devices  25 us (62%)
  Pallas kernels  6.84 us (17%)
  waiting for transfers between devices  4.81 us (12%)
  between operations  1.48 us (4%)
  other arithmetic  1.23 us (3%)
  local copies, waits for them, and re-layouts  1.04 us (3%)
    ppermute x4, starting transfers between devices, body(): chain0.append(lax.ppermute(a, AXES, ring))  8.81 us
    ppermute x3, starting transfers between devices, body(): chain1.append(lax.ppermute(b, AXES, ring))  7.98 us
    pallas_call x1, Pallas kernels, body(): pl.pallas_call(functools.partial(kernel, n_time, n, nf), out_shape=jax.Sh...  6.38 us
    ppermute x4, waiting for transfers between devices, body(): chain0.append(lax.ppermute(a, AXES, ring))  2.44 us
    ppermute x1, starting transfers between devices, rotate_frame(): lax.ppermute(block, 'frame', [(i, (i + hop) % nf) for i in range(nf)])  2 us
    ppermute x1, starting transfers between devices, body(): partner_two = lax.ppermute(two_back, AXES, core)  1.81 us
    ppermute x1, starting transfers between devices, body(): partner = lax.ppermute(state, AXES, core)  1.34 us
    select_n x1, other arithmetic, body(): own1 = jnp.where(parity == 0, chunk_b, chunk_a)  1.12 us
  transfers between devices with their start and end apart: 19, of which 6 were waited for; matrix products, arithmetic and copies ran while one was open for 0% of the time, Pallas kernels for 1%

profile of v6, /device:TPU:0, one launch (start us, length us, event | category | flops | bytes accessed | tf_op | source)
XLA Modules:
  0.0 40.4 jit_solution(10393160206140600587)
XLA Ops:
  0.0 0.9 %fusion = (bf16[512,64]{0,1:T(8,128)(2,1)S(1)}, bf16[512,64]{0,1:T(8,128)(2,1)S(1)}) fusion(bf16[1024,64]{0,1:T(8,128)(2,1)} %param.19), kind=kLoop, calls=%fused_computation.12 | loop fusion | bytes 262144 | tf_op jit(solution)/shard_map/slice | solution.py:246
  0.9 1.1 %select_bitcast_fusion = (bf16[256,512]{1,0:T(8,128)(2,1)S(1)}, bf16[256,512]{1,0:T(8,128)(2,1)S(1)}) fusion(pred[]{:T(512)S(6)} %eq.6, bf16[512,64]{0,1:T(8,128)(2,1)S(1)} %get-tuple-element.12, bf16[512,192]{0,1:T(8,128)(2,1)} %param.18, bf16[512,64]{0,1:T(8,128)(2,1)S(1)} %get-tuple-element.11, bf16[512,192]{0,1:T(8,128)(2,1)} %param.17), kind=kLoop, calls=%fused_computation.3 | loop fusion | flops 1310720 | bytes 1048577 | tf_op jit(solution)/shard_map/jit(_where)/select_n | solution.py:249
  2.1 3.1 %collective-permute-start = (bf16[256,512]{1,0:T(8,128)(2,1)S(1)}, bf16[256,512]{1,0:T(8,128)(2,1)S(1)}, u32[]{:S(2)}, u32[]{:S(2)}) collective-permute-start(bf16[256,512]{1,0:T(8,128)(2,1)S(1)} %get-tuple-element.10.rest_2_), channel_id=1, source_target_pairs={{0,2},{2,4},{4,6},{6,7},{7,5},{5,3},{3,1},{1,0},{8,9},{10,8},{12,1... | collective-permute-start | bytes 786440 | tf_op jit(solution)/shard_map/ppermute | solution.py:264
  5.1 1.6 %collective-permute-start.9 = (bf16[256,512]{1,0:T(8,128)(2,1)S(1)}, bf16[256,512]{1,0:T(8,128)(2,1)S(1)}, u32[]{:S(2)}, u32[]{:S(2)}) collective-permute-start(bf16[256,512]{1,0:T(8,128)(2,1)S(1)} %get-tuple-element.9.rest_10_), channel_id=1, source_target_pairs={{0,2},{2,4},{4,6},{6,7},{7,5},{5,3},{3,1},{1,0},{8,9},{10,8},{12,1... | collective-permute-start | bytes 786440 | tf_op jit(solution)/shard_map/ppermute | solution.py:266
  8.1 1.3 %collective-permute-done.rest_3_ = bf16[256,512]{1,0:T(8,128)(2,1)S(1)} collective-permute-done((bf16[256,512]{1,0:T(8,128)(2,1)S(1)}, bf16[256,512]{1,0:T(8,128)(2,1)S(1)}, u32[]{:S(2)}, u32[]{:S(2)}) %collective-permute-start) | collective-permute-done | bytes 262176 | tf_op jit(solution)/shard_map/ppermute | solution.py:264
  9.4 2.1 %collective-permute-start.6 = (bf16[256,512]{1,0:T(8,128)(2,1)S(1)}, bf16[256,512]{1,0:T(8,128)(2,1)S(1)}, u32[]{:S(2)}, u32[]{:S(2)}) collective-permute-start(bf16[256,512]{1,0:T(8,128)(2,1)S(1)} %collective-permute-done.rest_3_), channel_id=1, source_target_pairs={{0,2},{2,4},{4,6},{6,7},{7,5},{5,3},{3,1},{1,0},{8,9},{10,8},{12,1... | collective-permute-start | bytes 786440 | tf_op jit(solution)/shard_map/ppermute | solution.py:264
  11.5 0.7 %collective-permute-start.2 = (bf16[180,512]{1,0:T(8,128)(2,1)S(1)}, bf16[180,512]{1,0:T(8,128)(2,1)S(1)}, u32[]{:S(2)}, u32[]{:S(2)}) collective-permute-start(bf16[180,512]{1,0:T(8,128)(2,1)S(1)} %bitcast.24), channel_id=1, source_target_pairs={{1,2},{2,1},{3,4},{4,3},{5,6},{6,5},{9,10},{10,9},{11,12},{12,11},... | collective-permute-start | bytes 552968 | tf_op jit(solution)/shard_map/ppermute | solution.py:66
  12.2 2.0 %collective-permute-start.3 = (bf16[180,512]{1,0:T(8,128)(2,1)S(1)}, bf16[180,512]{1,0:T(8,128)(2,1)S(1)}, u32[]{:S(2)}, u32[]{:S(2)}) collective-permute-start(bf16[180,512]{1,0:T(8,128)(2,1)S(1)} %bitcast.25), channel_id=1, source_target_pairs={{0,16},{8,24},{16,0},{24,8},{1,17},{9,25},{17,1},{25,9},{2,18},{10... | collective-permute-start | bytes 552968 | tf_op jit(solution)/shard_map/ppermute | solution.py:58
  14.2 4.3 %collective-permute-start.11 = (bf16[256,512]{1,0:T(8,128)(2,1)S(1)}, bf16[256,512]{1,0:T(8,128)(2,1)S(1)}, u32[]{:S(2)}, u32[]{:S(2)}) collective-permute-start(bf16[256,512]{1,0:T(8,128)(2,1)S(1)} %collective-permute-done.9.rest_11_), channel_id=1, source_target_pairs={{0,2},{2,4},{4,6},{6,7},{7,5},{5,3},{3,1},{1,0},{8,9},{10,8},{12,1... | collective-permute-start | bytes 786440 | tf_op jit(solution)/shard_map/ppermute | solution.py:266
  18.5 1.6 %collective-permute-start.7 = (bf16[256,512]{1,0:T(8,128)(2,1)S(1)}, bf16[256,512]{1,0:T(8,128)(2,1)S(1)}, u32[]{:S(2)}, u32[]{:S(2)}) collective-permute-start(bf16[256,512]{1,0:T(8,128)(2,1)S(1)} %collective-permute-done.6.rest_4_), channel_id=1, source_target_pairs={{0,2},{2,4},{4,6},{6,7},{7,5},{5,3},{3,1},{1,0},{8,9},{10,8},{12,1... | collective-permute-start | bytes 786440 | tf_op jit(solution)/shard_map/ppermute | solution.py:264
  20.2 1.3 %collective-permute-start.4 = (bf16[180,512]{1,0:T(8,128)(2,1)S(1)}, bf16[180,512]{1,0:T(8,128)(2,1)S(1)}, u32[]{:S(2)}, u32[]{:S(2)}) collective-permute-start(bf16[180,512]{1,0:T(8,128)(2,1)S(1)} %bitcast.27), channel_id=1, source_target_pairs={{0,8},{1,9},{2,10},{3,11},{4,12},{5,13},{6,14},{7,15},{8,0},{9,1},... | collective-permute-start | bytes 552968 | tf_op jit(solution)/shard_map/ppermute | solution.py:272
  21.6 0.5 %collective-permute-start.16 = (bf16[256,512]{1,0:T(8,128)(2,1)S(1)}, bf16[256,512]{1,0:T(8,128)(2,1)S(1)}, u32[]{:S(2)}, u32[]{:S(2)}) collective-permute-start(bf16[256,512]{1,0:T(8,128)(2,1)S(1)} %collective-permute-done.rest_3_), channel_id=1, source_target_pairs={{0,8},{1,9},{2,10},{3,11},{4,12},{5,13},{6,14},{7,15},{8,0},{9,1},... | collective-permute-start | bytes 786440 | tf_op jit(solution)/shard_map/ppermute | solution.py:267
  22.1 0.7 %collective-permute-done.11.rest_12_ = bf16[256,512]{1,0:T(8,128)(2,1)S(1)} collective-permute-done((bf16[256,512]{1,0:T(8,128)(2,1)S(1)}, bf16[256,512]{1,0:T(8,128)(2,1)S(1)}, u32[]{:S(2)}, u32[]{:S(2)}) %collective-permute-start.11) | collective-permute-done | bytes 262176 | tf_op jit(solution)/shard_map/ppermute | solution.py:266
  22.8 2.1 %collective-permute-start.13 = (bf16[256,512]{1,0:T(8,128)(2,1)S(1)}, bf16[256,512]{1,0:T(8,128)(2,1)S(1)}, u32[]{:S(2)}, u32[]{:S(2)}) collective-permute-start(bf16[256,512]{1,0:T(8,128)(2,1)S(1)} %collective-permute-done.11.rest_12_), channel_id=1, source_target_pairs={{0,2},{2,4},{4,6},{6,7},{7,5},{5,3},{3,1},{1,0},{8,9},{10,8},{12,1... | collective-permute-start | bytes 786440 | tf_op jit(solution)/shard_map/ppermute | solution.py:266
  24.9 0.7 %collective-permute-done.7.rest_5_ = bf16[256,512]{1,0:T(8,128)(2,1)S(1)} collective-permute-done((bf16[256,512]{1,0:T(8,128)(2,1)S(1)}, bf16[256,512]{1,0:T(8,128)(2,1)S(1)}, u32[]{:S(2)}, u32[]{:S(2)}) %collective-permute-start.7) | collective-permute-done | bytes 262176 | tf_op jit(solution)/shard_map/ppermute | solution.py:264
  25.6 2.1 %collective-permute-start.8 = (bf16[256,512]{1,0:T(8,128)(2,1)S(1)}, bf16[256,512]{1,0:T(8,128)(2,1)S(1)}, u32[]{:S(2)}, u32[]{:S(2)}) collective-permute-start(bf16[256,512]{1,0:T(8,128)(2,1)S(1)} %collective-permute-done.7.rest_5_), channel_id=1, source_target_pairs={{0,2},{2,4},{4,6},{6,7},{7,5},{5,3},{3,1},{1,0},{8,9},{10,8},{12,1... | collective-permute-start | bytes 786440 | tf_op jit(solution)/shard_map/ppermute | solution.py:264
  27.7 1.8 %collective-permute-start.5 = (bf16[180,512]{1,0:T(8,128)(2,1)S(1)}, bf16[180,512]{1,0:T(8,128)(2,1)S(1)}, u32[]{:S(2)}, u32[]{:S(2)}) collective-permute-start(bf16[180,512]{1,0:T(8,128)(2,1)S(1)} %collective-permute-done.3), channel_id=1, source_target_pairs={{0,8},{1,9},{2,10},{3,11},{4,12},{5,13},{6,14},{7,15},{8,0},{9,1},... | collective-permute-start | bytes 552968 | tf_op jit(solution)/shard_map/ppermute | solution.py:273
  29.6 1.0 %collective-permute-done.5 = bf16[180,512]{1,0:T(8,128)(2,1)S(1)} collective-permute-done((bf16[180,512]{1,0:T(8,128)(2,1)S(1)}, bf16[180,512]{1,0:T(8,128)(2,1)S(1)}, u32[]{:S(2)}, u32[]{:S(2)}) %collective-permute-start.5) | collective-permute-done | bytes 184352 | tf_op jit(solution)/shard_map/ppermute | solution.py:273
  30.6 0.4 collective-permute-start.12
  31.1 0.4 collective-permute-start.18
  32.0 0.9 %collective-permute-start.15 = (bf16[256,512]{1,0:T(8,128)(2,1)S(1)}, bf16[256,512]{1,0:T(8,128)(2,1)S(1)}, u32[]{:S(2)}, u32[]{:S(2)}) collective-permute-start(bf16[256,512]{1,0:T(8,128)(2,1)S(1)} %collective-permute-done.8.rest_6_), channel_id=1, source_target_pairs={{0,8},{1,9},{2,10},{3,11},{4,12},{5,13},{6,14},{7,15},{8,0},{9,1},... | collective-permute-start | bytes 786440 | tf_op jit(solution)/shard_map/ppermute | solution.py:269
  33.0 0.5 %norm.1.rest_0_ = bf16[6,180,512]{2,1,0:T(8,128)(2,1)S(1)} custom-call(f32[1,512]{1,0:T(1,128)S(1)} %bitcast.22, bf16[6,180,512]{2,1,0:T(8,128)(2,1)S(1)} %bitcast_dynamic-update-slice_fusion.rows_ref), custom_call_target="tpu_custom_call" | custom-call | tf_op jit(solution)/shard_map/norm/pallas_call | solution.py:280
  33.5 0.6 %collective-permute-done.15.rest_14_ = bf16[256,512]{1,0:T(8,128)(2,1)S(1)} collective-permute-done((bf16[256,512]{1,0:T(8,128)(2,1)S(1)}, bf16[256,512]{1,0:T(8,128)(2,1)S(1)}, u32[]{:S(2)}, u32[]{:S(2)}) %collective-permute-start.15) | collective-permute-done | bytes 262176 | tf_op jit(solution)/shard_map/ppermute | solution.py:269
  34.0 6.4 %block.1 = bf16[180,512]{1,0:T(8,128)(2,1)} custom-call(s32[4]{0:T(128)S(1)} %pad_add_fusion.meta, f32[2,8]{1,0:T(2,128)S(1)} %copy-done.1, s32[8]{0:T(128)S(1)} %copy-done.2, bf16[6,180,512]{2,1,0:T(8,128)(2,1)S(1)} %norm.1.rest_0_, bf16[2,180,512]{2,1,0:T(8,128)(2,1)S(1)} %pad_maximum_fusion.rest_1_, bf16[256,512]{1,0:T(8,128)(2,1)S(1)} %get-tuple-element.10.rest_2_, ...), custom_call_target="tpu_custom_call" | custom-call | tf_op jit(solution)/shard_map/block/pallas_call | solution.py:289
  (36 shorter events, 1.0 us)
Async XLA Ops:
  0.0 11.5 %copy-start.3 = (bf16[1,1,180,512]{3,2,1,0:T(8,128)(2,1)S(1)}, bf16[1,1,180,512]{3,2,1,0:T(8,128)(2,1)}, u32[]{:S(2)}) copy-start(bf16[1,1,180,512]{3,2,1,0:T(8,128)(2,1)} %param.10) | copy-start | bytes 552964
  0.0 20.1 %copy-start.4 = (bf16[1,1,180,512]{3,2,1,0:T(8,128)(2,1)S(1)}, bf16[1,1,180,512]{3,2,1,0:T(8,128)(2,1)}, u32[]{:S(2)}) copy-start(bf16[1,1,180,512]{3,2,1,0:T(8,128)(2,1)} %param.11) | copy-start | bytes 552964
  2.1 7.4 %collective-permute-start = (bf16[256,512]{1,0:T(8,128)(2,1)S(1)}, bf16[256,512]{1,0:T(8,128)(2,1)S(1)}, u32[]{:S(2)}, u32[]{:S(2)}) collective-permute-start(bf16[256,512]{1,0:T(8,128)(2,1)S(1)} %get-tuple-element.10.rest_2_), channel_id=1, source_target_pairs={{0,2},{2,4},{4,6},{6,7},{7,5},{5,3},{3,1},{1,0},{8,9},{10,8},{12,1... | collective-permute-start | bytes 786440 | tf_op jit(solution)/shard_map/ppermute | solution.py:264
  5.1 9.1 %collective-permute-start.9 = (bf16[256,512]{1,0:T(8,128)(2,1)S(1)}, bf16[256,512]{1,0:T(8,128)(2,1)S(1)}, u32[]{:S(2)}, u32[]{:S(2)}) collective-permute-start(bf16[256,512]{1,0:T(8,128)(2,1)S(1)} %get-tuple-element.9.rest_10_), channel_id=1, source_target_pairs={{0,2},{2,4},{4,6},{6,7},{7,5},{5,3},{3,1},{1,0},{8,9},{10,8},{12,1... | collective-permute-start | bytes 786440 | tf_op jit(solution)/shard_map/ppermute | solution.py:266
  9.4 9.1 %collective-permute-start.6 = (bf16[256,512]{1,0:T(8,128)(2,1)S(1)}, bf16[256,512]{1,0:T(8,128)(2,1)S(1)}, u32[]{:S(2)}, u32[]{:S(2)}) collective-permute-start(bf16[256,512]{1,0:T(8,128)(2,1)S(1)} %collective-permute-done.rest_3_), channel_id=1, source_target_pairs={{0,2},{2,4},{4,6},{6,7},{7,5},{5,3},{3,1},{1,0},{8,9},{10,8},{12,1... | collective-permute-start | bytes 786440 | tf_op jit(solution)/shard_map/ppermute | solution.py:264
  11.5 8.7 %collective-permute-start.1 = (bf16[180,512]{1,0:T(8,128)(2,1)S(1)}, bf16[180,512]{1,0:T(8,128)(2,1)S(1)}, u32[]{:S(2)}, u32[]{:S(2)}) collective-permute-start(bf16[180,512]{1,0:T(8,128)(2,1)S(1)} %bitcast.23), channel_id=1, source_target_pairs={{0,1},{1,0},{2,3},{3,2},{4,5},{5,4},{6,7},{7,6},{8,9},{9,8},{10,11... | collective-permute-start | bytes 552968 | tf_op jit(solution)/shard_map/ppermute | solution.py:66
  11.5 10.0 %collective-permute-start.2 = (bf16[180,512]{1,0:T(8,128)(2,1)S(1)}, bf16[180,512]{1,0:T(8,128)(2,1)S(1)}, u32[]{:S(2)}, u32[]{:S(2)}) collective-permute-start(bf16[180,512]{1,0:T(8,128)(2,1)S(1)} %bitcast.24), channel_id=1, source_target_pairs={{1,2},{2,1},{3,4},{4,3},{5,6},{6,5},{9,10},{10,9},{11,12},{12,11},... | collective-permute-start | bytes 552968 | tf_op jit(solution)/shard_map/ppermute | solution.py:66
  12.2 9.4 %collective-permute-start.3 = (bf16[180,512]{1,0:T(8,128)(2,1)S(1)}, bf16[180,512]{1,0:T(8,128)(2,1)S(1)}, u32[]{:S(2)}, u32[]{:S(2)}) collective-permute-start(bf16[180,512]{1,0:T(8,128)(2,1)S(1)} %bitcast.25), channel_id=1, source_target_pairs={{0,16},{8,24},{16,0},{24,8},{1,17},{9,25},{17,1},{25,9},{2,18},{10... | collective-permute-start | bytes 552968 | tf_op jit(solution)/shard_map/ppermute | solution.py:58
  14.2 8.6 %collective-permute-start.11 = (bf16[256,512]{1,0:T(8,128)(2,1)S(1)}, bf16[256,512]{1,0:T(8,128)(2,1)S(1)}, u32[]{:S(2)}, u32[]{:S(2)}) collective-permute-start(bf16[256,512]{1,0:T(8,128)(2,1)S(1)} %collective-permute-done.9.rest_11_), channel_id=1, source_target_pairs={{0,2},{2,4},{4,6},{6,7},{7,5},{5,3},{3,1},{1,0},{8,9},{10,8},{12,1... | collective-permute-start | bytes 786440 | tf_op jit(solution)/shard_map/ppermute | solution.py:266
  18.5 7.1 %collective-permute-start.7 = (bf16[256,512]{1,0:T(8,128)(2,1)S(1)}, bf16[256,512]{1,0:T(8,128)(2,1)S(1)}, u32[]{:S(2)}, u32[]{:S(2)}) collective-permute-start(bf16[256,512]{1,0:T(8,128)(2,1)S(1)} %collective-permute-done.6.rest_4_), channel_id=1, source_target_pairs={{0,2},{2,4},{4,6},{6,7},{7,5},{5,3},{3,1},{1,0},{8,9},{10,8},{12,1... | collective-permute-start | bytes 786440 | tf_op jit(solution)/shard_map/ppermute | solution.py:264
  20.2 12.8 %copy-start = (f32[512]{0:T(512)S(1)}, f32[512]{0:T(512)}, u32[]{:S(2)}) copy-start(f32[512]{0:T(512)} %param.15) | copy-start | bytes 6148
  20.2 7.6 %collective-permute-start.4 = (bf16[180,512]{1,0:T(8,128)(2,1)S(1)}, bf16[180,512]{1,0:T(8,128)(2,1)S(1)}, u32[]{:S(2)}, u32[]{:S(2)}) collective-permute-start(bf16[180,512]{1,0:T(8,128)(2,1)S(1)} %bitcast.27), channel_id=1, source_target_pairs={{0,8},{1,9},{2,10},{3,11},{4,12},{5,13},{6,14},{7,15},{8,0},{9,1},... | collective-permute-start | bytes 552968 | tf_op jit(solution)/shard_map/ppermute | solution.py:272
  21.6 9.4 %collective-permute-start.10 = (bf16[256,512]{1,0:T(8,128)(2,1)S(1)}, bf16[256,512]{1,0:T(8,128)(2,1)S(1)}, u32[]{:S(2)}, u32[]{:S(2)}) collective-permute-start(bf16[256,512]{1,0:T(8,128)(2,1)S(1)} %collective-permute-done.9.rest_11_), channel_id=1, source_target_pairs={{0,8},{1,9},{2,10},{3,11},{4,12},{5,13},{6,14},{7,15},{8,0},{9,1},... | collective-permute-start | bytes 786440 | tf_op jit(solution)/shard_map/ppermute | solution.py:268
  21.6 9.5 %collective-permute-start.16 = (bf16[256,512]{1,0:T(8,128)(2,1)S(1)}, bf16[256,512]{1,0:T(8,128)(2,1)S(1)}, u32[]{:S(2)}, u32[]{:S(2)}) collective-permute-start(bf16[256,512]{1,0:T(8,128)(2,1)S(1)} %collective-permute-done.rest_3_), channel_id=1, source_target_pairs={{0,8},{1,9},{2,10},{3,11},{4,12},{5,13},{6,14},{7,15},{8,0},{9,1},... | collective-permute-start | bytes 786440 | tf_op jit(solution)/shard_map/ppermute | solution.py:267
  22.8 8.7 %collective-permute-start.13 = (bf16[256,512]{1,0:T(8,128)(2,1)S(1)}, bf16[256,512]{1,0:T(8,128)(2,1)S(1)}, u32[]{:S(2)}, u32[]{:S(2)}) collective-permute-start(bf16[256,512]{1,0:T(8,128)(2,1)S(1)} %collective-permute-done.11.rest_12_), channel_id=1, source_target_pairs={{0,2},{2,4},{4,6},{6,7},{7,5},{5,3},{3,1},{1,0},{8,9},{10,8},{12,1... | collective-permute-start | bytes 786440 | tf_op jit(solution)/shard_map/ppermute | solution.py:266
  25.6 6.4 %collective-permute-start.8 = (bf16[256,512]{1,0:T(8,128)(2,1)S(1)}, bf16[256,512]{1,0:T(8,128)(2,1)S(1)}, u32[]{:S(2)}, u32[]{:S(2)}) collective-permute-start(bf16[256,512]{1,0:T(8,128)(2,1)S(1)} %collective-permute-done.7.rest_5_), channel_id=1, source_target_pairs={{0,2},{2,4},{4,6},{6,7},{7,5},{5,3},{3,1},{1,0},{8,9},{10,8},{12,1... | collective-permute-start | bytes 786440 | tf_op jit(solution)/shard_map/ppermute | solution.py:264
  27.7 2.9 %collective-permute-start.5 = (bf16[180,512]{1,0:T(8,128)(2,1)S(1)}, bf16[180,512]{1,0:T(8,128)(2,1)S(1)}, u32[]{:S(2)}, u32[]{:S(2)}) collective-permute-start(bf16[180,512]{1,0:T(8,128)(2,1)S(1)} %collective-permute-done.3), channel_id=1, source_target_pairs={{0,8},{1,9},{2,10},{3,11},{4,12},{5,13},{6,14},{7,15},{8,0},{9,1},... | collective-permute-start | bytes 552968 | tf_op jit(solution)/shard_map/ppermute | solution.py:273
  30.6 2.8 %collective-permute-start.12 = (bf16[256,512]{1,0:T(8,128)(2,1)S(1)}, bf16[256,512]{1,0:T(8,128)(2,1)S(1)}, u32[]{:S(2)}, u32[]{:S(2)}) collective-permute-start(bf16[256,512]{1,0:T(8,128)(2,1)S(1)} %collective-permute-done.11.rest_12_), channel_id=1, source_target_pairs={{0,8},{1,9},{2,10},{3,11},{4,12},{5,13},{6,14},{7,15},{8,0},{9,1},... | collective-permute-start | bytes 786440 | tf_op jit(solution)/shard_map/ppermute | solution.py:268
  31.0 2.4 %collective-permute-start.17 = (bf16[256,512]{1,0:T(8,128)(2,1)S(1)}, bf16[256,512]{1,0:T(8,128)(2,1)S(1)}, u32[]{:S(2)}, u32[]{:S(2)}) collective-permute-start(bf16[256,512]{1,0:T(8,128)(2,1)S(1)} %collective-permute-done.6.rest_4_), channel_id=1, source_target_pairs={{0,8},{1,9},{2,10},{3,11},{4,12},{5,13},{6,14},{7,15},{8,0},{9,1},... | collective-permute-start | bytes 786440 | tf_op jit(solution)/shard_map/ppermute | solution.py:267
  31.1 2.3 %collective-permute-start.18 = (bf16[256,512]{1,0:T(8,128)(2,1)S(1)}, bf16[256,512]{1,0:T(8,128)(2,1)S(1)}, u32[]{:S(2)}, u32[]{:S(2)}) collective-permute-start(bf16[256,512]{1,0:T(8,128)(2,1)S(1)} %collective-permute-done.7.rest_5_), channel_id=1, source_target_pairs={{0,8},{1,9},{2,10},{3,11},{4,12},{5,13},{6,14},{7,15},{8,0},{9,1},... | collective-permute-start | bytes 786440 | tf_op jit(solution)/shard_map/ppermute | solution.py:267
  31.5 1.9 %collective-permute-start.14 = (bf16[256,512]{1,0:T(8,128)(2,1)S(1)}, bf16[256,512]{1,0:T(8,128)(2,1)S(1)}, u32[]{:S(2)}, u32[]{:S(2)}) collective-permute-start(bf16[256,512]{1,0:T(8,128)(2,1)S(1)} %collective-permute-done.13.rest_13_), channel_id=1, source_target_pairs={{0,8},{1,9},{2,10},{3,11},{4,12},{5,13},{6,14},{7,15},{8,0},{9,1},... | collective-permute-start | bytes 786440 | tf_op jit(solution)/shard_map/ppermute | solution.py:268
  32.0 2.0 %collective-permute-start.15 = (bf16[256,512]{1,0:T(8,128)(2,1)S(1)}, bf16[256,512]{1,0:T(8,128)(2,1)S(1)}, u32[]{:S(2)}, u32[]{:S(2)}) collective-permute-start(bf16[256,512]{1,0:T(8,128)(2,1)S(1)} %collective-permute-done.8.rest_6_), channel_id=1, source_target_pairs={{0,8},{1,9},{2,10},{3,11},{4,12},{5,13},{6,14},{7,15},{8,0},{9,1},... | collective-permute-start | bytes 786440 | tf_op jit(solution)/shard_map/ppermute | solution.py:269
  32.9 1.1 %copy-start.1 = (f32[2,8]{1,0:T(2,128)S(1)}, f32[2,8]{1,0:T(2,128)}, u32[]{:S(2)}) copy-start(f32[2,8]{1,0:T(2,128)} %scales.1) | copy-start | bytes 196
  32.9 1.1 %copy-start.2 = (s32[8]{0:T(128)S(1)}, s32[8]{0:T(128)}, u32[]{:S(2)}) copy-start(s32[8]{0:T(128)} %tally.1) | copy-start | bytes 100
